TPU v7x, 32 devices: a whole 2x2x4 slice. The times are simulated.
32 devices in a mesh: seq: 16 (over z, y, x), tp: 2 (over core).
Axes of the slice: x: 2, y: 2, z: 4, core: 2. Of those that a mesh axis runs over, the one named last changes fastest.
Arguments:
- tokens: bfloat16 [24576, 768], P('seq'), may hold values from -6 to 6
- short_lengths: int32 [16, 3], P('seq'), may hold values from 1 to 512, 1024 in all within a row
- query_weight: bfloat16 [768, 768], P(None, 'tp'), may hold values from -0.21875 to 0.21875
- key_weight: bfloat16 [768, 768], P(None, 'tp'), may hold values from -0.21875 to 0.21875
- value_weight: bfloat16 [768, 768], P(None, 'tp'), may hold values from -0.21875 to 0.21875
- conv_kernel: float32 [12, 33], P('tp'), may hold values from -0.3 to 0.3
- out_weight: bfloat16 [768, 768], P('tp'), may hold values from -0.625 to 0.625
- gain_one: float32 [768], replicated, may hold values from 0.5 to 1.5
- bias_one: float32 [768], replicated, may hold values from -1 to 1
- inner_weight: bfloat16 [768, 3072], P(None, 'tp'), may hold values from -0.21875 to 0.21875
- outer_weight: bfloat16 [3072, 768], P('tp'), may hold values from -0.109375 to 0.109375
- gain_two: float32 [768], replicated, may hold values from 0.5 to 1.5
- bias_two: float32 [768], replicated, may hold values from -1 to 1
- cotangent: bfloat16 [24576, 768], P('seq'), may hold values from -6 to 6
Outputs:
- output: bfloat16 [24576, 768], P('seq')
- token_grad: float32 [24576, 768], P('seq')
- query_grad: float32 [768, 768], P(None, 'tp')
- key_grad: float32 [768, 768], P(None, 'tp')
- value_grad: float32 [768, 768], P(None, 'tp')
- kernel_grad: float32 [12, 33], P('tp')
- out_grad: float32 [768, 768], P('tp')
- gain_one_grad: float32 [768], replicated
- bias_one_grad: float32 [768], replicated
- inner_grad: float32 [768, 3072], P(None, 'tp')
- outer_grad: float32 [3072, 768], P('tp')
- gain_two_grad: float32 [768], replicated
- bias_two_grad: float32 [768], replicated
Inputs may be any that keep to these rules, and one draw needn't show every extreme that they name: `short_lengths`: row d lists the lengths of device d's short items in order; they sum to 1024, and the largest of each row is exactly 512.
All inputs are finite; a program needn't handle non-finite values.
Results may differ from a plain program's by a relative error of at most 0.013.
Values may be sent and summed in bfloat16 or wider, within the bound.
No kernel may reach another device: no remote copies, remote signals or barrier semaphores. Data moves between devices by JAX's collectives and lax.ppermute only.
A program may use at most 320 MiB of HBM per device.

v0:
```python
import math

import jax
import jax.numpy as jnp
from jax import lax
from jax.experimental import pallas as pl
from jax.experimental.pallas import tpu as pltpu
from jax.sharding import PartitionSpec as P

TAU = 8
CONV_WIDTH = 33
HALF_WIDTH = 16
GROUP = 16
PIECE = 256
ITEMS = 2
REACH = 32
BAND_ROWS = PIECE + 2 * REACH
LINE = 640

COS_SCALE = 0.98
EPS_UNIT = 1e-06
EPS_NORM = 1e-05
NEAR_POLY = (1.158024787902832, -0.36302468180656433, 0.09245320409536362, -0.011449637822806835)
TAIL_POLY = tuple(
    0.5 * a for a in (0.254829592, -0.284496736, 1.421413741, -1.453152027, 1.061405429)
)
SLOPE_SCALE = TAU / math.pi
VMEM_BYTES = 60 * 2**20

F32 = jnp.float32
BF16 = jnp.bfloat16


def norm_terms(values):
    centered = values - jnp.mean(values, axis=-1, keepdims=True)
    inverse = lax.rsqrt(jnp.mean(centered * centered, axis=-1, keepdims=True) + EPS_NORM)
    return centered * inverse, inverse


def norm_back(scaled, unit, inverse):
    along = jnp.mean(scaled * unit, axis=-1, keepdims=True)
    return inverse * (scaled - jnp.mean(scaled, axis=-1, keepdims=True) - unit * along)


def gelu_terms(values):
    share = 1.0 / (1.0 + (0.3275911 * math.sqrt(0.5)) * jnp.abs(values))
    bell = jnp.exp(-0.5 * (values * values))
    poly = TAIL_POLY[4] * share + TAIL_POLY[3]
    for coefficient in TAIL_POLY[2::-1]:
        poly = poly * share + coefficient
    tail = poly * (share * bell)
    below = jnp.where(values < 0.0, tail, 1.0 - tail)
    return values * below, below + values * (bell * (1.0 / math.sqrt(2.0 * math.pi)))


def place_of_item(rows):
    item_at = lax.broadcasted_iota(jnp.int32, (rows, rows), 0)
    place_at = lax.broadcasted_iota(jnp.int32, (rows, rows), 1)
    hit = item_at == (place_at & 1) * PIECE + (place_at >> 1)
    return jnp.where(hit, 1.0, 0.0).astype(BF16)


def lasting(microseconds):
    return pl.CostEstimate(flops=microseconds * 1_150_000_000, bytes_accessed=0, transcendentals=0)


def contract(left, right, left_dim, right_dim):
    return lax.dot_general(
        left, right, (((left_dim,), (right_dim,)), ((), ())), preferred_element_type=F32
    )


def pair_terms(dots, same=None):
    upper = 1.0 / COS_SCALE + dots
    lower = 1.0 / COS_SCALE - dots
    upper_inv = lax.rsqrt(upper)
    lower_inv = lax.rsqrt(lower)
    wide = 1.0 / 0.7 + lower * lower_inv
    wide_inv = lax.rsqrt(wide)
    root = wide * wide_inv
    ratio = NEAR_POLY[3] * root + NEAR_POLY[2]
    ratio = ratio * root + NEAR_POLY[1]
    ratio = ratio * root + NEAR_POLY[0]
    near = ratio * ((upper * upper_inv) * wide_inv)
    if same is not None:
        near = jnp.where(same, near, 0.0)
    near_2 = near * near
    near_4 = near_2 * near_2
    weights = (near_4 * near_4).astype(BF16)
    slopes = ((near_4 * near_2) * (near * (upper_inv * lower_inv))).astype(BF16)
    return weights, slopes


def banded(line):
    wide = jnp.broadcast_to(line, (BAND_ROWS, line.shape[1]))
    return pltpu.roll(wide, 0, 1, stride=1, stride_axis=0)[:, :PIECE].astype(BF16)


def unbanded(products):
    rows_at = lax.broadcasted_iota(jnp.int32, (BAND_ROWS, BAND_ROWS), 0)
    rows_to = lax.broadcasted_iota(jnp.int32, (BAND_ROWS, BAND_ROWS), 1)
    flip = jnp.where(rows_at + rows_to == BAND_ROWS - 1, 1.0, 0.0)
    flipped = lax.dot_general(
        flip, products, (((1,), (0,)), ((), ())), precision=lax.Precision.HIGHEST,
        preferred_element_type=F32,
    )
    wide = jnp.concatenate([flipped, jnp.zeros((BAND_ROWS, LINE - PIECE), F32)], axis=1)
    return jnp.sum(pltpu.roll(wide, 0, 1, stride=1, stride_axis=0), axis=0, keepdims=True)


def padded_rows(dst, src, length):
    edge = jnp.zeros((REACH, dst.shape[1]), dst.dtype)
    dst[pl.ds(0, REACH), :] = edge
    dst[pl.ds(REACH + length, REACH), :] = edge
    for start in range(0, length, PIECE):
        dst[pl.ds(REACH + start, PIECE), :] = src[:, pl.ds(start, PIECE)].T


def rows_of(dst, src, length):
    for start in range(0, length, PIECE):
        dst[pl.ds(start, PIECE), :] = src[:, pl.ds(start, PIECE)].T


def long_forward(query, key, value, line):
    head_dim, length = query.shape
    blocks = length // PIECE
    step = 512

    def body(q_ref, k_ref, v_ref, line_ref, o_ref, w_ref, s_ref, key_rows, taps):
        block = pl.program_id(0)

        @pl.when(block == 0)
        def _():
            rows_of(key_rows, k_ref, length)
            taps[...] = jnp.zeros_like(taps)
            taps[pl.ds(length - REACH, BAND_ROWS), :] = banded(line_ref[...])

        q = q_ref[...]
        start = block * PIECE
        total = jnp.zeros((head_dim, PIECE), F32)
        for at in range(0, length, step):
            dots = contract(key_rows[pl.ds(at, step), :], q, 1, 0)
            weights, slopes = pair_terms(dots)
            near = pl.multiple_of(length + at - start, PIECE)
            weights = weights + taps[pl.ds(near, step), :]
            w_ref[pl.ds(at, step), :] = weights
            s_ref[pl.ds(at, step), :] = slopes
            total = total + contract(v_ref[:, pl.ds(at, step)], weights, 1, 0)
        o_ref[...] = total.astype(BF16)

    whole = pl.BlockSpec((head_dim, length), lambda i: (0, 0))
    large = pl.BlockSpec((None, length, PIECE), lambda i: (i, 0, 0))
    large_shape = jax.ShapeDtypeStruct((blocks, length, PIECE), BF16)
    return pl.pallas_call(
        body,
        grid=(blocks,),
        in_specs=[
            pl.BlockSpec((head_dim, PIECE), lambda i: (0, i)),
            whole,
            whole,
            pl.BlockSpec((1, LINE), lambda i: (0, 0)),
        ],
        out_specs=[pl.BlockSpec((None, head_dim, PIECE), lambda i: (i, 0, 0)), large, large],
        out_shape=[jax.ShapeDtypeStruct((blocks, head_dim, PIECE), BF16), large_shape, large_shape],
        scratch_shapes=[
            pltpu.VMEM((length, head_dim), BF16),
            pltpu.VMEM((2 * length, PIECE), BF16),
        ],
        compiler_params=pltpu.CompilerParams(vmem_limit_bytes=VMEM_BYTES),
        cost_estimate=lasting(70),
    )(query, key, value, line)


def long_back_values(value, grad, weights):
    head_dim, length = grad.shape
    blocks = length // PIECE
    step = 1024

    def body(v_ref, g_ref, w_ref, dv_ref, taps_ref, value_sum, value_rows, products):
        block = pl.program_id(0)

        @pl.when(block == 0)
        def _():
            padded_rows(value_rows, v_ref, length)
            value_sum[...] = jnp.zeros_like(value_sum)
            products[...] = jnp.zeros_like(products)

        g = g_ref[...]
        start = pl.multiple_of(block * PIECE, PIECE)
        products[...] += contract(value_rows[pl.ds(start, BAND_ROWS), :], g, 1, 0)
        for at in range(0, length, step):
            value_sum[:, pl.ds(at, step)] += contract(g, w_ref[pl.ds(at, step), :], 1, 1)

        @pl.when(block == blocks - 1)
        def _():
            for index in range(blocks):
                dv_ref[index] = value_sum[:, pl.ds(index * PIECE, PIECE)].astype(BF16)
            taps_ref[...] = unbanded(products[...])

    return pl.pallas_call(
        body,
        grid=(blocks,),
        in_specs=[
            pl.BlockSpec((head_dim, length), lambda i: (0, 0)),
            pl.BlockSpec((head_dim, PIECE), lambda i: (0, i)),
            pl.BlockSpec((None, length, PIECE), lambda i: (i, 0, 0)),
        ],
        out_specs=[
            pl.BlockSpec((blocks, head_dim, PIECE), lambda i: (0, 0, 0)),
            pl.BlockSpec((1, LINE), lambda i: (0, 0)),
        ],
        out_shape=[
            jax.ShapeDtypeStruct((blocks, head_dim, PIECE), BF16),
            jax.ShapeDtypeStruct((1, LINE), F32),
        ],
        scratch_shapes=[
            pltpu.VMEM((head_dim, length), F32),
            pltpu.VMEM((length + 2 * REACH, head_dim), BF16),
            pltpu.VMEM((BAND_ROWS, PIECE), F32),
        ],
        compiler_params=pltpu.CompilerParams(vmem_limit_bytes=VMEM_BYTES),
        cost_estimate=lasting(26),
    )(value, grad, weights)


def long_back_pairs(query, key, value, grad, slopes):
    head_dim, length = query.shape
    blocks = length // PIECE
    step = 1024

    def body(q_ref, k_ref, v_ref, g_ref, s_ref, dq_ref, dk_ref, value_rows, key_sum):
        block = pl.program_id(0)

        @pl.when(block == 0)
        def _():
            rows_of(value_rows, v_ref, length)
            key_sum[...] = jnp.zeros_like(key_sum)

        q = q_ref[...]
        g = g_ref[...]
        total = jnp.zeros((head_dim, PIECE), F32)
        for at in range(0, length, step):
            grad_weights = contract(value_rows[pl.ds(at, step), :], g, 1, 0)
            terms = grad_weights.astype(BF16) * s_ref[pl.ds(at, step), :]
            total = total + contract(k_ref[:, pl.ds(at, step)], terms, 1, 0)
            key_sum[:, pl.ds(at, step)] += contract(q, terms, 1, 1)
        dq_ref[...] = (total * SLOPE_SCALE).astype(BF16)

        @pl.when(block == blocks - 1)
        def _():
            for index in range(blocks):
                piece = key_sum[:, pl.ds(index * PIECE, PIECE)]
                dk_ref[index] = (piece * SLOPE_SCALE).astype(BF16)

    whole = pl.BlockSpec((head_dim, length), lambda i: (0, 0))
    piece = pl.BlockSpec((head_dim, PIECE), lambda i: (0, i))
    pieces_shape = jax.ShapeDtypeStruct((blocks, head_dim, PIECE), BF16)
    return pl.pallas_call(
        body,
        grid=(blocks,),
        in_specs=[
            piece,
            whole,
            whole,
            piece,
            pl.BlockSpec((None, length, PIECE), lambda i: (i, 0, 0)),
        ],
        out_specs=[
            pl.BlockSpec((None, head_dim, PIECE), lambda i: (i, 0, 0)),
            pl.BlockSpec((blocks, head_dim, PIECE), lambda i: (0, 0, 0)),
        ],
        out_shape=[pieces_shape] * 2,
        scratch_shapes=[
            pltpu.VMEM((length, head_dim), BF16),
            pltpu.VMEM((head_dim, length), F32),
        ],
        compiler_params=pltpu.CompilerParams(vmem_limit_bytes=VMEM_BYTES),
        cost_estimate=lasting(40),
    )(query, key, value, grad, slopes)


def short_forward(reach, ids_row, ids_col, pack, lines):
    _, heads, head_dim, length = pack.shape
    blocks = length // PIECE

    def body(
        reach_ref, row_ref, col_ref, q_ref, k_ref, v_ref, line_ref,
        o_ref, w_ref, s_ref, key_rows, total, taps,
    ):
        block = pl.program_id(0)

        @pl.when(block == 0)
        def _():
            taps[...] = jnp.zeros_like(taps)
            for h in range(heads):
                rows_of(key_rows.at[h], k_ref.at[h], length)
                taps[h, pl.ds(length - REACH, BAND_ROWS), :] = banded(line_ref[h])

        total[...] = jnp.zeros_like(total)
        own_ids = row_ref[...]

        def turn(step, carry):
            at = pl.multiple_of(step * PIECE, PIECE)
            same = col_ref[pl.ds(REACH + at, PIECE), :] == own_ids
            same_low = same.astype(F32).astype(BF16)
            near = pl.multiple_of(length + at - block * PIECE, PIECE)
            for h in range(heads):
                dots = contract(key_rows[h, pl.ds(at, PIECE), :], q_ref[h], 1, 0)
                weights, slopes = pair_terms(dots, same)
                weights = weights + taps[h, pl.ds(near, PIECE), :] * same_low
                w_ref[h, pl.ds(at, PIECE), :] = weights
                s_ref[h, pl.ds(at, PIECE), :] = slopes
                total[h] += contract(v_ref[h, :, pl.ds(at, PIECE)], weights, 1, 0)
            return carry

        lax.fori_loop(reach_ref[0, block], reach_ref[1, block], turn, 0)
        o_ref[...] = total[...].astype(BF16)

    def packed(which):
        return pl.BlockSpec((None, heads, head_dim, length), lambda i: (which, 0, 0, 0))

    block_spec = pl.BlockSpec((heads, head_dim, PIECE), lambda i: (0, 0, i))
    large = pl.BlockSpec((None, heads, length, PIECE), lambda i: (i, 0, 0, 0))
    large_shape = jax.ShapeDtypeStruct((blocks, heads, length, PIECE), BF16)
    return pl.pallas_call(
        body,
        grid=(blocks,),
        in_specs=[
            pl.BlockSpec(memory_space=pltpu.SMEM),
            pl.BlockSpec((1, PIECE), lambda i: (0, i)),
            pl.BlockSpec(ids_col.shape, lambda i: (0, 0)),
            pl.BlockSpec((None, heads, head_dim, PIECE), lambda i: (0, 0, 0, i)),
            packed(1),
            packed(2),
            pl.BlockSpec((heads, 1, LINE), lambda i: (0, 0, 0)),
        ],
        out_specs=[block_spec, large, large],
        out_shape=[jax.ShapeDtypeStruct((heads, head_dim, length), BF16), large_shape, large_shape],
        scratch_shapes=[
            pltpu.VMEM((heads, length, head_dim), BF16),
            pltpu.VMEM((heads, head_dim, PIECE), F32),
            pltpu.VMEM((heads, 2 * length, PIECE), BF16),
        ],
        compiler_params=pltpu.CompilerParams(vmem_limit_bytes=VMEM_BYTES),
        cost_estimate=lasting(28),
    )(reach, ids_row, ids_col, pack, pack, pack, lines)


def short_backward(reach, ids_row, ids_col, pack, grad, weights, slopes):
    _, heads, head_dim, length = pack.shape
    blocks = length // PIECE

    def body(
        reach_ref, row_ref, col_ref, q_ref, k_ref, v_ref, g_ref, w_ref, s_ref,
        dq_ref, dk_ref, dv_ref, taps_ref, value_rows, products,
    ):
        block = pl.program_id(0)

        @pl.when(block == 0)
        def _():
            for h in range(heads):
                padded_rows(value_rows.at[h], v_ref.at[h], length)
            dk_ref[...] = jnp.zeros_like(dk_ref)
            dv_ref[...] = jnp.zeros_like(dv_ref)
            products[...] = jnp.zeros_like(products)

        start = pl.multiple_of(block * PIECE, PIECE)
        near = (col_ref[pl.ds(start, BAND_ROWS), :] == row_ref[...]).astype(F32)
        for h in range(heads):
            products[h] += (
                contract(value_rows[h, pl.ds(start, BAND_ROWS), :], g_ref[h], 1, 0) * near
            )
        dq_ref[...] = jnp.zeros_like(dq_ref)

        def turn(step, carry):
            at = pl.multiple_of(step * PIECE, PIECE)
            for h in range(heads):
                own = g_ref[h]
                grad_weights = contract(value_rows[h, pl.ds(REACH + at, PIECE), :], own, 1, 0)
                terms = grad_weights.astype(BF16) * s_ref[h, pl.ds(at, PIECE), :]
                dq_ref[h] += contract(k_ref[h, :, pl.ds(at, PIECE)], terms, 1, 0) * SLOPE_SCALE
                dk_ref[h, :, pl.ds(at, PIECE)] += contract(q_ref[h], terms, 1, 1) * SLOPE_SCALE
                dv_ref[h, :, pl.ds(at, PIECE)] += contract(own, w_ref[h, pl.ds(at, PIECE), :], 1, 1)
            return carry

        lax.fori_loop(reach_ref[0, block], reach_ref[1, block], turn, 0)

        @pl.when(block == blocks - 1)
        def _():
            for h in range(heads):
                taps_ref[h] = unbanded(products[h])

    def packed(which):
        return pl.BlockSpec((None, heads, head_dim, length), lambda i: (which, 0, 0, 0))

    block_spec = pl.BlockSpec((heads, head_dim, PIECE), lambda i: (0, 0, i))
    whole = pl.BlockSpec((heads, head_dim, length), lambda i: (0, 0, 0))
    large = pl.BlockSpec((None, heads, length, PIECE), lambda i: (i, 0, 0, 0))
    whole_shape = jax.ShapeDtypeStruct((heads, head_dim, length), F32)
    return pl.pallas_call(
        body,
        grid=(blocks,),
        in_specs=[
            pl.BlockSpec(memory_space=pltpu.SMEM),
            pl.BlockSpec((1, PIECE), lambda i: (0, i)),
            pl.BlockSpec(ids_col.shape, lambda i: (0, 0)),
            pl.BlockSpec((None, heads, head_dim, PIECE), lambda i: (0, 0, 0, i)),
            packed(1),
            packed(2),
            block_spec,
            large,
            large,
        ],
        out_specs=[block_spec, whole, whole, pl.BlockSpec((heads, 1, LINE), lambda i: (0, 0, 0))],
        out_shape=[whole_shape] * 3 + [jax.ShapeDtypeStruct((heads, 1, LINE), F32)],
        scratch_shapes=[
            pltpu.VMEM((heads, length + 2 * REACH, head_dim), BF16),
            pltpu.VMEM((heads, BAND_ROWS, PIECE), F32),
        ],
        compiler_params=pltpu.CompilerParams(vmem_limit_bytes=VMEM_BYTES),
        cost_estimate=lasting(28),
    )(reach, ids_row, ids_col, pack, pack, pack, grad, weights, slopes)


def project_in(tokens, query_weight, key_weight, value_weight, heads):
    row_total, width = tokens.shape
    cols = query_weight.shape[1]
    head_dim = cols // heads
    blocks = row_total // PIECE
    long_rows = ITEMS * PIECE

    def body(t_ref, wq_ref, wk_ref, wv_ref, long_ref, short_ref, unit_ref, inv_ref, turned, rows):
        block = pl.program_id(0)

        @pl.when(block == 0)
        def _():
            for index, ref in enumerate((wq_ref, wk_ref, wv_ref)):
                turned[pl.ds(index * cols, cols), :] = ref[...].T
            long_ref[pl.ds(ITEMS * heads, GROUP - ITEMS * heads)] = jnp.zeros(
                (GROUP - ITEMS * heads, 3 * head_dim, PIECE), BF16
            )

        @pl.when(block < ITEMS)
        def _():
            item_at = lax.broadcasted_iota(jnp.int32, (PIECE, long_rows), 0)
            place_at = lax.broadcasted_iota(jnp.int32, (PIECE, long_rows), 1)
            pick = jnp.where(place_at == ITEMS * item_at + block, 1.0, 0.0).astype(BF16)
            rows[...] = contract(pick, t_ref[pl.ds(0, long_rows), :], 1, 0).astype(BF16)

        @pl.when(block >= ITEMS)
        def _():
            rows[...] = t_ref[pl.ds(pl.multiple_of(block * PIECE, PIECE), PIECE), :]

        parts = contract(turned[...], rows[...], 1, 1).reshape(3, heads, head_dim, PIECE)
        raw = parts[:2]
        inverse = lax.rsqrt(jnp.sum(raw * raw, axis=2, keepdims=True) + EPS_UNIT)
        unit = raw * inverse
        unit_ref[...] = unit
        inv_ref[...] = inverse
        low = unit.astype(BF16)
        short_ref[:2] = low
        short_ref[2] = parts[2].astype(BF16)

        @pl.when(block < ITEMS)
        def _():
            for h in range(heads):
                unit_at = block * heads + h
                long_ref[unit_at, pl.ds(0, head_dim), :] = low[0, h]
                long_ref[unit_at, pl.ds(head_dim, head_dim), :] = low[1, h]
                long_ref[unit_at, pl.ds(2 * head_dim, head_dim), :] = parts[2, h].astype(BF16)

    weight = pl.BlockSpec((width, cols), lambda i: (0, 0))
    return pl.pallas_call(
        body,
        grid=(blocks,),
        in_specs=[pl.BlockSpec((row_total, width), lambda i: (0, 0)), weight, weight, weight],
        out_specs=[
            pl.BlockSpec((GROUP, 3 * head_dim, PIECE), lambda i: (0, 0, 0)),
            pl.BlockSpec(
                (3, heads, head_dim, PIECE), lambda i: (0, 0, 0, jnp.maximum(i - ITEMS, 0))
            ),
            pl.BlockSpec((2, heads, head_dim, PIECE), lambda i: (0, 0, 0, i)),
            pl.BlockSpec((2, heads, 1, PIECE), lambda i: (0, 0, 0, i)),
        ],
        out_shape=[
            jax.ShapeDtypeStruct((GROUP, 3 * head_dim, PIECE), BF16),
            jax.ShapeDtypeStruct((3, heads, head_dim, row_total - long_rows), BF16),
            jax.ShapeDtypeStruct((2, heads, head_dim, row_total), F32),
            jax.ShapeDtypeStruct((2, heads, 1, row_total), F32),
        ],
        scratch_shapes=[pltpu.VMEM((3 * cols, width), BF16), pltpu.VMEM((PIECE, width), BF16)],
        compiler_params=pltpu.CompilerParams(vmem_limit_bytes=VMEM_BYTES),
        cost_estimate=lasting(10),
    )(tokens, query_weight, key_weight, value_weight)


def row_blocks(first, count, cols, span=PIECE):
    return pl.BlockSpec((span, cols), lambda i: (i + first, 0))


ANYWHERE = pl.BlockSpec(memory_space=pl.ANY)


def project_out_short(short_att, out_weight, row_total):
    heads, head_dim, short_rows = short_att.shape
    cols, width = out_weight.shape
    span = ITEMS * PIECE

    def body(a_ref, w_ref, mixed_ref, part_ref):
        mixed = a_ref[...].reshape(cols, span)
        mixed_ref[...] = mixed
        part_ref[...] = contract(mixed, w_ref[...], 0, 0).astype(BF16)

    return pl.pallas_call(
        body,
        grid=(short_rows // span,),
        in_specs=[
            pl.BlockSpec((heads, head_dim, span), lambda i: (0, 0, i)),
            pl.BlockSpec((cols, width), lambda i: (0, 0)),
        ],
        out_specs=[
            pl.BlockSpec((cols, span), lambda i: (0, i + 1)),
            pl.BlockSpec((span, width), lambda i: (i, 0)),
        ],
        out_shape=[
            jax.ShapeDtypeStruct((cols, row_total), BF16),
            jax.ShapeDtypeStruct((short_rows, width), BF16),
        ],
        compiler_params=pltpu.CompilerParams(vmem_limit_bytes=VMEM_BYTES),
        cost_estimate=lasting(4),
    )(short_att, out_weight)


def project_out_long(moved_low, moved_high, out_weight, mixed):
    cols, width = out_weight.shape
    half = moved_low.shape[1]
    head_dim = 2 * half
    heads = cols // head_dim
    span = ITEMS * PIECE

    def body(low_ref, high_ref, w_ref, old_ref, mixed_ref, part_ref, items):
        for h in range(heads):
            for item in range(ITEMS):
                for at, ref in ((0, low_ref), (half, high_ref)):
                    items[pl.ds(h * head_dim + at, half), pl.ds(item * PIECE, PIECE)] = ref[
                        item * heads + h
                    ]
        placed = contract(items[...], place_of_item(span), 1, 0).astype(BF16)
        mixed_ref[...] = placed
        part_ref[...] = contract(placed, w_ref[...], 0, 0).astype(BF16)

    return pl.pallas_call(
        body,
        grid=(1,),
        in_specs=[
            pl.BlockSpec((GROUP, half, PIECE), lambda i: (0, 0, 0)),
            pl.BlockSpec((GROUP, half, PIECE), lambda i: (0, 0, 0)),
            pl.BlockSpec((cols, width), lambda i: (0, 0)),
            ANYWHERE,
        ],
        out_specs=[
            pl.BlockSpec((cols, span), lambda i: (0, 0)),
            pl.BlockSpec((span, width), lambda i: (0, 0)),
        ],
        out_shape=[
            jax.ShapeDtypeStruct(mixed.shape, BF16),
            jax.ShapeDtypeStruct((span, width), BF16),
        ],
        scratch_shapes=[pltpu.VMEM((cols, span), BF16)],
        input_output_aliases={3: 0},
        compiler_params=pltpu.CompilerParams(vmem_limit_bytes=VMEM_BYTES),
        cost_estimate=lasting(3),
    )(moved_low, moved_high, out_weight, mixed)


def feed_forward(first, tokens, own, other, gain, bias, inner_weight, outer_weight, into=()):
    row_total, width = tokens.shape
    count = own.shape[0] // PIECE
    hidden_units = inner_weight.shape[1]

    def body(t_ref, own_ref, other_ref, gain_ref, bias_ref, inner_ref, outer_ref, *rest):
        unit_ref, inv_ref, low_ref, act_ref, slope_ref, part_ref = rest[len(into) :]
        hidden = t_ref[...].astype(F32) + (
            own_ref[...].astype(F32) + other_ref[...].astype(F32)
        )
        unit, inverse = norm_terms(hidden)
        unit_ref[...] = unit
        inv_ref[...] = inverse
        low = (unit * gain_ref[...] + bias_ref[...]).astype(BF16)
        low_ref[...] = low
        act, slope = gelu_terms(contract(low, inner_ref[...], 1, 0))
        act = act.astype(BF16)
        act_ref[...] = act
        slope_ref[...] = slope.astype(BF16)
        part_ref[...] = contract(act, outer_ref[...], 1, 0).astype(BF16)

    own_rows = row_blocks(0, count, width)
    rows = row_blocks(first, count, width)
    units = row_blocks(first, count, hidden_units)
    line = pl.BlockSpec((1, width), lambda i: (0, 0))
    return pl.pallas_call(
        body,
        grid=(count,),
        in_specs=[
            rows, own_rows, own_rows, line, line,
            pl.BlockSpec((width, hidden_units), lambda i: (0, 0)),
            pl.BlockSpec((hidden_units, width), lambda i: (0, 0)),
        ]
        + [ANYWHERE] * len(into),
        out_specs=[rows, row_blocks(first, count, 1), rows, units, units, own_rows],
        out_shape=[
            jax.ShapeDtypeStruct((row_total, width), F32),
            jax.ShapeDtypeStruct((row_total, 1), F32),
            jax.ShapeDtypeStruct((row_total, width), BF16),
            jax.ShapeDtypeStruct((row_total, hidden_units), BF16),
            jax.ShapeDtypeStruct((row_total, hidden_units), BF16),
            jax.ShapeDtypeStruct((count * PIECE, width), BF16),
        ],
        input_output_aliases={7 + at: at for at in range(len(into))},
        compiler_params=pltpu.CompilerParams(vmem_limit_bytes=VMEM_BYTES),
        cost_estimate=lasting(3 * count),
    )(tokens, own, other, gain, bias, inner_weight, outer_weight, *into)


def feed_back(
    first, unit_one, own, other, gain_one, bias_one, gain_two, bias_two, cotangent, slope,
    inner_weight, outer_weight, into=(),
):
    row_total, width = unit_one.shape
    count = own.shape[0] // PIECE
    hidden_units = inner_weight.shape[1]

    def body(
        unit_ref, own_ref, other_ref, gain_one_ref, bias_one_ref, gain_ref, bias_ref, g_ref,
        slope_ref, inner_ref, outer_ref, *rest,
    ):
        out_ref, sum_ref, low_ref, pre_ref, part_ref, gain_grad_ref, bias_grad_ref = rest[
            len(into) :
        ]

        @pl.when(pl.program_id(0) == 0)
        def _():
            gain_grad_ref[...] = jnp.zeros_like(gain_grad_ref)
            bias_grad_ref[...] = jnp.zeros_like(bias_grad_ref)

        normed = unit_ref[...] * gain_one_ref[...] + bias_one_ref[...]
        unit, inverse = norm_terms(
            normed + (own_ref[...].astype(F32) + other_ref[...].astype(F32))
        )
        out_ref[...] = (unit * gain_ref[...] + bias_ref[...]).astype(BF16)
        g = g_ref[...].astype(F32)
        gain_grad_ref[...] += jnp.sum(g * unit, axis=0, keepdims=True)
        bias_grad_ref[...] += jnp.sum(g, axis=0, keepdims=True)
        grad_sum = norm_back(g * gain_ref[...], unit, inverse)
        sum_ref[...] = grad_sum
        low = grad_sum.astype(BF16)
        low_ref[...] = low
        pre = contract(low, outer_ref[...], 1, 1) * slope_ref[...].astype(F32)
        pre = pre.astype(BF16)
        pre_ref[...] = pre
        part_ref[...] = contract(pre, inner_ref[...], 1, 1).astype(BF16)

    own_rows = row_blocks(0, count, width)
    rows = row_blocks(first, count, width)
    units = row_blocks(first, count, hidden_units)
    line = pl.BlockSpec((1, width), lambda i: (0, 0))
    return pl.pallas_call(
        body,
        grid=(count,),
        in_specs=[
            rows, own_rows, own_rows, line, line, line, line, rows, units,
            pl.BlockSpec((width, hidden_units), lambda i: (0, 0)),
            pl.BlockSpec((hidden_units, width), lambda i: (0, 0)),
        ]
        + [ANYWHERE] * len(into),
        out_specs=[rows, rows, rows, units, own_rows, line, line],
        out_shape=[
            jax.ShapeDtypeStruct((row_total, width), BF16),
            jax.ShapeDtypeStruct((row_total, width), F32),
            jax.ShapeDtypeStruct((row_total, width), BF16),
            jax.ShapeDtypeStruct((row_total, hidden_units), BF16),
            jax.ShapeDtypeStruct((count * PIECE, width), BF16),
            jax.ShapeDtypeStruct((1, width), F32),
            jax.ShapeDtypeStruct((1, width), F32),
        ],
        input_output_aliases={11 + at: at for at in range(len(into))},
        compiler_params=pltpu.CompilerParams(vmem_limit_bytes=VMEM_BYTES),
        cost_estimate=lasting(3 * count),
    )(
        unit_one, own, other, gain_one, bias_one, gain_two, bias_two, cotangent, slope,
        inner_weight, outer_weight, *into,
    )


def project_back(first, unit, inverse, grad_sum, own, other, gain, out_weight, heads, into=()):
    row_total, width = unit.shape
    cols = out_weight.shape[0]
    head_dim = cols // heads
    span = ITEMS * PIECE
    count = own.shape[0] // span
    is_long = first == 0

    def body(unit_ref, inv_ref, sum_ref, own_ref, other_ref, gain_ref, w_ref, *rest):
        hidden_ref, low_ref, att_ref, gain_grad_ref, bias_grad_ref = rest[len(into) :]

        @pl.when(pl.program_id(0) == 0)
        def _():
            gain_grad_ref[...] = jnp.zeros_like(gain_grad_ref)
            bias_grad_ref[...] = jnp.zeros_like(bias_grad_ref)

        unit = unit_ref[...]
        grad = sum_ref[...] + (own_ref[...].astype(F32) + other_ref[...].astype(F32))
        gain_grad_ref[...] += jnp.sum(grad * unit, axis=0, keepdims=True)
        bias_grad_ref[...] += jnp.sum(grad, axis=0, keepdims=True)
        hidden = norm_back(grad * gain_ref[...], unit, inv_ref[...])
        hidden_ref[...] = hidden
        low = hidden.astype(BF16)
        low_ref[...] = low
        att = contract(w_ref[...], low, 1, 1).astype(BF16)
        if is_long:
            items = contract(att, place_of_item(span), 1, 1).astype(BF16)
            for h in range(heads):
                for item in range(ITEMS):
                    att_ref[item * heads + h] = items[
                        h * head_dim : (h + 1) * head_dim, item * PIECE : (item + 1) * PIECE
                    ]
            att_ref[pl.ds(ITEMS * heads, GROUP - ITEMS * heads)] = jnp.zeros(
                (GROUP - ITEMS * heads, head_dim, PIECE), BF16
            )
        else:
            att_ref[...] = att.reshape(heads, head_dim, span)

    own_rows = row_blocks(0, count, width, span)
    rows = row_blocks(first, count, width, span)
    line = pl.BlockSpec((1, width), lambda i: (0, 0))
    if is_long:
        att_spec = pl.BlockSpec((GROUP, head_dim, PIECE), lambda i: (0, 0, 0))
        att_shape = (GROUP, head_dim, PIECE)
    else:
        att_spec = pl.BlockSpec((heads, head_dim, span), lambda i: (0, 0, i))
        att_shape = (heads, head_dim, count * span)
    return pl.pallas_call(
        body,
        grid=(count,),
        in_specs=[
            rows, row_blocks(first, count, 1, span), rows, own_rows, own_rows, line,
            pl.BlockSpec((cols, width), lambda i: (0, 0)),
        ]
        + [ANYWHERE] * len(into),
        out_specs=[rows, rows, att_spec, line, line],
        out_shape=[
            jax.ShapeDtypeStruct((row_total, width), F32),
            jax.ShapeDtypeStruct((row_total, width), BF16),
            jax.ShapeDtypeStruct(att_shape, BF16),
            jax.ShapeDtypeStruct((1, width), F32),
            jax.ShapeDtypeStruct((1, width), F32),
        ],
        input_output_aliases={7 + at: at for at in range(len(into))},
        compiler_params=pltpu.CompilerParams(vmem_limit_bytes=VMEM_BYTES),
        cost_estimate=lasting(4 * count),
    )(unit, inverse, grad_sum, own, other, gain, out_weight, *into)


NORM_SLOT = 16
OUT_SLOT = 8


def first_rows(source, mine_ref, away, second, count):
    first = lax.bitwise_xor(mine_ref[0], away)
    return source[pl.ds(pl.multiple_of((first * 4 + second) * count, count), count), :]


def terms_call(body, mine, rows, columns, lines, counts, width, scratch, microseconds):
    span = ITEMS * PIECE
    shape = (4, sum(counts), width)
    return counts, pl.pallas_call(
        body,
        grid=(rows[0].shape[0] // span,),
        in_specs=[pl.BlockSpec(memory_space=pltpu.SMEM)]
        + [pl.BlockSpec((span, array.shape[1]), lambda i: (i, 0)) for array in rows]
        + [pl.BlockSpec((array.shape[0], span), lambda i: (0, i)) for array in columns]
        + [pl.BlockSpec(array.shape, lambda i: (0, 0)) for array in lines],
        out_specs=[pl.BlockSpec(shape, lambda i: (0, 0, 0))] * 4,
        out_shape=[jax.ShapeDtypeStruct(shape, BF16)] * 4,
        scratch_shapes=[pltpu.VMEM(dims, F32) for dims in scratch],
        compiler_params=pltpu.CompilerParams(vmem_limit_bytes=VMEM_BYTES),
        cost_estimate=lasting(microseconds),
    )(mine, *rows, *columns, *lines)


def outer_terms(mine, act, grad_ffn, norm_lines):
    units, width = act.shape[1], grad_ffn.shape[1]
    counts = [units // 16, NORM_SLOT]

    def body(mine_ref, act_ref, ffn_ref, norm_ref, *rest):
        outs, (outer,) = rest[:4], rest[4:]

        @pl.when(pl.program_id(0) == 0)
        def _():
            outer[...] = jnp.zeros_like(outer)

        outer[...] += contract(act_ref[...], ffn_ref[...], 0, 0)

        @pl.when(pl.program_id(0) == pl.num_programs(0) - 1)
        def _():
            slot = lax.broadcasted_iota(jnp.int32, (NORM_SLOT, width), 0) == 0
            for away, ref in enumerate(outs):
                line = norm_ref[pl.ds(lax.bitwise_xor(mine_ref[0], away), 1), :]
                for second in range(4):
                    rows = first_rows(outer, mine_ref, away, second, counts[0])
                    ref[second, pl.ds(0, counts[0]), :] = rows.astype(BF16)
                    lines = jnp.where(slot, line if second == 0 else 0.0, 0.0)
                    ref[second, pl.ds(counts[0], NORM_SLOT), :] = lines.astype(BF16)

    return terms_call(
        body, mine, [act, grad_ffn], [], [norm_lines], counts, width, [(units, width)], 9
    )


def inner_terms(mine, normed, grad_pre, mixed, grad_proj):
    units, width, cols = grad_pre.shape[1], normed.shape[1], mixed.shape[0]
    counts = [width // 16, width // 16, cols // 16, OUT_SLOT]

    def body(mine_ref, low_ref, pre_ref, proj_ref, mixed_ref, *rest):
        outs, (inner, out) = rest[:4], rest[4:]

        @pl.when(pl.program_id(0) == 0)
        def _():
            inner[...] = jnp.zeros_like(inner)
            out[...] = jnp.zeros_like(out)

        inner[...] += contract(low_ref[...], pre_ref[...], 0, 0)
        out[...] += contract(mixed_ref[...], proj_ref[...], 1, 0)

        @pl.when(pl.program_id(0) == pl.num_programs(0) - 1)
        def _():
            for away, ref in enumerate(outs):
                for second in range(4):
                    both = first_rows(inner, mine_ref, away, second, counts[0]).astype(BF16)
                    ref[second, pl.ds(0, counts[0]), :] = both[:, :width]
                    ref[second, pl.ds(counts[0], counts[1]), :] = both[:, width:]
                    tail = jnp.concatenate(
                        [
                            first_rows(out, mine_ref, away, second, counts[2]),
                            jnp.zeros((OUT_SLOT, width), F32),
                        ],
                        axis=0,
                    )
                    ref[second, pl.ds(counts[0] + counts[1], counts[2] + OUT_SLOT), :] = (
                        tail.astype(BF16)
                    )

    return terms_call(
        body, mine, [normed, grad_pre, grad_proj], [mixed], [], counts, width,
        [(width, units), (cols, width)], 9,
    )


def next_terms(part, counts, bits):
    places, at, pieces = 1 << len(bits), 0, []
    for index, count in enumerate(counts):
        pieces.append(part[at : at + count].reshape(places, -1, part.shape[1]))
        at, counts[index] = at + count, count // places
    return terms_for(jnp.concatenate(pieces, axis=1), bits)


def gathered_sums(gathered, counts, targets, shapes):
    peers = gathered.shape[0]
    width = gathered.shape[2]
    groups = bit_groups(peers)

    def body(in_ref, *outs):
        for at_place in range(peers):
            order = 0
            for bits in groups:
                size = 1 << len(bits)
                order = order * size + ((at_place >> bits[0]) & (size - 1))
            at = 0
            for count, target in zip(counts, targets):
                if target is not None:
                    index, column = target
                    rows = in_ref[at_place, pl.ds(at, count), :].astype(F32)
                    if column is not None:
                        outs[index][pl.ds(order * count, count), pl.ds(column, width)] = rows
                    elif order % (peers // 4) == 0:
                        outs[index][pl.ds(order // (peers // 4), 1), :] = rows[:1]
                at += count

    def whole(shape):
        return pl.BlockSpec(shape, lambda: (0,) * len(shape))

    return pl.pallas_call(
        body,
        in_specs=[whole(gathered.shape)],
        out_specs=[whole(shape) for shape in shapes],
        out_shape=[jax.ShapeDtypeStruct(shape, F32) for shape in shapes],
        compiler_params=pltpu.CompilerParams(vmem_limit_bytes=VMEM_BYTES),
        cost_estimate=lasting(4),
    )(gathered)


def placed_sums(mine, arrays, counts, targets, shapes):
    width = arrays[0].shape[2]

    def body(mine_ref, *refs):
        ins, outs = refs[: len(arrays)], refs[len(arrays) :]
        for first_away, ref in enumerate(ins):
            first = lax.bitwise_xor(mine_ref[0], first_away)
            for second_away in range(ref.shape[0]):
                second = lax.bitwise_xor(mine_ref[1], second_away)
                order = first * ref.shape[0] + second
                at = 0
                for count, target in zip(counts, targets):
                    rows = pl.ds(at, count)
                    at += count
                    if target is None:
                        continue
                    out = outs[target[0]]
                    if target[1] is not None:
                        to = pl.ds(pl.multiple_of(order * count, count), count)
                        out[to, pl.ds(target[1], width)] = ref[second_away, rows, :].astype(F32)
                    elif out.shape[0] > 4:
                        out[pl.ds(order, 1), :] = ref[second_away, rows, :].astype(F32)[:1]
                    else:

                        @pl.when(second == 0)
                        def _():
                            out[pl.ds(first, 1), :] = ref[second_away, rows, :].astype(F32)[:1]

    def whole(shape):
        return pl.BlockSpec(shape, lambda: (0,) * len(shape))

    return pl.pallas_call(
        body,
        in_specs=[pl.BlockSpec(memory_space=pltpu.SMEM)] + [whole(array.shape) for array in arrays],
        out_specs=[whole(shape) for shape in shapes],
        out_shape=[jax.ShapeDtypeStruct(shape, F32) for shape in shapes],
        compiler_params=pltpu.CompilerParams(vmem_limit_bytes=VMEM_BYTES),
        cost_estimate=lasting(4),
    )(mine, *arrays)


def gathered_or_placed(part, steps, counts, targets, shapes):
    peers = lax.axis_size("seq")
    place = lax.axis_index("seq")
    if len(steps) != 2 or any(len(bits) != 2 for bits in steps):
        gathered = lax.all_gather(part, "seq", axis=0)
        taken = [target for target in targets if target is None or target[1] is not None or
                 shapes[target[0]][0] == 4]
        sums = gathered_sums(gathered, counts[: len(taken)], taken, [
            shape for shape in shapes if shape[0] != peers])
        return sums if len(sums) == len(shapes) else [
            *sums, gathered[:, sum(counts[:-1])].astype(F32)]
    arrays = [part[None]] + [came[None] for came in terms_sent([part] * 4, steps[1])]
    own = jnp.concatenate(arrays, axis=0)
    arrays = [own] + terms_sent([own] * 4, steps[0])
    mine = jnp.stack([place & 3, (place >> 2) & 3]).astype(jnp.int32)
    return placed_sums(mine, arrays, counts, targets, shapes)


def unit_back(moved_pairs, moved_values, short_parts, unit, inverse):
    heads, head_dim = unit.shape[1:3]
    short_heads, _, short_rows = short_parts[0][0].shape
    count = len(short_parts)
    span = ITEMS * PIECE
    blocks = 1 + short_rows // span
    cols = heads * head_dim

    def body(*refs):
        pairs_ref, values_ref = refs[:2]
        short_refs = refs[2 : 2 + 3 * count]
        unit_ref, inv_ref, out_ref, items = refs[2 + 3 * count :]
        block = pl.program_id(0)

        def short_part(which):
            return jnp.concatenate([short_refs[3 * at + which][...] for at in range(count)], axis=0)

        def back(which, grad):
            unit = unit_ref[which]
            along = jnp.sum(unit * grad, axis=1, keepdims=True)
            return ((grad - unit * along) * inv_ref[which]).astype(BF16).reshape(cols, span)

        @pl.when(block == 0)
        def _():
            def long_part(ref, at):
                part = pl.ds(at, head_dim)
                heads_of = [
                    jnp.concatenate([ref[h, part, :], ref[heads + h, part, :]], axis=1)
                    for h in range(heads)
                ]
                return jnp.stack(heads_of, axis=0)

            for which in range(2):
                items[pl.ds(which * cols, cols), :] = back(
                    which, long_part(pairs_ref, which * head_dim).astype(F32)
                )
            items[pl.ds(2 * cols, cols), :] = long_part(values_ref, 0).reshape(cols, span)
            out_ref[...] = contract(items[...], place_of_item(span), 1, 0).astype(BF16)

        @pl.when(block > 0)
        def _():
            out_ref[pl.ds(0, cols), :] = back(0, short_part(0))
            out_ref[pl.ds(cols, cols), :] = back(1, short_part(1))
            out_ref[pl.ds(2 * cols, cols), :] = short_part(2).astype(BF16).reshape(
                cols, span
            )

    short = pl.BlockSpec(
        (short_heads, head_dim, span), lambda i: (0, 0, jnp.maximum(i - 1, 0))
    )
    return pl.pallas_call(
        body,
        grid=(blocks,),
        in_specs=[
            pl.BlockSpec((GROUP, moved_pairs.shape[1], PIECE), lambda i: (0, 0, 0)),
            pl.BlockSpec((GROUP, head_dim, PIECE), lambda i: (0, 0, 0)),
        ]
        + [short] * (3 * count)
        + [
            pl.BlockSpec((2, heads, head_dim, span), lambda i: (0, 0, 0, i)),
            pl.BlockSpec((2, heads, 1, span), lambda i: (0, 0, 0, i)),
        ],
        out_specs=pl.BlockSpec((3 * cols, span), lambda i: (0, i)),
        out_shape=jax.ShapeDtypeStruct((3 * cols, span * blocks), BF16),
        scratch_shapes=[pltpu.VMEM((3 * cols, span), BF16)],
        compiler_params=pltpu.CompilerParams(vmem_limit_bytes=VMEM_BYTES),
        cost_estimate=lasting(8),
    )(moved_pairs, moved_values, *sum(map(tuple, short_parts), ()), unit, inverse)


def other_half(part):
    return lax.ppermute(part, "tp", [(0, 1), (1, 0)])


def bit_groups(peers):
    bits = peers.bit_length() - 1
    return [list(range(low, min(low + 2, bits))) for low in range(0, bits, 2)]


def terms_for(part, bits):
    mine = (lax.axis_index("seq") >> bits[0]) & ((1 << len(bits)) - 1)
    return [
        lax.dynamic_index_in_dim(part, mine ^ away, 0, False) for away in range(1 << len(bits))
    ]


def in_order(gathered, peers):
    sizes = [1 << len(bits) for bits in reversed(bit_groups(peers))]
    count = len(sizes)
    array = gathered.reshape(sizes + list(gathered.shape[1:]))
    array = jnp.transpose(array, list(range(count))[::-1] + [count, count + 1])
    return array.reshape(-1, gathered.shape[-1])


def terms_sent(terms, bits, first=1):
    peers = lax.axis_size("seq")
    terms = terms if first > 1 else terms[1:]
    return [
        lax.ppermute(term, "seq", [(i, i ^ (away << bits[0])) for i in range(peers)])
        for away, term in enumerate(terms, first)
    ]


def terms_gathered(own, bits):
    mine = (lax.axis_index("seq") >> bits[0]) & ((1 << len(bits)) - 1)
    every = jnp.stack([own] + terms_sent([own] * (1 << len(bits)), bits), axis=0)
    return jnp.stack(
        [
            lax.dynamic_index_in_dim(every, mine ^ place, 0, False)
            for place in range(1 << len(bits))
        ],
        axis=0,
    )


def terms_summed(own, came):
    total = own.astype(F32)
    for term in came:
        total = total + term.astype(F32)
    return total.astype(BF16)


def after(first, second):
    return lax.optimization_barrier((first, second))


def shards(
    tokens,
    short_lengths,
    query_weight,
    key_weight,
    value_weight,
    conv_kernel,
    out_weight,
    gain_one,
    bias_one,
    inner_weight,
    outer_weight,
    gain_two,
    bias_two,
    cotangent,
):
    row_total, width = tokens.shape
    heads_dev = conv_kernel.shape[0]
    head_cols = query_weight.shape[1]
    head_dim = head_cols // heads_dev
    short_rows = row_total - ITEMS * PIECE
    units = ITEMS * heads_dev
    place = lax.axis_index("seq") % GROUP
    groups = [
        [first + i for i in range(GROUP)] for first in range(0, lax.axis_size("seq"), GROUP)
    ]

    def exchange(pieces):
        return lax.all_to_all(pieces, "seq", 0, 0, axis_index_groups=groups)

    def by_position(moved, count):
        return jnp.transpose(moved, (1, 0, 2)).reshape(count, head_dim, GROUP * PIECE)

    item_ends = jnp.cumsum(short_lengths[0])
    positions = jnp.arange(short_rows, dtype=jnp.int32)
    item_ids = jnp.sum((positions[:, None] >= item_ends[None, :]).astype(jnp.int32), axis=1)
    ids_row = item_ids[None, :]
    ids_col = jnp.pad(item_ids, (REACH, REACH), constant_values=-1)[:, None]
    item_starts = jnp.concatenate([jnp.zeros((1,), jnp.int32), item_ends[:-1]])
    block_first = jnp.arange(0, short_rows, PIECE, dtype=jnp.int32)
    block_last = block_first + (PIECE - 1)
    inside = (item_starts[None, :] <= block_last[:, None]) & (
        item_ends[None, :] > block_first[:, None]
    )
    lowest = jnp.min(jnp.where(inside, item_starts[None, :], short_rows), axis=1)
    highest = jnp.max(jnp.where(inside, item_ends[None, :], 0), axis=1)
    reach = jnp.stack([lowest // PIECE, (highest + PIECE - 1) // PIECE]).astype(jnp.int32)

    last_tap = LINE - REACH - HALF_WIDTH
    lines = jnp.pad(
        conv_kernel[:, ::-1], ((0, 0), (last_tap, LINE - last_tap - CONV_WIDTH))
    )[:, None, :]
    unit_head = place % heads_dev
    long_line = lax.dynamic_index_in_dim(lines, unit_head, 0, False)

    long_send, short_pack, unit, inverse = project_in(
        tokens, query_weight, key_weight, value_weight, heads_dev
    )
    lines_of = [line[None, :] for line in (gain_one, bias_one, gain_two, bias_two)]
    gain_one, bias_one, gain_two, bias_two = lines_of

    long_moved = exchange(long_send)
    short_att, short_w, short_s = short_forward(reach, ids_row, ids_col, short_pack, lines)
    mixed, short_proj = project_out_short(short_att, out_weight, row_total)
    long_moved, short_proj = after(long_moved, short_proj)
    long_pack = by_position(long_moved, 3)
    long_att, long_w, long_s = long_forward(long_pack[0], long_pack[1], long_pack[2], long_line)

    long_att, short_proj = after(long_att, short_proj)
    long_halves = jnp.split(long_att, 2, axis=1)
    low_half = exchange(long_halves[0])
    first_short = ITEMS
    *forward, short_ffn = feed_forward(
        first_short, tokens, short_proj, other_half(short_proj), gain_one, bias_one, inner_weight,
        outer_weight,
    )
    low_half, short_ffn, high_half = lax.optimization_barrier(
        (low_half, short_ffn, long_halves[1])
    )
    high_half = exchange(high_half)
    *backward, short_back, short_gain_two, short_bias_two = feed_back(
        first_short, forward[0], short_ffn, other_half(short_ffn), gain_one, bias_one, gain_two,
        bias_two, cotangent, forward[4], inner_weight, outer_weight,
    )
    high_half, short_back = after(high_half, short_back)
    short_back_other = other_half(short_back)

    mixed, long_proj = project_out_long(low_half, high_half, out_weight, mixed)
    *forward, long_ffn = feed_forward(
        0, tokens, long_proj, other_half(long_proj), gain_one, bias_one, inner_weight,
        outer_weight, forward,
    )
    norm_unit, norm_inverse, normed_low, act_low, act_slope = forward
    *backward, long_back, long_gain_two, long_bias_two = feed_back(
        0, norm_unit, long_ffn, other_half(long_ffn), gain_one, bias_one, gain_two, bias_two,
        cotangent, act_slope, inner_weight, outer_weight, backward,
    )
    output, grad_sum, grad_ffn_low, grad_pre_low = backward
    long_back_other = other_half(long_back)
    grad_hidden, grad_proj_low, short_grad, short_gain_one, short_bias_one = project_back(
        1, norm_unit, norm_inverse, grad_sum, short_back, short_back_other, gain_one, out_weight,
        heads_dev,
    )
    grad_hidden, grad_proj_low, long_grad, long_gain_one, long_bias_one = project_back(
        0, norm_unit, norm_inverse, grad_sum, long_back, long_back_other, gain_one, out_weight,
        heads_dev, (grad_hidden, grad_proj_low),
    )
    norm_lines = jnp.concatenate(
        [
            long_gain_one + short_gain_one,
            long_bias_one + short_bias_one,
            long_gain_two + short_gain_two,
            long_bias_two + short_bias_two,
        ],
        axis=0,
    )

    peers = lax.axis_size("seq")
    steps = bit_groups(peers)
    long_grad, norm_lines = after(long_grad, norm_lines)
    long_grad = exchange(long_grad)
    mine = (lax.axis_index("seq") & 3).astype(jnp.int32)[None]
    outer_counts, outer_terms_now = outer_terms(mine, act_low, grad_ffn_low, norm_lines)
    outer_terms_now, grad_pre_low = after(outer_terms_now, grad_pre_low)
    outer_came = terms_sent(outer_terms_now, steps[0])
    inner_counts, inner_terms_now = inner_terms(
        mine, normed_low, grad_pre_low, mixed, grad_proj_low
    )
    inner_terms_now, long_grad = after(inner_terms_now, long_grad)
    long_grad = by_position(long_grad, 1)[0]
    long_dv, long_taps = long_back_values(long_pack[2], long_grad, long_w)
    outer_came, own, inner_terms_now, long_dv, long_grad = lax.optimization_barrier(
        (outer_came, outer_terms_now[0], inner_terms_now, long_dv, long_grad)
    )
    outer_part = terms_summed(own, outer_came)
    inner_came = terms_sent(inner_terms_now, steps[0])
    outer_terms_now, long_dv, long_grad = lax.optimization_barrier(
        (terms_for(outer_part, steps[1]), long_dv, long_grad)
    )
    outer_came = terms_sent(outer_terms_now, steps[1])
    long_dv = exchange(long_dv)
    long_dq, long_dk = long_back_pairs(
        long_pack[0], long_pack[1], long_pack[2], long_grad, long_s
    )
    outer_came, outer_own, inner_came, inner_own, long_dv, long_dq, long_dk, short_grad = (
        lax.optimization_barrier(
            (
                outer_came, outer_terms_now[0], inner_came, inner_terms_now[0], long_dv, long_dq,
                long_dk, short_grad,
            )
        )
    )
    outer_part = terms_summed(outer_own, outer_came)
    for bits in steps[2:]:
        terms = next_terms(outer_part, outer_counts, bits)
        outer_part = terms_summed(terms[0], terms_sent(terms, bits))
    inner_part = terms_summed(inner_own, inner_came)
    long_back = jnp.concatenate([long_dq, long_dk], axis=1)
    inner_terms_now, outer_part, long_back, short_grad = lax.optimization_barrier(
        (terms_for(inner_part, steps[1]), outer_part, long_back, short_grad)
    )
    outer_sum, norm_sums = gathered_or_placed(
        outer_part, steps, outer_counts, [(0, 0), (1, None)], [outer_weight.shape, (4, width)]
    )
    long_back = exchange(long_back)
    inner_came = terms_sent(inner_terms_now, steps[1])
    *short_parts, short_taps = short_backward(
        reach, ids_row, ids_col, short_pack, short_grad, short_w, short_s
    )
    long_back, short_parts, short_taps = lax.optimization_barrier(
        (long_back, short_parts, short_taps)
    )
    grads_low = unit_back(long_back, long_dv, [short_parts], unit, inverse)
    own, grads_low = after(inner_terms_now[0], grads_low)
    inner_part = terms_summed(own, inner_came)
    for bits in steps[2:]:
        terms = next_terms(inner_part, inner_counts, bits)
        inner_part = terms_summed(terms[0], terms_sent(terms, bits))

    first_tap = BAND_ROWS - 1 - REACH + HALF_WIDTH
    taps = slice(first_tap, first_tap - CONV_WIDTH, -1)
    owner = (jnp.arange(heads_dev) == unit_head) & (place < units)
    kernel_part = short_taps[:, 0, taps] + jnp.where(owner[:, None], long_taps[:, taps], 0.0)
    taps_line = kernel_part.reshape(1, -1)
    taps_line = jnp.pad(taps_line, ((0, 15), (0, width - taps_line.shape[1]))).astype(BF16)
    inner_sum, out_sum, tap_lines = gathered_or_placed(
        jnp.concatenate([inner_part, taps_line], axis=0), steps, inner_counts + [16],
        [(0, 0), (0, width), (1, 0), None, (2, None)],
        [inner_weight.shape, out_weight.shape, (peers, width)],
    )
    kernel_sum = jnp.sum(tap_lines[:, : heads_dev * CONV_WIDTH], axis=0).reshape(
        heads_dev, CONV_WIDTH
    )

    weight_part = contract(tokens, grads_low, 0, 1).astype(BF16)
    terms = terms_for(weight_part.reshape(1 << len(steps[0]), -1, 3 * head_cols), steps[0])
    terms, grads_low = after(terms, grads_low)
    came = terms_sent(terms, steps[0])
    weight_all = jnp.concatenate([query_weight, key_weight, value_weight], axis=1)
    token_own = contract(grads_low, weight_all, 0, 1).astype(BF16)
    own, token_own = after(terms[0], token_own)
    weight_part = terms_summed(own, came)
    for bits in steps[1:]:
        terms = terms_for(weight_part.reshape(1 << len(bits), -1, 3 * head_cols), bits)
        weight_part = terms_summed(terms[0], terms_sent(terms, bits))
    for bits in reversed(steps):
        weight_part = terms_gathered(weight_part, bits).reshape(-1, 3 * head_cols)
    weight_sum = weight_part.astype(F32)
    token_grad = grad_hidden + (token_own.astype(F32) + other_half(token_own).astype(F32))
    return (
        output,
        token_grad,
        weight_sum[:, :head_cols],
        weight_sum[:, head_cols : 2 * head_cols],
        weight_sum[:, 2 * head_cols :],
        kernel_sum,
        out_sum,
        norm_sums[0],
        norm_sums[1],
        inner_sum,
        outer_sum,
        norm_sums[2],
        norm_sums[3],
    )


def solution(mesh):
    rows = P("seq", None)
    columns = P(None, "tp")
    split_rows = P("tp", None)
    return jax.shard_map(
        shards,
        mesh=mesh,
        in_specs=(
            rows, rows, columns, columns, columns, split_rows, split_rows,
            P(), P(), columns, split_rows, P(), P(), rows,
        ),
        out_specs=(
            rows, rows, columns, columns, columns, split_rows, split_rows,
            P(), P(), columns, split_rows, P(), P(),
        ),
        check_vma=False,
    )
```

profile of v0, /device:TPU:0, one launch (start us, length us, event | category | flops | bytes accessed | tf_op | source)
XLA Modules:
  0.0 522.3 jit_solution(15451136158791127115)
XLA Ops:
  0.6 9.9 %shard_map.237 = (bf16[16,192,256]{2,1,0:T(8,128)(2,1)}, bf16[3,6,64,1024]{3,2,1,0:T(8,128)(2,1)}, f32[2,6,64,1536]{3,2,1,0:T(8,128)}, f32[2,6,1,1536]{3,2,1,0:T(1,128)}) custom-call(bf16[1536,768]{1,0:T(8,128)(2,1)} %t_ref.5, bf16[768,384]{1,0:T(8,128)(2,1)} %wq_ref.1, bf16[768,384]{1,0:T(8,128)(2,1)} %wk_ref.1, bf16[768,384]{1,0:T(8,128)(2,1)} %wv_ref.1), custom_call_target="tpu_custom_call" | custom-call | flops 11500000256 | tf_op jit(solution)/shard_map/pallas_call | solution.py:473
  10.6 8.5 %all-to-all-start = ((bf16[16,192,256]{2,1,0:T(8,128)(2,1)}), bf16[16,192,256]{2,1,0:T(8,128)(2,1)S(1)}, u32[]{:S(2)}, u32[]{:S(2)}) async-start(bf16[16,192,256]{2,1,0:T(8,128)(2,1)} %get-tuple-element.154), calls=%async_computation | async-start | bytes 3145728 | tf_op jit(solution)/shard_map/all_to_all | solution.py:1115
  22.8 26.4 %shard_map.238 = (bf16[6,64,1024]{2,1,0:T(8,128)(2,1)}, bf16[4,6,1024,256]{3,2,1,0:T(8,128)(2,1)}, bf16[4,6,1024,256]{3,2,1,0:T(8,128)(2,1)}) custom-call(s32[2,4]{1,0:T(2,128)} %pad_add_fusion.reach_ref, s32[1,1024]{1,0:T(1,128)} %bitcast.132, s32[1088,1]{1,0:T(8,128)} %broadcast_in_dim.117.col_ref, ...), custom_call_target="tpu_custom_call" | custom-call | flops 32199999488 | tf_op jit(solution)/shard_map/pallas_call | solution.py:325
  49.2 3.4 shard_map.239
  55.9 71.3 %shard_map.240 = (bf16[16,64,256]{2,1,0:T(8,128)(2,1)}, bf16[16,4096,256]{2,1,0:T(8,128)(2,1)}, bf16[16,4096,256]{2,1,0:T(8,128)(2,1)}) custom-call(bf16[64,4096]{1,0:T(8,128)(2,1)} %bitcast.115, bf16[64,4096]{1,0:T(8,128)(2,1)} %bitcast.117, bf16[64,4096]{1,0:T(8,128)(2,1)} %bitcast.112, f32[1,640]{1,0:T(1,128)} %pad_dynamic-slice_fusion.line_ref), custom_call_target="tpu_custom_call" | custom-call | flops 80499998720 | tf_op jit(solution)/shard_map/pallas_call | solution.py:154
  130.3 15.1 %all-to-all-start.1 = ((bf16[16,32,256]{2,1,0:T(8,128)(2,1)}), bf16[16,32,256]{2,1,0:T(8,128)(2,1)S(1)}, u32[]{:S(2)}, u32[]{:S(2)}) async-start(bf16[16,32,256]{2,1,0:T(8,128)(2,1)} %get-tuple-element.324), calls=%async_computation.1 | async-start | bytes 524288 | tf_op jit(solution)/shard_map/all_to_all | solution.py:1115
  146.6 14.6 %shard_map.241 = (f32[1536,768]{1,0:T(8,128)}, f32[1536,1]{1,0:T(8,128)}, bf16[1536,768]{1,0:T(8,128)(2,1)}, bf16[1536,1536]{1,0:T(8,128)(2,1)}, bf16[1536,1536]{1,0:T(8,128)(2,1)}, /*index=5*/bf16[1024,768]{1,0:T(8,128)(2,1)}) custom-call(bf16[1536,768]{1,0:T(8,128)(2,1)} %t_ref.5, bf16[1024,768]{1,0:T(8,128)(2,1)} %get-tuple-element.162.own_ref, ...), custom_call_target="tpu_custom_call" | custom-call | flops 13799999488 | tf_op jit(solution)/shard_map/pallas_call | solution.py:601
  162.7 6.8 %all-to-all-start.2 = ((bf16[16,32,256]{2,1,0:T(8,128)(2,1)}), bf16[16,32,256]{2,1,0:T(8,128)(2,1)S(1)}, u32[]{:S(2)}, u32[]{:S(2)}) async-start(bf16[16,32,256]{2,1,0:T(8,128)(2,1)} %get-tuple-element.165), calls=%async_computation.2 | async-start | bytes 524288 | tf_op jit(solution)/shard_map/all_to_all | solution.py:1115
  170.7 13.3 %shard_map.242 = (bf16[1536,768]{1,0:T(8,128)(2,1)}, f32[1536,768]{1,0:T(8,128)}, bf16[1536,768]{1,0:T(8,128)(2,1)}, bf16[1536,1536]{1,0:T(8,128)(2,1)}, bf16[10...) custom-call(f32[1536,768]{1,0:T(8,128)} %get-tuple-element.166.unit_ref.rest_0_, ...), custom_call_target="tpu_custom_call" | custom-call | flops 13799999488 | tf_op jit(solution)/shard_map/pallas_call | solution.py:667
  184.7 3.2 shard_map.243
  191.2 9.3 %shard_map.244 = (f32[1536,768]{1,0:T(8,128)}, f32[1536,1]{1,0:T(8,128)}, bf16[1536,768]{1,0:T(8,128)(2,1)}, bf16[1536,1536]{1,0:T(8,128)(2,1)}, bf16[1536,1536]{1,0:T(8,128)(2,1)}, /*index=5*/bf16[512,768]{1,0:T(8,128)(2,1)}) custom-call(bf16[1536,768]{1,0:T(8,128)(2,1)} %t_ref.5, ...), custom_call_target="tpu_custom_call", output_to_operand_aliasing={{0}: (7, {}), {1}: (8, {}), {2}: (9, {}), {3}: (10, {}), {4... | custom-call | flops 6899999744 | tf_op jit(solution)/shard_map/pallas_call | solution.py:601
  204.0 8.7 %shard_map.245 = (bf16[1536,768]{1,0:T(8,128)(2,1)}, f32[1536,768]{1,0:T(8,128)}, bf16[1536,768]{1,0:T(8,128)(2,1)}, bf16[1536,1536]{1,0:T(8,128)(2,1)}, bf16[51...) custom-call(f32[1536,768]{1,0:T(8,128)} %get-tuple-element.176.unit_, ...), custom_call_target="tpu_custom_call", output_to_operand_aliasing={{0}: (11, {}), {1}: (12, {}), {2}: (13, {}), {3}: (14, {})} | custom-call | flops 6899999744 | tf_op jit(solution)/shard_map/pallas_call | solution.py:667
  214.3 7.0 %shard_map.246 = (f32[1536,768]{1,0:T(8,128)}, bf16[1536,768]{1,0:T(8,128)(2,1)}, bf16[6,64,1024]{2,1,0:T(8,128)(2,1)}, f32[1,768]{1,0:T(1,128)}, f32[1,768]{1,0:T(1,128)}) custom-call(f32[1536,768]{1,0:T(8,128)} %get-tuple-element.176.unit_ref, f32[1536,1]{1,0:T(8,128)} %get-tuple-element.184.inv_ref, f32[1536,768]{1,0:T(8,128)} %get-tuple-element.185.sum_ref, ...), custom_call_target="tpu_custom_call" | custom-call | flops 9200000000 | tf_op jit(solution)/shard_map/pallas_call | solution.py:742
  222.2 5.2 %shard_map.247 = (f32[1536,768]{1,0:T(8,128)}, bf16[1536,768]{1,0:T(8,128)(2,1)}, bf16[16,64,256]{2,1,0:T(8,128)(2,1)}, f32[1,768]{1,0:T(1,128)}, f32[1,768]{1,0:T(1,128)}) custom-call(f32[1536,768]{1,0:T(8,128)} %get-tuple-element.176.unit_ref, f32[1536,1]{1,0:T(8,128)} %get-tuple-element.184.inv_ref, ...), custom_call_target="tpu_custom_call", output_to_operand_aliasing={{0}: (7, {}), {1}: (8, {})} | custom-call | flops 4600000000 | tf_op jit(solution)/shard_map/pallas_call | solution.py:742
  229.4 8.1 %all-to-all-start.3 = ((bf16[16,64,256]{2,1,0:T(8,128)(2,1)}), bf16[16,64,256]{2,1,0:T(8,128)(2,1)S(1)}, u32[]{:S(2)}, u32[]{:S(2)}) async-start(bf16[16,64,256]{2,1,0:T(8,128)(2,1)} %get-tuple-element.220), calls=%async_computation.3 | async-start | bytes 1048576 | tf_op jit(solution)/shard_map/all_to_all | solution.py:1115
  237.5 8.2 %shard_map.248 = (bf16[4,112,768]{2,1,0:T(8,128)(2,1)}, bf16[4,112,768]{2,1,0:T(8,128)(2,1)}, bf16[4,112,768]{2,1,0:T(8,128)(2,1)}, bf16[4,112,768]{2,1,0:T(8,128)(2,1)}) custom-call(s32[1]{0:T(128)} %bitcast.8.mine_ref, bf16[1536,1536]{1,0:T(8,128)(2,1)} %get-tuple-element.191.act_ref, bf16[1536,768]{1,0:T(8,128)(2,1)} %get-tuple-element.192.ffn_ref, ...), custom_call_target="tpu_custom_call" | custom-call | flops 10350000128 | tf_op jit(solution)/shard_map/pallas_call | solution.py:776
  249.2 9.7 %shard_map.249 = (bf16[4,128,768]{2,1,0:T(8,128)(2,1)}, bf16[4,128,768]{2,1,0:T(8,128)(2,1)}, bf16[4,128,768]{2,1,0:T(8,128)(2,1)}, bf16[4,128,768]{2,1,0:T(8,128)(2,1)}) custom-call(s32[1]{0:T(128)} %bitcast.8.mine_ref, bf16[1536,768]{1,0:T(8,128)(2,1)} %get-tuple-element.212.low_ref, bf16[1536,1536]{1,0:T(8,128)(2,1)} %get-tuple-element.213.pre_ref, ...), custom_call_target="tpu_custom_call" | custom-call | flops 10350000128 | tf_op jit(solution)/shard_map/pallas_call | solution.py:776
  259.8 23.0 %shard_map.250 = (bf16[16,64,256]{2,1,0:T(8,128)(2,1)}, f32[1,640]{1,0:T(1,128)}) custom-call(bf16[64,4096]{1,0:T(8,128)(2,1)} %bitcast.113, bf16[64,4096]{1,0:T(8,128)(2,1)} %bitcast.119, bf16[16,4096,256]{2,1,0:T(8,128)(2,1)} %get-tuple-element.226.w_ref), custom_call_target="tpu_custom_call" | custom-call | flops 29899999232 | tf_op jit(solution)/shard_map/pallas_call | solution.py:200
  284.0 2.9 collective-permute-start.10
  288.4 5.6 %all-to-all-start.4 = ((bf16[16,64,256]{2,1,0:T(8,128)(2,1)}), bf16[16,64,256]{2,1,0:T(8,128)(2,1)}, u32[]{:S(2)}, u32[]{:S(2)}) async-start(bf16[16,64,256]{2,1,0:T(8,128)(2,1)} %get-tuple-element.242), calls=%async_computation.4 | async-start | bytes 1048576 | tf_op jit(solution)/shard_map/all_to_all | solution.py:1115
  297.5 32.2 %shard_map.251 = (bf16[16,64,256]{2,1,0:T(8,128)(2,1)}, bf16[16,64,256]{2,1,0:T(8,128)(2,1)}) custom-call(bf16[64,4096]{1,0:T(8,128)(2,1)} %bitcast.116, bf16[64,4096]{1,0:T(8,128)(2,1)} %bitcast.118, bf16[64,4096]{1,0:T(8,128)(2,1)} %bitcast.114, bf16[64,4096]{1,0:T(8,128)(2,1)} %bitcast.120, bf16[16,4096,256]{2,1,0:T(8,128)(2,1)} %get-tuple-element.244.s_ref), custom_call_target="tpu_custom_call" | custom-call | flops 46000001024 | tf_op jit(solution)/shard_map/pallas_call | solution.py:258
  332.5 3.8 collective-permute-done.9
  341.5 2.4 collective-permute-start.38
  344.1 7.0 %all-to-all-start.5 = ((bf16[16,128,256]{2,1,0:T(8,128)(2,1)}), bf16[16,128,256]{2,1,0:T(8,128)(2,1)S(1)}, u32[]{:S(2)}, u32[]{:S(2)}) async-start(bf16[16,128,256]{2,1,0:T(8,128)(2,1)} %pad_maximum_fusion.2), calls=%async_computation.5 | async-start | bytes 2097152 | tf_op jit(solution)/shard_map/all_to_all | solution.py:1115
  353.2 2.4 collective-permute-start.29
  355.6 24.7 %shard_map.252 = (f32[6,64,1024]{2,1,0:T(8,128)}, f32[6,64,1024]{2,1,0:T(8,128)}, f32[6,64,1024]{2,1,0:T(8,128)}, f32[6,1,640]{2,1,0:T(1,128)}) custom-call(s32[2,4]{1,0:T(2,128)} %pad_add_fusion.reach_ref, s32[1,1024]{1,0:T(1,128)} %bitcast.133, s32[1088,1]{1,0:T(8,128)} %broadcast_in_dim.117.col_ref, ...), custom_call_target="tpu_custom_call" | custom-call | flops 32199999488 | tf_op jit(solution)/shard_map/pallas_call | solution.py:400
  384.0 8.4 %shard_map.253 = bf16[1152,1536]{1,0:T(8,128)(2,1)} custom-call(bf16[16,128,256]{2,1,0:T(8,128)(2,1)} %copy-done.1, bf16[16,64,256]{2,1,0:T(8,128)(2,1)} %all-to-all-done.4.refs_1_, f32[6,64,1024]{2,1,0:T(8,128)} %get-tuple-element.270.refs_2_, f32[6,64,1024]{2,1,0:T(8,128)} %get-tuple-element.271.refs_3_, f32[6,64,1024]{2,1,0:T(8,128)} %get-tuple-element.272.refs_4_, ...), custom_call_target="tpu_custom_call" | custom-call | flops 9200000000 | tf_op jit(solution)/shard_map/pallas_call | solution.py:1011
  392.4 5.4 %convolution_convert_fusion.1 = bf16[1152,768]{0,1:T(8,128)(2,1)S(1)} fusion(bf16[1152,1536]{1,0:T(8,128)(2,1)} %shard_map.253, bf16[1536,768]{1,0:T(8,128)(2,1)S(1)} %copy-done), kind=kOutput, calls=%fused_computation.2 | convolution fusion | flops 2718793728 | bytes 7667712 | tf_op jit(solution)/shard_map/dot_general | solution.py:68
  399.5 3.8 convolution_convert_fusion
  405.7 6.0 %collective-permute-start.17 = (bf16[192,1152]{1,0:T(8,128)(2,1)}, bf16[192,1152]{1,0:T(8,128)(2,1)S(1)}, u32[]{:S(2)}, u32[]{:S(2)}) collective-permute-start(bf16[192,1152]{1,0:T(8,128)(2,1)} %get-tuple-element.281), channel_id=1, source_target_pairs={{0,4},{2,6},{4,0},{6,2},{8,12},{10,14},{12,8},{14,10},{16,20},{18,... | collective-permute-start | bytes 1327112 | tf_op jit(solution)/shard_map/ppermute | solution.py:1059
  417.4 5.0 collective-permute-start.31
  422.5 6.4 %collective-permute-done.17 = bf16[192,1152]{1,0:T(8,128)(2,1)S(1)} collective-permute-done((bf16[192,1152]{1,0:T(8,128)(2,1)}, bf16[192,1152]{1,0:T(8,128)(2,1)S(1)}, u32[]{:S(2)}, u32[]{:S(2)}) %collective-permute-start.17) | collective-permute-done | bytes 442400 | tf_op jit(solution)/shard_map/ppermute | solution.py:1059
  432.0 4.5 collective-permute-start.33
  436.9 6.1 %collective-permute-done.32 = bf16[144,768]{1,0:T(8,128)(2,1)S(1)} collective-permute-done((bf16[144,768]{1,0:T(8,128)(2,1)S(1)}, bf16[144,768]{1,0:T(8,128)(2,1)S(1)}, u32[]{:S(2)}, u32[]{:S(2)}) %collective-permute-start.32) | collective-permute-done | bytes 221216 | tf_op jit(solution)/shard_map/ppermute | solution.py:1059
  443.5 3.5 collective-permute-start.20
  447.7 2.6 collective-permute-start.21
  451.3 2.7 collective-permute-start.34
  454.2 2.8 collective-permute-start.35
  457.1 5.4 %collective-permute-start.36 = (bf16[4,144,768]{2,1,0:T(8,128)(2,1)}, bf16[4,144,768]{2,1,0:T(8,128)(2,1)}, u32[]{:S(2)}, u32[]{:S(2)}) collective-permute-start(bf16[4,144,768]{2,1,0:T(8,128)(2,1)} %pad_maximum_fusion.3.refs_0_), channel_id=1, source_target_pairs={{0,6},{2,4},{4,2},{6,0},{8,14},{10,12},{12,10},{14,8},{16,22},{18,... | collective-permute-start | bytes 2654216 | tf_op jit(solution)/shard_map/ppermute | solution.py:1059
  463.3 4.4 shard_map.255
  468.8 3.3 collective-permute-start.24
  473.5 2.5 collective-permute-done.24
  477.0 4.1 collective-permute-start.26
  481.2 18.0 %collective-permute-done.35.refs_2_ = bf16[4,144,768]{2,1,0:T(8,128)(2,1)} collective-permute-done((bf16[4,144,768]{2,1,0:T(8,128)(2,1)}, bf16[4,144,768]{2,1,0:T(8,128)(2,1)}, u32[]{:S(2)}, u32[]{:S(2)}) %collective-permute-start.35) | collective-permute-done | bytes 884768 | tf_op jit(solution)/shard_map/ppermute | solution.py:1059
  499.1 2.8 collective-permute-start.27
  501.9 4.9 shard_map.254
  508.3 3.8 collective-permute-done.26
  517.3 4.6 add_add_fusion
  (209 shorter events, 77.0 us)
Async XLA Ops:
  10.6 42.6 %all-to-all-start = ((bf16[16,192,256]{2,1,0:T(8,128)(2,1)}), bf16[16,192,256]{2,1,0:T(8,128)(2,1)S(1)}, u32[]{:S(2)}, u32[]{:S(2)}) async-start(bf16[16,192,256]{2,1,0:T(8,128)(2,1)} %get-tuple-element.154), calls=%async_computation | async-start | bytes 3145728 | tf_op jit(solution)/shard_map/all_to_all | solution.py:1115
  127.2 18.3 %collective-permute-start = (bf16[1024,768]{1,0:T(8,128)(2,1)S(1)}, bf16[1024,768]{1,0:T(8,128)(2,1)S(1)}, u32[]{:S(2)}, u32[]{:S(2)}) collective-permute-start(bf16[1024,768]{1,0:T(8,128)(2,1)S(1)} %copy-done.23), channel_id=1, source_target_pairs={{0,1},{1,0},{2,3},{3,2},{4,5},{5,4},{6,7},{7,6},{8,9},{9,8},{10,11... | collective-permute-start | bytes 4718600 | tf_op jit(solution)/shard_map/ppermute | solution.py:1032
  130.3 31.0 %all-to-all-start.1 = ((bf16[16,32,256]{2,1,0:T(8,128)(2,1)}), bf16[16,32,256]{2,1,0:T(8,128)(2,1)S(1)}, u32[]{:S(2)}, u32[]{:S(2)}) async-start(bf16[16,32,256]{2,1,0:T(8,128)(2,1)} %get-tuple-element.324), calls=%async_computation.1 | async-start | bytes 524288 | tf_op jit(solution)/shard_map/all_to_all | solution.py:1115
  161.3 8.3 %collective-permute-start.1 = (bf16[1024,768]{1,0:T(8,128)(2,1)}, bf16[1024,768]{1,0:T(8,128)(2,1)S(1)}, u32[]{:S(2)}, u32[]{:S(2)}) collective-permute-start(bf16[1024,768]{1,0:T(8,128)(2,1)} %get-tuple-element.167.own_ref), channel_id=1, source_target_pairs={{0,1},{1,0},{2,3},{3,2},{4,5},{5,4},{6,7},{7,6},{8,9},{9,8},{10,11... | collective-permute-start | bytes 4718600 | tf_op jit(solution)/shard_map/ppermute | solution.py:1032
  162.7 21.3 %all-to-all-start.2 = ((bf16[16,32,256]{2,1,0:T(8,128)(2,1)}), bf16[16,32,256]{2,1,0:T(8,128)(2,1)S(1)}, u32[]{:S(2)}, u32[]{:S(2)}) async-start(bf16[16,32,256]{2,1,0:T(8,128)(2,1)} %get-tuple-element.165), calls=%async_computation.2 | async-start | bytes 524288 | tf_op jit(solution)/shard_map/all_to_all | solution.py:1115
  188.1 26.2 %collective-permute-start.5 = (bf16[1024,768]{1,0:T(8,128)(2,1)S(1)}, bf16[1024,768]{1,0:T(8,128)(2,1)}, u32[]{:S(2)}, u32[]{:S(2)}) collective-permute-start(bf16[1024,768]{1,0:T(8,128)(2,1)S(1)} %copy-done.22), channel_id=1, source_target_pairs={{0,1},{1,0},{2,3},{3,2},{4,5},{5,4},{6,7},{7,6},{8,9},{9,8},{10,11... | collective-permute-start | bytes 4718600 | tf_op jit(solution)/shard_map/ppermute | solution.py:1032
  200.5 2.5 collective-permute-start.3
  212.7 8.6 %collective-permute-start.4 = (bf16[512,768]{1,0:T(8,128)(2,1)}, bf16[512,768]{1,0:T(8,128)(2,1)S(1)}, u32[]{:S(2)}, u32[]{:S(2)}) collective-permute-start(bf16[512,768]{1,0:T(8,128)(2,1)} %get-tuple-element.186.own_ref), channel_id=1, source_target_pairs={{0,1},{1,0},{2,3},{3,2},{4,5},{5,4},{6,7},{7,6},{8,9},{9,8},{10,11... | collective-permute-start | bytes 2359304 | tf_op jit(solution)/shard_map/ppermute | solution.py:1032
  229.4 29.5 %all-to-all-start.3 = ((bf16[16,64,256]{2,1,0:T(8,128)(2,1)}), bf16[16,64,256]{2,1,0:T(8,128)(2,1)S(1)}, u32[]{:S(2)}, u32[]{:S(2)}) async-start(bf16[16,64,256]{2,1,0:T(8,128)(2,1)} %get-tuple-element.220), calls=%async_computation.3 | async-start | bytes 1048576 | tf_op jit(solution)/shard_map/all_to_all | solution.py:1115
  245.7 37.1 %collective-permute-start.6 = (bf16[4,112,768]{2,1,0:T(8,128)(2,1)}, bf16[4,112,768]{2,1,0:T(8,128)(2,1)S(1)}, u32[]{:S(2)}, u32[]{:S(2)}) collective-permute-start(bf16[4,112,768]{2,1,0:T(8,128)(2,1)} %get-tuple-element.208), channel_id=1, source_target_pairs={{0,2},{2,0},{4,6},{6,4},{8,10},{10,8},{12,14},{14,12},{16,18},{18,... | collective-permute-start | bytes 2064392 | tf_op jit(solution)/shard_map/ppermute | solution.py:1059
  247.8 35.1 %collective-permute-start.7 = (bf16[4,112,768]{2,1,0:T(8,128)(2,1)}, bf16[4,112,768]{2,1,0:T(8,128)(2,1)S(1)}, u32[]{:S(2)}, u32[]{:S(2)}) collective-permute-start(bf16[4,112,768]{2,1,0:T(8,128)(2,1)} %get-tuple-element.209), channel_id=1, source_target_pairs={{0,4},{2,6},{4,0},{6,2},{8,12},{10,14},{12,8},{14,10},{16,20},{18,... | collective-permute-start | bytes 2064392 | tf_op jit(solution)/shard_map/ppermute | solution.py:1059
  249.2 33.6 %collective-permute-start.8 = (bf16[4,112,768]{2,1,0:T(8,128)(2,1)}, bf16[4,112,768]{2,1,0:T(8,128)(2,1)S(1)}, u32[]{:S(2)}, u32[]{:S(2)}) collective-permute-start(bf16[4,112,768]{2,1,0:T(8,128)(2,1)} %get-tuple-element.210), channel_id=1, source_target_pairs={{0,6},{2,4},{4,2},{6,0},{8,14},{10,12},{12,10},{14,8},{16,22},{18,... | collective-permute-start | bytes 2064392 | tf_op jit(solution)/shard_map/ppermute | solution.py:1059
  284.0 46.5 %collective-permute-start.10 = (bf16[112,768]{1,0:T(8,128)(2,1)}, bf16[112,768]{1,0:T(8,128)(2,1)S(1)}, u32[]{:S(2)}, u32[]{:S(2)}) collective-permute-start(bf16[112,768]{1,0:T(8,128)(2,1)} %get-tuple-element.235), channel_id=1, source_target_pairs={{0,16},{2,18},{4,20},{6,22},{8,24},{10,26},{12,28},{14,30},{16,0},... | collective-permute-start | bytes 516104 | tf_op jit(solution)/shard_map/ppermute | solution.py:1059
  286.9 45.6 %collective-permute-start.11 = (bf16[112,768]{1,0:T(8,128)(2,1)}, bf16[112,768]{1,0:T(8,128)(2,1)}, u32[]{:S(2)}, u32[]{:S(2)}) collective-permute-start(bf16[112,768]{1,0:T(8,128)(2,1)} %get-tuple-element.236), channel_id=1, source_target_pairs={{0,24},{2,26},{4,28},{6,30},{8,16},{10,18},{12,20},{14,22},{16,8},... | collective-permute-start | bytes 516104 | tf_op jit(solution)/shard_map/ppermute | solution.py:1059
  288.4 47.9 %all-to-all-start.4 = ((bf16[16,64,256]{2,1,0:T(8,128)(2,1)}), bf16[16,64,256]{2,1,0:T(8,128)(2,1)}, u32[]{:S(2)}, u32[]{:S(2)}) async-start(bf16[16,64,256]{2,1,0:T(8,128)(2,1)} %get-tuple-element.242), calls=%async_computation.4 | async-start | bytes 1048576 | tf_op jit(solution)/shard_map/all_to_all | solution.py:1115
  294.0 42.3 %collective-permute-start.12 = (bf16[4,128,768]{2,1,0:T(8,128)(2,1)}, bf16[4,128,768]{2,1,0:T(8,128)(2,1)S(1)}, u32[]{:S(2)}, u32[]{:S(2)}) collective-permute-start(bf16[4,128,768]{2,1,0:T(8,128)(2,1)} %get-tuple-element.238), channel_id=1, source_target_pairs={{0,2},{2,0},{4,6},{6,4},{8,10},{10,8},{12,14},{14,12},{16,18},{18,... | collective-permute-start | bytes 2359304 | tf_op jit(solution)/shard_map/ppermute | solution.py:1059
  295.9 40.4 %collective-permute-start.13 = (bf16[4,128,768]{2,1,0:T(8,128)(2,1)}, bf16[4,128,768]{2,1,0:T(8,128)(2,1)S(1)}, u32[]{:S(2)}, u32[]{:S(2)}) collective-permute-start(bf16[4,128,768]{2,1,0:T(8,128)(2,1)} %get-tuple-element.239), channel_id=1, source_target_pairs={{0,4},{2,6},{4,0},{6,2},{8,12},{10,14},{12,8},{14,10},{16,20},{18,... | collective-permute-start | bytes 2359304 | tf_op jit(solution)/shard_map/ppermute | solution.py:1059
  297.3 38.9 %collective-permute-start.14 = (bf16[4,128,768]{2,1,0:T(8,128)(2,1)}, bf16[4,128,768]{2,1,0:T(8,128)(2,1)S(1)}, u32[]{:S(2)}, u32[]{:S(2)}) collective-permute-start(bf16[4,128,768]{2,1,0:T(8,128)(2,1)} %get-tuple-element.240), channel_id=1, source_target_pairs={{0,6},{2,4},{4,2},{6,0},{8,14},{10,12},{12,10},{14,8},{16,22},{18,... | collective-permute-start | bytes 2359304 | tf_op jit(solution)/shard_map/ppermute | solution.py:1059
  330.5 5.7 %collective-permute-start.9 = (bf16[112,768]{1,0:T(8,128)(2,1)}, bf16[112,768]{1,0:T(8,128)(2,1)}, u32[]{:S(2)}, u32[]{:S(2)}) collective-permute-start(bf16[112,768]{1,0:T(8,128)(2,1)} %get-tuple-element.234), channel_id=1, source_target_pairs={{0,8},{2,10},{4,12},{6,14},{8,0},{10,2},{12,4},{14,6},{16,24},{18,... | collective-permute-start | bytes 516104 | tf_op jit(solution)/shard_map/ppermute | solution.py:1059
  339.7 40.7 %collective-permute-start.37 = (bf16[112,768]{1,0:T(8,128)(2,1)S(1)}, bf16[112,768]{1,0:T(8,128)(2,1)S(1)}, u32[]{:S(2)}, u32[]{:S(2)}) collective-permute-start(bf16[112,768]{1,0:T(8,128)(2,1)S(1)} %add_convert_fusion.4), channel_id=1, source_target_pairs={{0,8},{2,10},{4,12},{6,14},{8,0},{10,2},{12,4},{14,6},{16,24},{18,... | collective-permute-start | bytes 516104 | tf_op jit(solution)/shard_map/ppermute | solution.py:1059
  341.5 38.9 %collective-permute-start.38 = (bf16[112,768]{1,0:T(8,128)(2,1)S(1)}, bf16[112,768]{1,0:T(8,128)(2,1)S(1)}, u32[]{:S(2)}, u32[]{:S(2)}) collective-permute-start(bf16[112,768]{1,0:T(8,128)(2,1)S(1)} %add_convert_fusion.4), channel_id=1, source_target_pairs={{0,16},{2,18},{4,20},{6,22},{8,24},{10,26},{12,28},{14,30},{16,0},... | collective-permute-start | bytes 516104 | tf_op jit(solution)/shard_map/ppermute | solution.py:1059
  343.9 36.6 %collective-permute-start.39 = (bf16[112,768]{1,0:T(8,128)(2,1)S(1)}, bf16[112,768]{1,0:T(8,128)(2,1)S(1)}, u32[]{:S(2)}, u32[]{:S(2)}) collective-permute-start(bf16[112,768]{1,0:T(8,128)(2,1)S(1)} %add_convert_fusion.4), channel_id=1, source_target_pairs={{0,24},{2,26},{4,28},{6,30},{8,16},{10,18},{12,20},{14,22},{16,8},... | collective-permute-start | bytes 516104 | tf_op jit(solution)/shard_map/ppermute | solution.py:1059
  344.1 38.9 %all-to-all-start.5 = ((bf16[16,128,256]{2,1,0:T(8,128)(2,1)}), bf16[16,128,256]{2,1,0:T(8,128)(2,1)S(1)}, u32[]{:S(2)}, u32[]{:S(2)}) async-start(bf16[16,128,256]{2,1,0:T(8,128)(2,1)} %pad_maximum_fusion.2), calls=%async_computation.5 | async-start | bytes 2097152 | tf_op jit(solution)/shard_map/all_to_all | solution.py:1115
  351.1 60.6 %collective-permute-start.28 = (bf16[128,768]{1,0:T(8,128)(2,1)}, bf16[128,768]{1,0:T(8,128)(2,1)}, u32[]{:S(2)}, u32[]{:S(2)}) collective-permute-start(bf16[128,768]{1,0:T(8,128)(2,1)} %get-tuple-element.284), channel_id=1, source_target_pairs={{0,8},{2,10},{4,12},{6,14},{8,0},{10,2},{12,4},{14,6},{16,24},{18,... | collective-permute-start | bytes 589832 | tf_op jit(solution)/shard_map/ppermute | solution.py:1059
  353.2 58.6 %collective-permute-start.29 = (bf16[128,768]{1,0:T(8,128)(2,1)}, bf16[128,768]{1,0:T(8,128)(2,1)}, u32[]{:S(2)}, u32[]{:S(2)}) collective-permute-start(bf16[128,768]{1,0:T(8,128)(2,1)} %get-tuple-element.285), channel_id=1, source_target_pairs={{0,16},{2,18},{4,20},{6,22},{8,24},{10,26},{12,28},{14,30},{16,0},... | collective-permute-start | bytes 589832 | tf_op jit(solution)/shard_map/ppermute | solution.py:1059
  380.3 33.0 %collective-permute-start.30 = (bf16[128,768]{1,0:T(8,128)(2,1)}, bf16[128,768]{1,0:T(8,128)(2,1)}, u32[]{:S(2)}, u32[]{:S(2)}) collective-permute-start(bf16[128,768]{1,0:T(8,128)(2,1)} %get-tuple-element.286), channel_id=1, source_target_pairs={{0,24},{2,26},{4,28},{6,30},{8,16},{10,18},{12,20},{14,22},{16,8},... | collective-permute-start | bytes 589832 | tf_op jit(solution)/shard_map/ppermute | solution.py:1059
  404.3 13.2 %collective-permute-start.16 = (bf16[192,1152]{1,0:T(8,128)(2,1)}, bf16[192,1152]{1,0:T(8,128)(2,1)S(1)}, u32[]{:S(2)}, u32[]{:S(2)}) collective-permute-start(bf16[192,1152]{1,0:T(8,128)(2,1)} %get-tuple-element.280), channel_id=1, source_target_pairs={{0,2},{2,0},{4,6},{6,4},{8,10},{10,8},{12,14},{14,12},{16,18},{18,... | collective-permute-start | bytes 1327112 | tf_op jit(solution)/shard_map/ppermute | solution.py:1059
  405.7 23.1 %collective-permute-start.17 = (bf16[192,1152]{1,0:T(8,128)(2,1)}, bf16[192,1152]{1,0:T(8,128)(2,1)S(1)}, u32[]{:S(2)}, u32[]{:S(2)}) collective-permute-start(bf16[192,1152]{1,0:T(8,128)(2,1)} %get-tuple-element.281), channel_id=1, source_target_pairs={{0,4},{2,6},{4,0},{6,2},{8,12},{10,14},{12,8},{14,10},{16,20},{18,... | collective-permute-start | bytes 1327112 | tf_op jit(solution)/shard_map/ppermute | solution.py:1059
  411.8 20.2 %collective-permute-start.18 = (bf16[192,1152]{1,0:T(8,128)(2,1)S(1)}, bf16[192,1152]{1,0:T(8,128)(2,1)S(1)}, u32[]{:S(2)}, u32[]{:S(2)}) collective-permute-start(bf16[192,1152]{1,0:T(8,128)(2,1)S(1)} %get-tuple-element.282), channel_id=1, source_target_pairs={{0,6},{2,4},{4,2},{6,0},{8,14},{10,12},{12,10},{14,8},{16,22},{18,... | collective-permute-start | bytes 1327112 | tf_op jit(solution)/shard_map/ppermute | solution.py:1059
  411.8 45.2 %collective-permute-start.40 = (bf16[4,112,768]{2,1,0:T(8,128)(2,1)}, bf16[4,112,768]{2,1,0:T(8,128)(2,1)S(1)}, u32[]{:S(2)}, u32[]{:S(2)}) collective-permute-start(bf16[4,112,768]{2,1,0:T(8,128)(2,1)} %pad_maximum_fusion.4.refs_0_), channel_id=1, source_target_pairs={{0,2},{2,0},{4,6},{6,4},{8,10},{10,8},{12,14},{14,12},{16,18},{18,... | collective-permute-start | bytes 2064392 | tf_op jit(solution)/shard_map/ppermute | solution.py:1059
  413.3 49.1 %collective-permute-start.41 = (bf16[4,112,768]{2,1,0:T(8,128)(2,1)}, bf16[4,112,768]{2,1,0:T(8,128)(2,1)S(1)}, u32[]{:S(2)}, u32[]{:S(2)}) collective-permute-start(bf16[4,112,768]{2,1,0:T(8,128)(2,1)} %pad_maximum_fusion.4.refs_0_), channel_id=1, source_target_pairs={{0,4},{2,6},{4,0},{6,2},{8,12},{10,14},{12,8},{14,10},{16,20},{18,... | collective-permute-start | bytes 2064392 | tf_op jit(solution)/shard_map/ppermute | solution.py:1059
  417.4 19.3 %collective-permute-start.31 = (bf16[144,768]{1,0:T(8,128)(2,1)S(1)}, bf16[144,768]{1,0:T(8,128)(2,1)S(1)}, u32[]{:S(2)}, u32[]{:S(2)}) collective-permute-start(bf16[144,768]{1,0:T(8,128)(2,1)S(1)} %get-tuple-element.333), channel_id=1, source_target_pairs={{0,8},{2,10},{4,12},{6,14},{8,0},{10,2},{12,4},{14,6},{16,24},{18,... | collective-permute-start | bytes 663560 | tf_op jit(solution)/shard_map/ppermute | solution.py:1059
  428.8 14.1 %collective-permute-start.32 = (bf16[144,768]{1,0:T(8,128)(2,1)S(1)}, bf16[144,768]{1,0:T(8,128)(2,1)S(1)}, u32[]{:S(2)}, u32[]{:S(2)}) collective-permute-start(bf16[144,768]{1,0:T(8,128)(2,1)S(1)} %get-tuple-element.333), channel_id=1, source_target_pairs={{0,16},{2,18},{4,20},{6,22},{8,24},{10,26},{12,28},{14,30},{16,0},... | collective-permute-start | bytes 663560 | tf_op jit(solution)/shard_map/ppermute | solution.py:1059
  432.0 11.5 %collective-permute-start.33 = (bf16[144,768]{1,0:T(8,128)(2,1)S(1)}, bf16[144,768]{1,0:T(8,128)(2,1)S(1)}, u32[]{:S(2)}, u32[]{:S(2)}) collective-permute-start(bf16[144,768]{1,0:T(8,128)(2,1)S(1)} %get-tuple-element.333), channel_id=1, source_target_pairs={{0,24},{2,26},{4,28},{6,30},{8,16},{10,18},{12,20},{14,22},{16,8},... | collective-permute-start | bytes 663560 | tf_op jit(solution)/shard_map/ppermute | solution.py:1059
  436.8 26.5 %collective-permute-start.42 = (bf16[4,112,768]{2,1,0:T(8,128)(2,1)S(1)}, bf16[4,112,768]{2,1,0:T(8,128)(2,1)}, u32[]{:S(2)}, u32[]{:S(2)}) collective-permute-start(bf16[4,112,768]{2,1,0:T(8,128)(2,1)S(1)} %copy-done.6), channel_id=1, source_target_pairs={{0,6},{2,4},{4,2},{6,0},{8,14},{10,12},{12,10},{14,8},{16,22},{18,... | collective-permute-start | bytes 2064392 | tf_op jit(solution)/shard_map/ppermute | solution.py:1059
  442.9 4.7 collective-permute-start.19
  443.5 7.8 %collective-permute-start.20 = (bf16[48,1152]{1,0:T(8,128)(2,1)S(1)}, bf16[48,1152]{1,0:T(8,128)(2,1)S(1)}, u32[]{:S(2)}, u32[]{:S(2)}) collective-permute-start(bf16[48,1152]{1,0:T(8,128)(2,1)S(1)} %get-tuple-element.331), channel_id=1, source_target_pairs={{0,16},{2,18},{4,20},{6,22},{8,24},{10,26},{12,28},{14,30},{16,0},... | collective-permute-start | bytes 331784 | tf_op jit(solution)/shard_map/ppermute | solution.py:1059
  447.7 6.5 %collective-permute-start.21 = (bf16[48,1152]{1,0:T(8,128)(2,1)S(1)}, bf16[48,1152]{1,0:T(8,128)(2,1)S(1)}, u32[]{:S(2)}, u32[]{:S(2)}) collective-permute-start(bf16[48,1152]{1,0:T(8,128)(2,1)S(1)} %get-tuple-element.330), channel_id=1, source_target_pairs={{0,24},{2,26},{4,28},{6,30},{8,16},{10,18},{12,20},{14,22},{16,8},... | collective-permute-start | bytes 331784 | tf_op jit(solution)/shard_map/ppermute | solution.py:1059
  451.3 25.7 %collective-permute-start.34 = (bf16[4,144,768]{2,1,0:T(8,128)(2,1)}, bf16[4,144,768]{2,1,0:T(8,128)(2,1)}, u32[]{:S(2)}, u32[]{:S(2)}) collective-permute-start(bf16[4,144,768]{2,1,0:T(8,128)(2,1)} %pad_maximum_fusion.3.refs_0_), channel_id=1, source_target_pairs={{0,2},{2,0},{4,6},{6,4},{8,10},{10,8},{12,14},{14,12},{16,18},{18,... | collective-permute-start | bytes 2654216 | tf_op jit(solution)/shard_map/ppermute | solution.py:1059
  454.2 44.9 %collective-permute-start.35 = (bf16[4,144,768]{2,1,0:T(8,128)(2,1)}, bf16[4,144,768]{2,1,0:T(8,128)(2,1)}, u32[]{:S(2)}, u32[]{:S(2)}) collective-permute-start(bf16[4,144,768]{2,1,0:T(8,128)(2,1)} %pad_maximum_fusion.3.refs_0_), channel_id=1, source_target_pairs={{0,4},{2,6},{4,0},{6,2},{8,12},{10,14},{12,8},{14,10},{16,20},{18,... | collective-permute-start | bytes 2654216 | tf_op jit(solution)/shard_map/ppermute | solution.py:1059
  457.1 44.9 %collective-permute-start.36 = (bf16[4,144,768]{2,1,0:T(8,128)(2,1)}, bf16[4,144,768]{2,1,0:T(8,128)(2,1)}, u32[]{:S(2)}, u32[]{:S(2)}) collective-permute-start(bf16[4,144,768]{2,1,0:T(8,128)(2,1)} %pad_maximum_fusion.3.refs_0_), channel_id=1, source_target_pairs={{0,6},{2,4},{4,2},{6,0},{8,14},{10,12},{12,10},{14,8},{16,22},{18,... | collective-permute-start | bytes 2654216 | tf_op jit(solution)/shard_map/ppermute | solution.py:1059
  463.3 5.5 %collective-permute-start.22 = (bf16[48,1152]{1,0:T(8,128)(2,1)S(1)}, bf16[48,1152]{1,0:T(8,128)(2,1)S(1)}, u32[]{:S(2)}, u32[]{:S(2)}) collective-permute-start(bf16[48,1152]{1,0:T(8,128)(2,1)S(1)} %fusion.9), channel_id=1, source_target_pairs={{0,8},{2,10},{4,12},{6,14},{8,0},{10,2},{12,4},{14,6},{16,24},{18,... | collective-permute-start | bytes 331784 | tf_op jit(solution)/shard_map/ppermute | solution.py:1059
  467.6 5.9 %collective-permute-start.23 = (bf16[48,1152]{1,0:T(8,128)(2,1)S(1)}, bf16[48,1152]{1,0:T(8,128)(2,1)S(1)}, u32[]{:S(2)}, u32[]{:S(2)}) collective-permute-start(bf16[48,1152]{1,0:T(8,128)(2,1)S(1)} %fusion.9), channel_id=1, source_target_pairs={{0,16},{2,18},{4,20},{6,22},{8,24},{10,26},{12,28},{14,30},{16,0},... | collective-permute-start | bytes 331784 | tf_op jit(solution)/shard_map/ppermute | solution.py:1059
  468.8 7.3 %collective-permute-start.24 = (bf16[48,1152]{1,0:T(8,128)(2,1)S(1)}, bf16[48,1152]{1,0:T(8,128)(2,1)S(1)}, u32[]{:S(2)}, u32[]{:S(2)}) collective-permute-start(bf16[48,1152]{1,0:T(8,128)(2,1)S(1)} %fusion.9), channel_id=1, source_target_pairs={{0,24},{2,26},{4,28},{6,30},{8,16},{10,18},{12,20},{14,22},{16,8},... | collective-permute-start | bytes 331784 | tf_op jit(solution)/shard_map/ppermute | solution.py:1059
  473.5 42.7 %collective-permute-start.15 = (bf16[1536,768]{1,0:T(8,128)(2,1)S(1)}, bf16[1536,768]{1,0:T(8,128)(2,1)}, u32[]{:S(2)}, u32[]{:S(2)}) collective-permute-start(bf16[1536,768]{1,0:T(8,128)(2,1)S(1)} %convolution_convert_fusion), channel_id=1, source_target_pairs={{0,1},{1,0},{2,3},{3,2},{4,5},{5,4},{6,7},{7,6},{8,9},{9,8},{10,11... | collective-permute-start | bytes 7077896 | tf_op jit(solution)/shard_map/ppermute | solution.py:1032
  476.2 32.0 %collective-permute-start.25 = (bf16[192,1152]{1,0:T(8,128)(2,1)S(1)}, bf16[192,1152]{1,0:T(8,128)(2,1)S(1)}, u32[]{:S(2)}, u32[]{:S(2)}) collective-permute-start(bf16[192,1152]{1,0:T(8,128)(2,1)S(1)} %bitcast.105), channel_id=1, source_target_pairs={{0,2},{2,0},{4,6},{6,4},{8,10},{10,8},{12,14},{14,12},{16,18},{18,... | collective-permute-start | bytes 1327112 | tf_op jit(solution)/shard_map/ppermute | solution.py:1059
  477.0 35.1 %collective-permute-start.26 = (bf16[192,1152]{1,0:T(8,128)(2,1)S(1)}, bf16[192,1152]{1,0:T(8,128)(2,1)}, u32[]{:S(2)}, u32[]{:S(2)}) collective-permute-start(bf16[192,1152]{1,0:T(8,128)(2,1)S(1)} %bitcast.106), channel_id=1, source_target_pairs={{0,4},{2,6},{4,0},{6,2},{8,12},{10,14},{12,8},{14,10},{16,20},{18,... | collective-permute-start | bytes 1327112 | tf_op jit(solution)/shard_map/ppermute | solution.py:1059
  499.1 13.0 %collective-permute-start.27 = (bf16[192,1152]{1,0:T(8,128)(2,1)S(1)}, bf16[192,1152]{1,0:T(8,128)(2,1)}, u32[]{:S(2)}, u32[]{:S(2)}) collective-permute-start(bf16[192,1152]{1,0:T(8,128)(2,1)S(1)} %bitcast.107), channel_id=1, source_target_pairs={{0,6},{2,4},{4,2},{6,0},{8,14},{10,12},{12,10},{14,8},{16,22},{18,... | collective-permute-start | bytes 1327112 | tf_op jit(solution)/shard_map/ppermute | solution.py:1059
  (36 other events, 454.6 us)
where the time goes:
time: 532 us; the launch traced here: 522 us
  Pallas kernels  288 us (54%)
  starting transfers between devices  126 us (24%)
  waiting for transfers between devices  50.8 us (10%)
  local copies, waits for them, and re-layouts  28.2 us (5%)
  other arithmetic  19.1 us (4%)
  matrix products  9.21 us (2%)
    ppermute x36, starting transfers between devices, terms_sent(): lax.ppermute(term, 'seq', [(i, i ^ away << bits[0]) for i in range(peers)])  73.1 us
    pallas_call x1, Pallas kernels, long_forward(): pl.pallas_call(body, grid=(blocks,), in_specs=[pl.BlockSpec((head_dim, PI...  71.3 us
    all_to_all x6, starting transfers between devices, exchange(): return lax.all_to_all(pieces, 'seq', 0, 0, axis_index_groups=groups)  51.1 us
    ppermute x36, waiting for transfers between devices, terms_sent(): lax.ppermute(term, 'seq', [(i, i ^ away << bits[0]) for i in range(peers)])  44.3 us
    pallas_call x1, Pallas kernels, long_back_pairs(): pl.pallas_call(body, grid=(blocks,), in_specs=[piece, whole, whole, piece...  32.2 us
    pallas_call x1, Pallas kernels, short_forward(): pl.pallas_call(body, grid=(blocks,), in_specs=[pl.BlockSpec(memory_space=...  26.4 us
    pallas_call x1, Pallas kernels, short_backward(): pl.pallas_call(body, grid=(blocks,), in_specs=[pl.BlockSpec(memory_space=...  24.7 us
    pallas_call x2, Pallas kernels, feed_forward(): pl.pallas_call(body, grid=(count,), in_specs=[rows, own_rows, own_rows, l...  23.9 us
  transfers between devices with their start and end apart: 49, of which 14 were waited for; matrix products, arithmetic and copies ran while one was open for 6% of the time, Pallas kernels for 38%

commit v1 on v0

--- a/solution.py
+++ b/solution.py
@@ -219,7 +219,7 @@
             pltpu.VMEM((BAND_ROWS, PIECE), F32),
         ],
         compiler_params=pltpu.CompilerParams(vmem_limit_bytes=VMEM_BYTES),
-        cost_estimate=lasting(26),
+        cost_estimate=lasting(1),
     )(value, grad, weights)
 
 
@@ -531,20 +531,18 @@
     )(short_att, out_weight)
 
 
-def project_out_long(moved_low, moved_high, out_weight, mixed):
+def project_out_long(moved, out_weight, mixed):
     cols, width = out_weight.shape
-    half = moved_low.shape[1]
-    head_dim = 2 * half
+    head_dim = moved.shape[1]
     heads = cols // head_dim
     span = ITEMS * PIECE
 
-    def body(low_ref, high_ref, w_ref, old_ref, mixed_ref, part_ref, items):
+    def body(m_ref, w_ref, old_ref, mixed_ref, part_ref, items):
         for h in range(heads):
             for item in range(ITEMS):
-                for at, ref in ((0, low_ref), (half, high_ref)):
-                    items[pl.ds(h * head_dim + at, half), pl.ds(item * PIECE, PIECE)] = ref[
-                        item * heads + h
-                    ]
+                items[pl.ds(h * head_dim, head_dim), pl.ds(item * PIECE, PIECE)] = m_ref[
+                    item * heads + h
+                ]
         placed = contract(items[...], place_of_item(span), 1, 0).astype(BF16)
         mixed_ref[...] = placed
         part_ref[...] = contract(placed, w_ref[...], 0, 0).astype(BF16)
@@ -553,8 +551,7 @@
         body,
         grid=(1,),
         in_specs=[
-            pl.BlockSpec((GROUP, half, PIECE), lambda i: (0, 0, 0)),
-            pl.BlockSpec((GROUP, half, PIECE), lambda i: (0, 0, 0)),
+            pl.BlockSpec((GROUP, head_dim, PIECE), lambda i: (0, 0, 0)),
             pl.BlockSpec((cols, width), lambda i: (0, 0)),
             ANYWHERE,
         ],
@@ -567,10 +564,10 @@
             jax.ShapeDtypeStruct((span, width), BF16),
         ],
         scratch_shapes=[pltpu.VMEM((cols, span), BF16)],
-        input_output_aliases={3: 0},
+        input_output_aliases={2: 0},
         compiler_params=pltpu.CompilerParams(vmem_limit_bytes=VMEM_BYTES),
         cost_estimate=lasting(3),
-    )(moved_low, moved_high, out_weight, mixed)
+    )(moved, out_weight, mixed)
 
 
 def feed_forward(first, tokens, own, other, gain, bias, inner_weight, outer_weight, into=()):
@@ -899,33 +896,33 @@
     )(gathered)
 
 
-def placed_sums(mine, arrays, counts, targets, shapes):
+def placed_sums(mine, arrays, aways, counts, targets, shapes):
     width = arrays[0].shape[2]
 
     def body(mine_ref, *refs):
         ins, outs = refs[: len(arrays)], refs[len(arrays) :]
-        for first_away, ref in enumerate(ins):
+        pieces = [(ref, at, *away) for ref, pairs in zip(ins, aways) for at, away in enumerate(pairs)]
+        for ref, piece, first_away, second_away in pieces:
             first = lax.bitwise_xor(mine_ref[0], first_away)
-            for second_away in range(ref.shape[0]):
-                second = lax.bitwise_xor(mine_ref[1], second_away)
-                order = first * ref.shape[0] + second
-                at = 0
-                for count, target in zip(counts, targets):
-                    rows = pl.ds(at, count)
-                    at += count
-                    if target is None:
-                        continue
-                    out = outs[target[0]]
-                    if target[1] is not None:
-                        to = pl.ds(pl.multiple_of(order * count, count), count)
-                        out[to, pl.ds(target[1], width)] = ref[second_away, rows, :].astype(F32)
-                    elif out.shape[0] > 4:
-                        out[pl.ds(order, 1), :] = ref[second_away, rows, :].astype(F32)[:1]
-                    else:
-
-                        @pl.when(second == 0)
-                        def _():
-                            out[pl.ds(first, 1), :] = ref[second_away, rows, :].astype(F32)[:1]
+            second = lax.bitwise_xor(mine_ref[1], second_away)
+            order = first * 4 + second
+            at = 0
+            for count, target in zip(counts, targets):
+                rows = pl.ds(at, count)
+                at += count
+                if target is None:
+                    continue
+                out = outs[target[0]]
+                if target[1] is not None:
+                    to = pl.ds(pl.multiple_of(order * count, count), count)
+                    out[to, pl.ds(target[1], width)] = ref[piece, rows, :].astype(F32)
+                elif out.shape[0] > 4:
+                    out[pl.ds(order, 1), :] = ref[piece, rows, :].astype(F32)[:1]
+                else:
+
+                    @pl.when(second == 0)
+                    def _():
+                        out[pl.ds(first, 1), :] = ref[piece, rows, :].astype(F32)[:1]
 
     def whole(shape):
         return pl.BlockSpec(shape, lambda: (0,) * len(shape))
@@ -940,22 +937,54 @@
     )(mine, *arrays)
 
 
-def gathered_or_placed(part, steps, counts, targets, shapes):
+def by_twos(steps):
+    return len(steps) == 2 and all(len(bits) == 2 for bits in steps)
+
+
+def across(array, mask):
+    peers = lax.axis_size("seq")
+    return lax.ppermute(array, "seq", [(i, i ^ mask) for i in range(peers)])
+
+
+def gather_second(part, steps):
+    if not by_twos(steps):
+        return part
+    came = [came[None] for came in terms_sent([part] * 4, steps[1])]
+    return jnp.concatenate([part[None]] + came, axis=0)
+
+
+def gather_near(own, steps):
+    return (across(own[:2], 1), across(own[2:], 2)) if by_twos(steps) else ()
+
+
+def gather_far(own, near, steps):
+    if not near:
+        return ()
+    return (
+        across(jnp.concatenate([own[:2], near[0]], axis=0), 2),
+        across(jnp.concatenate([own[2:], near[1]], axis=0), 1),
+    )
+
+
+def placed(own, near, far, counts, targets, shapes):
     peers = lax.axis_size("seq")
     place = lax.axis_index("seq")
-    if len(steps) != 2 or any(len(bits) != 2 for bits in steps):
-        gathered = lax.all_gather(part, "seq", axis=0)
-        taken = [target for target in targets if target is None or target[1] is not None or
-                 shapes[target[0]][0] == 4]
-        sums = gathered_sums(gathered, counts[: len(taken)], taken, [
-            shape for shape in shapes if shape[0] != peers])
-        return sums if len(sums) == len(shapes) else [
-            *sums, gathered[:, sum(counts[:-1])].astype(F32)]
-    arrays = [part[None]] + [came[None] for came in terms_sent([part] * 4, steps[1])]
-    own = jnp.concatenate(arrays, axis=0)
-    arrays = [own] + terms_sent([own] * 4, steps[0])
+    if not near:
+        gathered = lax.all_gather(own, "seq", axis=0)
+        single = [target for target in targets if target is not None and target[1] is None]
+        if not single or shapes[single[0][0]][0] == 4:
+            return gathered_sums(gathered, counts, targets, shapes)
+        sums = gathered_sums(gathered, counts[:-1], targets[:-1], shapes[:-1])
+        return [*sums, gathered[:, sum(counts[:-1])].astype(F32)]
     mine = jnp.stack([place & 3, (place >> 2) & 3]).astype(jnp.int32)
-    return placed_sums(mine, arrays, counts, targets, shapes)
+    aways = [
+        [(0, 0), (0, 1), (0, 2), (0, 3)],
+        [(1, 0), (1, 1)],
+        [(2, 2), (2, 3)],
+        [(2, 0), (2, 1), (3, 0), (3, 1)],
+        [(1, 2), (1, 3), (3, 2), (3, 3)],
+    ]
+    return placed_sums(mine, [own, *near, *far], aways, counts, targets, shapes)
 
 
 def unit_back(moved_pairs, moved_values, short_parts, unit, inverse):
@@ -1153,25 +1182,15 @@
     long_att, long_w, long_s = long_forward(long_pack[0], long_pack[1], long_pack[2], long_line)
 
     long_att, short_proj = after(long_att, short_proj)
-    long_halves = jnp.split(long_att, 2, axis=1)
-    low_half = exchange(long_halves[0])
-    first_short = ITEMS
+    long_att = exchange(long_att)
     *forward, short_ffn = feed_forward(
-        first_short, tokens, short_proj, other_half(short_proj), gain_one, bias_one, inner_weight,
+        ITEMS, tokens, short_proj, other_half(short_proj), gain_one, bias_one, inner_weight,
         outer_weight,
     )
-    low_half, short_ffn, high_half = lax.optimization_barrier(
-        (low_half, short_ffn, long_halves[1])
-    )
-    high_half = exchange(high_half)
-    *backward, short_back, short_gain_two, short_bias_two = feed_back(
-        first_short, forward[0], short_ffn, other_half(short_ffn), gain_one, bias_one, gain_two,
-        bias_two, cotangent, forward[4], inner_weight, outer_weight,
-    )
-    high_half, short_back = after(high_half, short_back)
-    short_back_other = other_half(short_back)
-
-    mixed, long_proj = project_out_long(low_half, high_half, out_weight, mixed)
+    long_att, short_ffn = after(long_att, short_ffn)
+    short_ffn_other = other_half(short_ffn)
+
+    mixed, long_proj = project_out_long(long_att, out_weight, mixed)
     *forward, long_ffn = feed_forward(
         0, tokens, long_proj, other_half(long_proj), gain_one, bias_one, inner_weight,
         outer_weight, forward,
@@ -1179,17 +1198,24 @@
     norm_unit, norm_inverse, normed_low, act_low, act_slope = forward
     *backward, long_back, long_gain_two, long_bias_two = feed_back(
         0, norm_unit, long_ffn, other_half(long_ffn), gain_one, bias_one, gain_two, bias_two,
+        cotangent, act_slope, inner_weight, outer_weight,
+    )
+    grad_hidden, grad_proj_low, long_grad, long_gain_one, long_bias_one = project_back(
+        0, norm_unit, norm_inverse, backward[1], long_back, other_half(long_back), gain_one,
+        out_weight, heads_dev,
+    )
+    long_grad, backward, short_ffn, short_ffn_other = lax.optimization_barrier(
+        (long_grad, backward, short_ffn, short_ffn_other)
+    )
+    long_grad = exchange(long_grad)
+    *backward, short_back, short_gain_two, short_bias_two = feed_back(
+        ITEMS, norm_unit, short_ffn, short_ffn_other, gain_one, bias_one, gain_two, bias_two,
         cotangent, act_slope, inner_weight, outer_weight, backward,
     )
     output, grad_sum, grad_ffn_low, grad_pre_low = backward
-    long_back_other = other_half(long_back)
     grad_hidden, grad_proj_low, short_grad, short_gain_one, short_bias_one = project_back(
-        1, norm_unit, norm_inverse, grad_sum, short_back, short_back_other, gain_one, out_weight,
-        heads_dev,
-    )
-    grad_hidden, grad_proj_low, long_grad, long_gain_one, long_bias_one = project_back(
-        0, norm_unit, norm_inverse, grad_sum, long_back, long_back_other, gain_one, out_weight,
-        heads_dev, (grad_hidden, grad_proj_low),
+        1, norm_unit, norm_inverse, grad_sum, short_back, other_half(short_back), gain_one,
+        out_weight, heads_dev, (grad_hidden, grad_proj_low),
     )
     norm_lines = jnp.concatenate(
         [
@@ -1203,8 +1229,6 @@
 
     peers = lax.axis_size("seq")
     steps = bit_groups(peers)
-    long_grad, norm_lines = after(long_grad, norm_lines)
-    long_grad = exchange(long_grad)
     mine = (lax.axis_index("seq") & 3).astype(jnp.int32)[None]
     outer_counts, outer_terms_now = outer_terms(mine, act_low, grad_ffn_low, norm_lines)
     outer_terms_now, grad_pre_low = after(outer_terms_now, grad_pre_low)
@@ -1245,19 +1269,22 @@
     inner_terms_now, outer_part, long_back, short_grad = lax.optimization_barrier(
         (terms_for(inner_part, steps[1]), outer_part, long_back, short_grad)
     )
-    outer_sum, norm_sums = gathered_or_placed(
-        outer_part, steps, outer_counts, [(0, 0), (1, None)], [outer_weight.shape, (4, width)]
-    )
+    outer_own = gather_second(outer_part, steps)
     long_back = exchange(long_back)
     inner_came = terms_sent(inner_terms_now, steps[1])
+    outer_own, short_grad = after(outer_own, short_grad)
+    outer_near = gather_near(outer_own, steps)
     *short_parts, short_taps = short_backward(
         reach, ids_row, ids_col, short_pack, short_grad, short_w, short_s
     )
-    long_back, short_parts, short_taps = lax.optimization_barrier(
-        (long_back, short_parts, short_taps)
-    )
+    long_back, short_parts, short_taps, outer_own, outer_near = lax.optimization_barrier(
+        (long_back, short_parts, short_taps, outer_own, outer_near)
+    )
+    outer_far = gather_far(outer_own, outer_near, steps)
     grads_low = unit_back(long_back, long_dv, [short_parts], unit, inverse)
-    own, grads_low = after(inner_terms_now[0], grads_low)
+    own, grads_low, outer_far = lax.optimization_barrier(
+        (inner_terms_now[0], grads_low, outer_far)
+    )
     inner_part = terms_summed(own, inner_came)
     for bits in steps[2:]:
         terms = next_terms(inner_part, inner_counts, bits)
@@ -1269,14 +1296,13 @@
     kernel_part = short_taps[:, 0, taps] + jnp.where(owner[:, None], long_taps[:, taps], 0.0)
     taps_line = kernel_part.reshape(1, -1)
     taps_line = jnp.pad(taps_line, ((0, 15), (0, width - taps_line.shape[1]))).astype(BF16)
-    inner_sum, out_sum, tap_lines = gathered_or_placed(
-        jnp.concatenate([inner_part, taps_line], axis=0), steps, inner_counts + [16],
-        [(0, 0), (0, width), (1, 0), None, (2, None)],
-        [inner_weight.shape, out_weight.shape, (peers, width)],
-    )
-    kernel_sum = jnp.sum(tap_lines[:, : heads_dev * CONV_WIDTH], axis=0).reshape(
-        heads_dev, CONV_WIDTH
-    )
+    outer_sum, norm_sums = placed(
+        outer_own, outer_near, outer_far, outer_counts, [(0, 0), (1, None)],
+        [outer_weight.shape, (4, width)],
+    )
+    inner_own = gather_second(jnp.concatenate([inner_part, taps_line], axis=0), steps)
+    inner_near = gather_near(inner_own, steps)
+    inner_far = gather_far(inner_own, inner_near, steps)
 
     weight_part = contract(tokens, grads_low, 0, 1).astype(BF16)
     terms = terms_for(weight_part.reshape(1 << len(steps[0]), -1, 3 * head_cols), steps[0])
@@ -1293,6 +1319,14 @@
         weight_part = terms_gathered(weight_part, bits).reshape(-1, 3 * head_cols)
     weight_sum = weight_part.astype(F32)
     token_grad = grad_hidden + (token_own.astype(F32) + other_half(token_own).astype(F32))
+    inner_sum, out_sum, tap_lines = placed(
+        inner_own, inner_near, inner_far, inner_counts + [16],
+        [(0, 0), (0, width), (1, 0), None, (2, None)],
+        [inner_weight.shape, out_weight.shape, (peers, width)],
+    )
+    kernel_sum = jnp.sum(tap_lines[:, : heads_dev * CONV_WIDTH], axis=0).reshape(
+        heads_dev, CONV_WIDTH
+    )
     return (
         output,
         token_grad,

time: 532 us -> 514 us (0.966)
  starting transfers between devices: 126 us -> 107 us
  other arithmetic: 19.1 us -> 24.5 us
    ppermute x36 -> x30, starting transfers between devices: 73.1 us -> 49.7 us  [terms_sent(): lax.ppermute(term, 'seq', [(i, i ^ away << bits[0]) for i in range(peers)])]
    ppermute x0 -> x8, waiting for transfers between devices: none -> 12.8 us  [across(): return lax.ppermute(array, 'seq', [(i, i ^ mask) for i in range(peers)])]
    ppermute x0 -> x8, starting transfers between devices: none -> 12.7 us  [across(): return lax.ppermute(array, 'seq', [(i, i ^ mask) for i in range(peers)])]
    ppermute x36 -> x30, waiting for transfers between devices: 44.3 us -> 31.9 us  [terms_sent(): lax.ppermute(term, 'seq', [(i, i ^ away << bits[0]) for i in range(peers)])]
    all_to_all x6 -> x5, starting transfers between devices: 51.1 us -> 43.5 us  [exchange(): return lax.all_to_all(pieces, 'seq', 0, 0, axis_index_groups=groups)]
  transfers between devices with their start and end apart: 49 -> 50, of which waited for: 14 -> 18; matrix products, arithmetic and copies ran while one was open for 6% -> 7% of each run, Pallas kernels for 38% -> 36%
where the time goes in v1:
time: 514 us; the launch traced here: 505 us
  Pallas kernels  288 us (56%)
  starting transfers between devices  107 us (21%)
  waiting for transfers between devices  51.9 us (10%)
  other arithmetic  24.5 us (5%)
  local copies, waits for them, and re-layouts  22.9 us (4%)
  matrix products  9.29 us (2%)
    pallas_call x1, Pallas kernels, long_forward(): pl.pallas_call(body, grid=(blocks,), in_specs=[pl.BlockSpec((head_dim, PI...  71.3 us
    ppermute x30, starting transfers between devices, terms_sent(): lax.ppermute(term, 'seq', [(i, i ^ away << bits[0]) for i in range(peers)])  49.7 us
    all_to_all x5, starting transfers between devices, exchange(): return lax.all_to_all(pieces, 'seq', 0, 0, axis_index_groups=groups)  43.5 us
    pallas_call x1, Pallas kernels, long_back_pairs(): pl.pallas_call(body, grid=(blocks,), in_specs=[piece, whole, whole, piece...  32.2 us
    ppermute x30, waiting for transfers between devices, terms_sent(): lax.ppermute(term, 'seq', [(i, i ^ away << bits[0]) for i in range(peers)])  31.9 us
    pallas_call x1, Pallas kernels, short_forward(): pl.pallas_call(body, grid=(blocks,), in_specs=[pl.BlockSpec(memory_space=...  26.4 us
    pallas_call x1, Pallas kernels, short_backward(): pl.pallas_call(body, grid=(blocks,), in_specs=[pl.BlockSpec(memory_space=...  24.7 us
    pallas_call x2, Pallas kernels, feed_forward(): pl.pallas_call(body, grid=(count,), in_specs=[rows, own_rows, own_rows, l...  24 us
  transfers between devices with their start and end apart: 50, of which 18 were waited for; matrix products, arithmetic and copies ran while one was open for 7% of the time, Pallas kernels for 36%

profile of v1, /device:TPU:0, one launch (start us, length us, event | category | flops | bytes accessed | tf_op | source)
XLA Modules:
  0.0 504.9 jit_solution(16386853429142096638)
XLA Ops:
  0.6 9.9 %shard_map.237 = (bf16[16,192,256]{2,1,0:T(8,128)(2,1)}, bf16[3,6,64,1024]{3,2,1,0:T(8,128)(2,1)}, f32[2,6,64,1536]{3,2,1,0:T(8,128)}, f32[2,6,1,1536]{3,2,1,0:T(1,128)}) custom-call(bf16[1536,768]{1,0:T(8,128)(2,1)} %t_ref.5, bf16[768,384]{1,0:T(8,128)(2,1)} %wq_ref.1, bf16[768,384]{1,0:T(8,128)(2,1)} %wk_ref.1, bf16[768,384]{1,0:T(8,128)(2,1)} %wv_ref.1), custom_call_target="tpu_custom_call" | custom-call | flops 11500000256 | tf_op jit(solution)/shard_map/pallas_call | solution.py:473
  10.6 8.5 %all-to-all-start = ((bf16[16,192,256]{2,1,0:T(8,128)(2,1)}), bf16[16,192,256]{2,1,0:T(8,128)(2,1)S(1)}, u32[]{:S(2)}, u32[]{:S(2)}) async-start(bf16[16,192,256]{2,1,0:T(8,128)(2,1)} %get-tuple-element.163), calls=%async_computation | async-start | bytes 3145728 | tf_op jit(solution)/shard_map/all_to_all | solution.py:1144
  22.8 26.4 %shard_map.238 = (bf16[6,64,1024]{2,1,0:T(8,128)(2,1)}, bf16[4,6,1024,256]{3,2,1,0:T(8,128)(2,1)}, bf16[4,6,1024,256]{3,2,1,0:T(8,128)(2,1)}) custom-call(s32[2,4]{1,0:T(2,128)} %pad_add_fusion.reach_ref, s32[1,1024]{1,0:T(1,128)} %bitcast.132, s32[1088,1]{1,0:T(8,128)} %broadcast_in_dim.117.col_ref, ...), custom_call_target="tpu_custom_call" | custom-call | flops 32199999488 | tf_op jit(solution)/shard_map/pallas_call | solution.py:325
  49.2 3.3 shard_map.239
  55.9 71.3 %shard_map.240 = (bf16[16,64,256]{2,1,0:T(8,128)(2,1)}, bf16[16,4096,256]{2,1,0:T(8,128)(2,1)}, bf16[16,4096,256]{2,1,0:T(8,128)(2,1)}) custom-call(bf16[64,4096]{1,0:T(8,128)(2,1)} %bitcast.121, bf16[64,4096]{1,0:T(8,128)(2,1)} %bitcast.123, bf16[64,4096]{1,0:T(8,128)(2,1)} %bitcast.101, f32[1,640]{1,0:T(1,128)} %pad_dynamic-slice_fusion.line_ref), custom_call_target="tpu_custom_call" | custom-call | flops 80499998720 | tf_op jit(solution)/shard_map/pallas_call | solution.py:154
  128.5 16.9 %all-to-all-start.1 = ((bf16[16,64,256]{2,1,0:T(8,128)(2,1)}), bf16[16,64,256]{2,1,0:T(8,128)(2,1)S(1)}, u32[]{:S(2)}, u32[]{:S(2)}) async-start(bf16[16,64,256]{2,1,0:T(8,128)(2,1)} %get-tuple-element.170), calls=%async_computation.1 | async-start | bytes 1048576 | tf_op jit(solution)/shard_map/all_to_all | solution.py:1144
  145.4 14.6 %shard_map.241 = (f32[1536,768]{1,0:T(8,128)}, f32[1536,1]{1,0:T(8,128)}, bf16[1536,768]{1,0:T(8,128)(2,1)}, bf16[1536,1536]{1,0:T(8,128)(2,1)}, bf16[1536,1536]{1,0:T(8,128)(2,1)}, /*index=5*/bf16[1024,768]{1,0:T(8,128)(2,1)}) custom-call(bf16[1536,768]{1,0:T(8,128)(2,1)} %t_ref.5, bf16[1024,768]{1,0:T(8,128)(2,1)} %get-tuple-element.171.own_ref, ...), custom_call_target="tpu_custom_call" | custom-call | flops 13799999488 | tf_op jit(solution)/shard_map/pallas_call | solution.py:598
  161.6 3.0 shard_map.242
  164.6 2.5 collective-permute-done.1.other_ref
  168.0 9.4 %shard_map.243 = (f32[1536,768]{1,0:T(8,128)}, f32[1536,1]{1,0:T(8,128)}, bf16[1536,768]{1,0:T(8,128)(2,1)}, bf16[1536,1536]{1,0:T(8,128)(2,1)}, bf16[1536,1536]{1,0:T(8,128)(2,1)}, /*index=5*/bf16[512,768]{1,0:T(8,128)(2,1)}) custom-call(bf16[1536,768]{1,0:T(8,128)(2,1)} %t_ref.5, ...), custom_call_target="tpu_custom_call", output_to_operand_aliasing={{0}: (7, {}), {1}: (8, {}), {2}: (9, {}), {3}: (10, {}), {4... | custom-call | flops 6899999744 | tf_op jit(solution)/shard_map/pallas_call | solution.py:598
  180.8 8.7 %shard_map.244 = (bf16[1536,768]{1,0:T(8,128)(2,1)}, f32[1536,768]{1,0:T(8,128)}, bf16[1536,768]{1,0:T(8,128)(2,1)}, bf16[1536,1536]{1,0:T(8,128)(2,1)}, bf16[51...) custom-call(f32[1536,768]{1,0:T(8,128)} %get-tuple-element.181.unit_ref, ...), custom_call_target="tpu_custom_call" | custom-call | flops 6899999744 | tf_op jit(solution)/shard_map/pallas_call | solution.py:664
  189.8 2.4 collective-permute-done.3.other_ref
  193.0 5.2 %shard_map.245 = (f32[1536,768]{1,0:T(8,128)}, bf16[1536,768]{1,0:T(8,128)(2,1)}, bf16[16,64,256]{2,1,0:T(8,128)(2,1)}, f32[1,768]{1,0:T(1,128)}, f32[1,768]{1,0:T(1,128)}) custom-call(f32[1536,768]{1,0:T(8,128)} %get-tuple-element.181.unit_ref, f32[1536,1]{1,0:T(8,128)} %get-tuple-element.182.inv_ref, f32[1536,768]{1,0:T(8,128)} %get-tuple-element.195.sum_ref.rest_1_, ...), custom_call_target="tpu_custom_call" | custom-call | flops 4600000000 | tf_op jit(solution)/shard_map/pallas_call | solution.py:739
  198.2 13.3 %shard_map.246 = (bf16[1536,768]{1,0:T(8,128)(2,1)}, f32[1536,768]{1,0:T(8,128)}, bf16[1536,768]{1,0:T(8,128)(2,1)}, bf16[1536,1536]{1,0:T(8,128)(2,1)}, bf16[10...) custom-call(f32[1536,768]{1,0:T(8,128)} %get-tuple-element.181.unit_, ...), custom_call_target="tpu_custom_call", output_to_operand_aliasing={{0}: (11, {}), {1}: (12, {}), {2}: (13, {}), {3}: (14, {})} | custom-call | flops 13799999488 | tf_op jit(solution)/shard_map/pallas_call | solution.py:664
  211.7 6.4 %all-to-all-start.2 = ((bf16[16,64,256]{2,1,0:T(8,128)(2,1)}), bf16[16,64,256]{2,1,0:T(8,128)(2,1)S(1)}, u32[]{:S(2)}, u32[]{:S(2)}) async-start(bf16[16,64,256]{2,1,0:T(8,128)(2,1)} %get-tuple-element.231), calls=%async_computation.2 | async-start | bytes 1048576 | tf_op jit(solution)/shard_map/all_to_all | solution.py:1144
  220.7 6.9 %shard_map.247 = (f32[1536,768]{1,0:T(8,128)}, bf16[1536,768]{1,0:T(8,128)(2,1)}, bf16[6,64,1024]{2,1,0:T(8,128)(2,1)}, f32[1,768]{1,0:T(1,128)}, f32[1,768]{1,0:T(1,128)}) custom-call(f32[1536,768]{1,0:T(8,128)} %get-tuple-element.181.unit_ref, f32[1536,1]{1,0:T(8,128)} %get-tuple-element.182.inv_ref, ...), custom_call_target="tpu_custom_call", output_to_operand_aliasing={{0}: (7, {}), {1}: (8, {})} | custom-call | flops 9200000000 | tf_op jit(solution)/shard_map/pallas_call | solution.py:739
  229.6 8.2 %shard_map.248 = (bf16[4,112,768]{2,1,0:T(8,128)(2,1)}, bf16[4,112,768]{2,1,0:T(8,128)(2,1)}, bf16[4,112,768]{2,1,0:T(8,128)(2,1)}, bf16[4,112,768]{2,1,0:T(8,128)(2,1)}) custom-call(s32[1]{0:T(128)} %bitcast.8.mine_ref, bf16[1536,1536]{1,0:T(8,128)(2,1)} %get-tuple-element.204.act_ref, bf16[1536,768]{1,0:T(8,128)(2,1)} %get-tuple-element.205.ffn_ref, ...), custom_call_target="tpu_custom_call" | custom-call | flops 10350000128 | tf_op jit(solution)/shard_map/pallas_call | solution.py:773
  241.3 9.7 %shard_map.249 = (bf16[4,128,768]{2,1,0:T(8,128)(2,1)}, bf16[4,128,768]{2,1,0:T(8,128)(2,1)}, bf16[4,128,768]{2,1,0:T(8,128)(2,1)}, bf16[4,128,768]{2,1,0:T(8,128)(2,1)}) custom-call(s32[1]{0:T(128)} %bitcast.8.mine_ref, bf16[1536,768]{1,0:T(8,128)(2,1)} %get-tuple-element.223.low_ref, bf16[1536,1536]{1,0:T(8,128)(2,1)} %get-tuple-element.224.pre_ref, ...), custom_call_target="tpu_custom_call" | custom-call | flops 10350000128 | tf_op jit(solution)/shard_map/pallas_call | solution.py:773
  251.9 23.0 %shard_map.250 = (bf16[16,64,256]{2,1,0:T(8,128)(2,1)}, f32[1,640]{1,0:T(1,128)}) custom-call(bf16[64,4096]{1,0:T(8,128)(2,1)} %bitcast.102, bf16[64,4096]{1,0:T(8,128)(2,1)} %bitcast.104, bf16[16,4096,256]{2,1,0:T(8,128)(2,1)} %get-tuple-element.237.w_ref), custom_call_target="tpu_custom_call" | custom-call | flops 1150000000 | tf_op jit(solution)/shard_map/pallas_call | solution.py:200
  276.0 2.9 collective-permute-start.10
  281.9 6.1 %all-to-all-start.3 = ((bf16[16,64,256]{2,1,0:T(8,128)(2,1)}), bf16[16,64,256]{2,1,0:T(8,128)(2,1)}, u32[]{:S(2)}, u32[]{:S(2)}) async-start(bf16[16,64,256]{2,1,0:T(8,128)(2,1)} %get-tuple-element.253), calls=%async_computation.3 | async-start | bytes 1048576 | tf_op jit(solution)/shard_map/all_to_all | solution.py:1144
  292.0 2.4 collective-permute-start.14
  294.4 32.2 %shard_map.251 = (bf16[16,64,256]{2,1,0:T(8,128)(2,1)}, bf16[16,64,256]{2,1,0:T(8,128)(2,1)}) custom-call(bf16[64,4096]{1,0:T(8,128)(2,1)} %bitcast.122, bf16[64,4096]{1,0:T(8,128)(2,1)} %bitcast.124, bf16[64,4096]{1,0:T(8,128)(2,1)} %bitcast.103, bf16[64,4096]{1,0:T(8,128)(2,1)} %bitcast.105, bf16[16,4096,256]{2,1,0:T(8,128)(2,1)} %get-tuple-element.255.s_ref), custom_call_target="tpu_custom_call" | custom-call | flops 46000001024 | tf_op jit(solution)/shard_map/pallas_call | solution.py:258
  333.7 2.4 collective-permute-start.16
  336.8 5.6 %all-to-all-start.4 = ((bf16[16,128,256]{2,1,0:T(8,128)(2,1)}), bf16[16,128,256]{2,1,0:T(8,128)(2,1)S(1)}, u32[]{:S(2)}, u32[]{:S(2)}) async-start(bf16[16,128,256]{2,1,0:T(8,128)(2,1)} %pad_maximum_fusion.2), calls=%async_computation.4 | async-start | bytes 2097152 | tf_op jit(solution)/shard_map/all_to_all | solution.py:1144
  342.4 2.1 collective-permute-start.35
  344.5 2.4 collective-permute-start.36
  347.0 8.2 %collective-permute-done.16 = bf16[112,768]{1,0:T(8,128)(2,1)S(1)} collective-permute-done((bf16[112,768]{1,0:T(8,128)(2,1)S(1)}, bf16[112,768]{1,0:T(8,128)(2,1)S(1)}, u32[]{:S(2)}, u32[]{:S(2)}) %collective-permute-start.16) | collective-permute-done | bytes 172064 | tf_op jit(solution)/shard_map/ppermute | solution.py:1088
  356.8 24.7 %shard_map.252 = (f32[6,64,1024]{2,1,0:T(8,128)}, f32[6,64,1024]{2,1,0:T(8,128)}, f32[6,64,1024]{2,1,0:T(8,128)}, f32[6,1,640]{2,1,0:T(1,128)}) custom-call(s32[2,4]{1,0:T(2,128)} %pad_add_fusion.reach_ref, s32[1,1024]{1,0:T(1,128)} %bitcast.133, s32[1088,1]{1,0:T(8,128)} %broadcast_in_dim.117.col_ref, ...), custom_call_target="tpu_custom_call" | custom-call | flops 32199999488 | tf_op jit(solution)/shard_map/pallas_call | solution.py:400
  384.3 8.2 %collective-permute-start.20 = (bf16[4,112,768]{2,1,0:T(8,128)(2,1)}, bf16[4,112,768]{2,1,0:T(8,128)(2,1)}, u32[]{:S(2)}, u32[]{:S(2)}) collective-permute-start(bf16[4,112,768]{2,1,0:T(8,128)(2,1)} %pad_maximum_fusion.8), channel_id=1, source_target_pairs={{0,4},{2,6},{4,0},{6,2},{8,12},{10,14},{12,8},{14,10},{16,20},{18,... | collective-permute-start | bytes 2064392 | tf_op jit(solution)/shard_map/ppermute | solution.py:946
  393.5 8.4 %shard_map.253 = bf16[1152,1536]{1,0:T(8,128)(2,1)} custom-call(bf16[16,128,256]{2,1,0:T(8,128)(2,1)} %copy-done.2, bf16[16,64,256]{2,1,0:T(8,128)(2,1)} %all-to-all-done.3.refs_1_, f32[6,64,1024]{2,1,0:T(8,128)} %get-tuple-element.284.refs_2_, f32[6,64,1024]{2,1,0:T(8,128)} %get-tuple-element.285.refs_3_, f32[6,64,1024]{2,1,0:T(8,128)} %get-tuple-element.286.refs_4_, ...), custom_call_target="tpu_custom_call" | custom-call | flops 9200000000 | tf_op jit(solution)/shard_map/pallas_call | solution.py:1040
  403.1 6.8 %collective-permute-start.38 = (bf16[144,768]{1,0:T(8,128)(2,1)S(1)}, bf16[144,768]{1,0:T(8,128)(2,1)S(1)}, u32[]{:S(2)}, u32[]{:S(2)}) collective-permute-start(bf16[144,768]{1,0:T(8,128)(2,1)S(1)} %get-tuple-element.356), channel_id=1, source_target_pairs={{0,8},{2,10},{4,12},{6,14},{8,0},{10,2},{12,4},{14,6},{16,24},{18,... | collective-permute-start | bytes 663560 | tf_op jit(solution)/shard_map/ppermute | solution.py:1088
  409.9 5.5 %convolution_convert_fusion.1 = bf16[1152,768]{0,1:T(8,128)(2,1)S(1)} fusion(bf16[1152,1536]{1,0:T(8,128)(2,1)} %shard_map.253, bf16[1536,768]{1,0:T(8,128)(2,1)S(1)} %copy-done.1), kind=kOutput, calls=%fused_computation.2 | convolution fusion | flops 2718793728 | bytes 7667712 | tf_op jit(solution)/shard_map/dot_general | solution.py:68
  416.0 3.2 collective-permute-start.25
  419.2 3.8 convolution_convert_fusion
  424.0 2.4 collective-permute-start.40
  431.0 3.0 collective-permute-start.27
  436.1 2.0 collective-permute-done.26
  438.2 5.4 %collective-permute-done.28 = bf16[48,1152]{1,0:T(8,128)(2,1)S(1)} collective-permute-done((bf16[48,1152]{1,0:T(8,128)(2,1)S(1)}, bf16[48,1152]{1,0:T(8,128)(2,1)S(1)}, u32[]{:S(2)}, u32[]{:S(2)}) %collective-permute-start.28) | collective-permute-done | bytes 110624 | tf_op jit(solution)/shard_map/ppermute | solution.py:1088
  443.6 2.2 collective-permute-start.29
  451.4 3.0 collective-permute-done.31
  455.9 2.2 collective-permute-start.34
  458.1 4.4 shard_map.255
  464.0 2.3 pad_maximum_fusion.6
  467.6 5.8 %collective-permute-done.33 = bf16[192,1152]{1,0:T(8,128)(2,1)} collective-permute-done((bf16[192,1152]{1,0:T(8,128)(2,1)S(1)}, bf16[192,1152]{1,0:T(8,128)(2,1)}, u32[]{:S(2)}, u32[]{:S(2)}) %collective-permute-start.33) | collective-permute-done | bytes 442400 | tf_op jit(solution)/shard_map/ppermute | solution.py:1088
  477.6 12.7 %collective-permute-done.43.refs_3_ = bf16[4,144,768]{2,1,0:T(8,128)(2,1)S(1)} collective-permute-done((bf16[4,144,768]{2,1,0:T(8,128)(2,1)S(1)}, bf16[4,144,768]{2,1,0:T(8,128)(2,1)S(1)}, u32[]{:S(2)}, u32[]{:S(2)}) %collective-permute-start.43) | collective-permute-done | bytes 884768 | tf_op jit(solution)/shard_map/ppermute | solution.py:946
  492.2 4.9 shard_map.254
  498.6 5.9 %add_add_fusion = f32[1536,768]{1,0:T(8,128)} fusion(f32[1536,768]{1,0:T(8,128)} %get-tuple-element.203, bf16[1536,768]{1,0:T(8,128)(2,1)} %collective-permute-done.22, bf16[1536,768]{1,0:T(8,128)(2,1)S(1)} %convolution_convert_fusion), kind=kLoop, calls=%fused_computation | loop fusion | flops 4718592 | bytes 14155776 | tf_op jit(solution)/shard_map/add | solution.py:1321
  (215 shorter events, 72.5 us)
Async XLA Ops:
  10.6 42.6 %all-to-all-start = ((bf16[16,192,256]{2,1,0:T(8,128)(2,1)}), bf16[16,192,256]{2,1,0:T(8,128)(2,1)S(1)}, u32[]{:S(2)}, u32[]{:S(2)}) async-start(bf16[16,192,256]{2,1,0:T(8,128)(2,1)} %get-tuple-element.163), calls=%async_computation | async-start | bytes 3145728 | tf_op jit(solution)/shard_map/all_to_all | solution.py:1144
  127.2 18.1 %collective-permute-start = (bf16[1024,768]{1,0:T(8,128)(2,1)S(1)}, bf16[1024,768]{1,0:T(8,128)(2,1)}, u32[]{:S(2)}, u32[]{:S(2)}) collective-permute-start(bf16[1024,768]{1,0:T(8,128)(2,1)S(1)} %copy-done.25), channel_id=1, source_target_pairs={{0,1},{1,0},{2,3},{3,2},{4,5},{5,4},{6,7},{7,6},{8,9},{9,8},{10,11... | collective-permute-start | bytes 4718600 | tf_op jit(solution)/shard_map/ppermute | solution.py:1061
  128.5 32.3 %all-to-all-start.1 = ((bf16[16,64,256]{2,1,0:T(8,128)(2,1)}), bf16[16,64,256]{2,1,0:T(8,128)(2,1)S(1)}, u32[]{:S(2)}, u32[]{:S(2)}) async-start(bf16[16,64,256]{2,1,0:T(8,128)(2,1)} %get-tuple-element.170), calls=%async_computation.1 | async-start | bytes 1048576 | tf_op jit(solution)/shard_map/all_to_all | solution.py:1144
  178.8 19.4 %collective-permute-start.4 = (bf16[1024,768]{1,0:T(8,128)(2,1)S(1)}, bf16[1024,768]{1,0:T(8,128)(2,1)}, u32[]{:S(2)}, u32[]{:S(2)}) collective-permute-start(bf16[1024,768]{1,0:T(8,128)(2,1)S(1)} %copy-done.24), channel_id=1, source_target_pairs={{0,1},{1,0},{2,3},{3,2},{4,5},{5,4},{6,7},{7,6},{8,9},{9,8},{10,11... | collective-permute-start | bytes 4718600 | tf_op jit(solution)/shard_map/ppermute | solution.py:1061
  189.6 2.6 collective-permute-start.3
  211.5 8.0 %collective-permute-start.5 = (bf16[1024,768]{1,0:T(8,128)(2,1)}, bf16[1024,768]{1,0:T(8,128)(2,1)S(1)}, u32[]{:S(2)}, u32[]{:S(2)}) collective-permute-start(bf16[1024,768]{1,0:T(8,128)(2,1)} %get-tuple-element.200.own_ref), channel_id=1, source_target_pairs={{0,1},{1,0},{2,3},{3,2},{4,5},{5,4},{6,7},{7,6},{8,9},{9,8},{10,11... | collective-permute-start | bytes 4718600 | tf_op jit(solution)/shard_map/ppermute | solution.py:1061
  211.7 39.3 %all-to-all-start.2 = ((bf16[16,64,256]{2,1,0:T(8,128)(2,1)}), bf16[16,64,256]{2,1,0:T(8,128)(2,1)S(1)}, u32[]{:S(2)}, u32[]{:S(2)}) async-start(bf16[16,64,256]{2,1,0:T(8,128)(2,1)} %get-tuple-element.231), calls=%async_computation.2 | async-start | bytes 1048576 | tf_op jit(solution)/shard_map/all_to_all | solution.py:1144
  237.8 37.0 %collective-permute-start.6 = (bf16[4,112,768]{2,1,0:T(8,128)(2,1)}, bf16[4,112,768]{2,1,0:T(8,128)(2,1)S(1)}, u32[]{:S(2)}, u32[]{:S(2)}) collective-permute-start(bf16[4,112,768]{2,1,0:T(8,128)(2,1)} %get-tuple-element.219), channel_id=1, source_target_pairs={{0,2},{2,0},{4,6},{6,4},{8,10},{10,8},{12,14},{14,12},{16,18},{18,... | collective-permute-start | bytes 2064392 | tf_op jit(solution)/shard_map/ppermute | solution.py:1088
  239.9 35.0 %collective-permute-start.7 = (bf16[4,112,768]{2,1,0:T(8,128)(2,1)}, bf16[4,112,768]{2,1,0:T(8,128)(2,1)S(1)}, u32[]{:S(2)}, u32[]{:S(2)}) collective-permute-start(bf16[4,112,768]{2,1,0:T(8,128)(2,1)} %get-tuple-element.220), channel_id=1, source_target_pairs={{0,4},{2,6},{4,0},{6,2},{8,12},{10,14},{12,8},{14,10},{16,20},{18,... | collective-permute-start | bytes 2064392 | tf_op jit(solution)/shard_map/ppermute | solution.py:1088
  241.3 33.6 %collective-permute-start.8 = (bf16[4,112,768]{2,1,0:T(8,128)(2,1)}, bf16[4,112,768]{2,1,0:T(8,128)(2,1)S(1)}, u32[]{:S(2)}, u32[]{:S(2)}) collective-permute-start(bf16[4,112,768]{2,1,0:T(8,128)(2,1)} %get-tuple-element.221), channel_id=1, source_target_pairs={{0,6},{2,4},{4,2},{6,0},{8,14},{10,12},{12,10},{14,8},{16,22},{18,... | collective-permute-start | bytes 2064392 | tf_op jit(solution)/shard_map/ppermute | solution.py:1088
  276.0 16.0 %collective-permute-start.10 = (bf16[112,768]{1,0:T(8,128)(2,1)S(1)}, bf16[112,768]{1,0:T(8,128)(2,1)S(1)}, u32[]{:S(2)}, u32[]{:S(2)}) collective-permute-start(bf16[112,768]{1,0:T(8,128)(2,1)S(1)} %get-tuple-element.246), channel_id=1, source_target_pairs={{0,16},{2,18},{4,20},{6,22},{8,24},{10,26},{12,28},{14,30},{16,0},... | collective-permute-start | bytes 516104 | tf_op jit(solution)/shard_map/ppermute | solution.py:1088
  280.4 46.2 %collective-permute-start.11 = (bf16[112,768]{1,0:T(8,128)(2,1)}, bf16[112,768]{1,0:T(8,128)(2,1)}, u32[]{:S(2)}, u32[]{:S(2)}) collective-permute-start(bf16[112,768]{1,0:T(8,128)(2,1)} %get-tuple-element.247), channel_id=1, source_target_pairs={{0,24},{2,26},{4,28},{6,30},{8,16},{10,18},{12,20},{14,22},{16,8},... | collective-permute-start | bytes 516104 | tf_op jit(solution)/shard_map/ppermute | solution.py:1088
  281.9 44.7 %collective-permute-start.9 = (bf16[112,768]{1,0:T(8,128)(2,1)}, bf16[112,768]{1,0:T(8,128)(2,1)}, u32[]{:S(2)}, u32[]{:S(2)}) collective-permute-start(bf16[112,768]{1,0:T(8,128)(2,1)} %get-tuple-element.245), channel_id=1, source_target_pairs={{0,8},{2,10},{4,12},{6,14},{8,0},{10,2},{12,4},{14,6},{16,24},{18,... | collective-permute-start | bytes 516104 | tf_op jit(solution)/shard_map/ppermute | solution.py:1088
  281.9 46.8 %all-to-all-start.3 = ((bf16[16,64,256]{2,1,0:T(8,128)(2,1)}), bf16[16,64,256]{2,1,0:T(8,128)(2,1)}, u32[]{:S(2)}, u32[]{:S(2)}) async-start(bf16[16,64,256]{2,1,0:T(8,128)(2,1)} %get-tuple-element.253), calls=%async_computation.3 | async-start | bytes 1048576 | tf_op jit(solution)/shard_map/all_to_all | solution.py:1144
  288.0 38.6 %collective-permute-start.12 = (bf16[4,128,768]{2,1,0:T(8,128)(2,1)}, bf16[4,128,768]{2,1,0:T(8,128)(2,1)S(1)}, u32[]{:S(2)}, u32[]{:S(2)}) collective-permute-start(bf16[4,128,768]{2,1,0:T(8,128)(2,1)} %get-tuple-element.249), channel_id=1, source_target_pairs={{0,2},{2,0},{4,6},{6,4},{8,10},{10,8},{12,14},{14,12},{16,18},{18,... | collective-permute-start | bytes 2359304 | tf_op jit(solution)/shard_map/ppermute | solution.py:1088
  289.9 37.8 %collective-permute-start.13 = (bf16[4,128,768]{2,1,0:T(8,128)(2,1)}, bf16[4,128,768]{2,1,0:T(8,128)(2,1)S(1)}, u32[]{:S(2)}, u32[]{:S(2)}) collective-permute-start(bf16[4,128,768]{2,1,0:T(8,128)(2,1)} %get-tuple-element.250), channel_id=1, source_target_pairs={{0,4},{2,6},{4,0},{6,2},{8,12},{10,14},{12,8},{14,10},{16,20},{18,... | collective-permute-start | bytes 2359304 | tf_op jit(solution)/shard_map/ppermute | solution.py:1088
  292.0 36.7 %collective-permute-start.14 = (bf16[4,128,768]{2,1,0:T(8,128)(2,1)}, bf16[4,128,768]{2,1,0:T(8,128)(2,1)S(1)}, u32[]{:S(2)}, u32[]{:S(2)}) collective-permute-start(bf16[4,128,768]{2,1,0:T(8,128)(2,1)} %get-tuple-element.251), channel_id=1, source_target_pairs={{0,6},{2,4},{4,2},{6,0},{8,14},{10,12},{12,10},{14,8},{16,22},{18,... | collective-permute-start | bytes 2359304 | tf_op jit(solution)/shard_map/ppermute | solution.py:1088
  332.2 14.7 %collective-permute-start.15 = (bf16[112,768]{1,0:T(8,128)(2,1)S(1)}, bf16[112,768]{1,0:T(8,128)(2,1)S(1)}, u32[]{:S(2)}, u32[]{:S(2)}) collective-permute-start(bf16[112,768]{1,0:T(8,128)(2,1)S(1)} %add_convert_fusion.4), channel_id=1, source_target_pairs={{0,8},{2,10},{4,12},{6,14},{8,0},{10,2},{12,4},{14,6},{16,24},{18,... | collective-permute-start | bytes 516104 | tf_op jit(solution)/shard_map/ppermute | solution.py:1088
  333.7 21.4 %collective-permute-start.16 = (bf16[112,768]{1,0:T(8,128)(2,1)S(1)}, bf16[112,768]{1,0:T(8,128)(2,1)S(1)}, u32[]{:S(2)}, u32[]{:S(2)}) collective-permute-start(bf16[112,768]{1,0:T(8,128)(2,1)S(1)} %add_convert_fusion.4), channel_id=1, source_target_pairs={{0,16},{2,18},{4,20},{6,22},{8,24},{10,26},{12,28},{14,30},{16,0},... | collective-permute-start | bytes 516104 | tf_op jit(solution)/shard_map/ppermute | solution.py:1088
  336.1 19.1 %collective-permute-start.17 = (bf16[112,768]{1,0:T(8,128)(2,1)S(1)}, bf16[112,768]{1,0:T(8,128)(2,1)S(1)}, u32[]{:S(2)}, u32[]{:S(2)}) collective-permute-start(bf16[112,768]{1,0:T(8,128)(2,1)S(1)} %add_convert_fusion.4), channel_id=1, source_target_pairs={{0,24},{2,26},{4,28},{6,30},{8,16},{10,18},{12,20},{14,22},{16,8},... | collective-permute-start | bytes 516104 | tf_op jit(solution)/shard_map/ppermute | solution.py:1088
  336.8 44.8 %all-to-all-start.4 = ((bf16[16,128,256]{2,1,0:T(8,128)(2,1)}), bf16[16,128,256]{2,1,0:T(8,128)(2,1)S(1)}, u32[]{:S(2)}, u32[]{:S(2)}) async-start(bf16[16,128,256]{2,1,0:T(8,128)(2,1)} %pad_maximum_fusion.2), calls=%async_computation.4 | async-start | bytes 2097152 | tf_op jit(solution)/shard_map/all_to_all | solution.py:1144
  342.4 59.5 %collective-permute-start.35 = (bf16[128,768]{1,0:T(8,128)(2,1)}, bf16[128,768]{1,0:T(8,128)(2,1)S(1)}, u32[]{:S(2)}, u32[]{:S(2)}) collective-permute-start(bf16[128,768]{1,0:T(8,128)(2,1)} %get-tuple-element.301), channel_id=1, source_target_pairs={{0,8},{2,10},{4,12},{6,14},{8,0},{10,2},{12,4},{14,6},{16,24},{18,... | collective-permute-start | bytes 589832 | tf_op jit(solution)/shard_map/ppermute | solution.py:1088
  344.5 57.4 %collective-permute-start.36 = (bf16[128,768]{1,0:T(8,128)(2,1)}, bf16[128,768]{1,0:T(8,128)(2,1)}, u32[]{:S(2)}, u32[]{:S(2)}) collective-permute-start(bf16[128,768]{1,0:T(8,128)(2,1)} %get-tuple-element.302), channel_id=1, source_target_pairs={{0,16},{2,18},{4,20},{6,22},{8,24},{10,26},{12,28},{14,30},{16,0},... | collective-permute-start | bytes 589832 | tf_op jit(solution)/shard_map/ppermute | solution.py:1088
  346.9 55.0 %collective-permute-start.37 = (bf16[128,768]{1,0:T(8,128)(2,1)}, bf16[128,768]{1,0:T(8,128)(2,1)}, u32[]{:S(2)}, u32[]{:S(2)}) collective-permute-start(bf16[128,768]{1,0:T(8,128)(2,1)} %get-tuple-element.303), channel_id=1, source_target_pairs={{0,24},{2,26},{4,28},{6,30},{8,16},{10,18},{12,20},{14,22},{16,8},... | collective-permute-start | bytes 589832 | tf_op jit(solution)/shard_map/ppermute | solution.py:1088
  355.3 26.3 %collective-permute-start.18 = (bf16[2,112,768]{2,1,0:T(8,128)(2,1)S(1)}, bf16[2,112,768]{2,1,0:T(8,128)(2,1)S(1)}, u32[]{:S(2)}, u32[]{:S(2)}) collective-permute-start(bf16[2,112,768]{2,1,0:T(8,128)(2,1)S(1)} %get-tuple-element.340), channel_id=1, source_target_pairs={{0,2},{2,0},{4,6},{6,4},{8,10},{10,8},{12,14},{14,12},{16,18},{18,... | collective-permute-start | bytes 1032200 | tf_op jit(solution)/shard_map/ppermute | solution.py:946
  356.8 24.8 %collective-permute-start.19 = (bf16[2,112,768]{2,1,0:T(8,128)(2,1)S(1)}, bf16[2,112,768]{2,1,0:T(8,128)(2,1)S(1)}, u32[]{:S(2)}, u32[]{:S(2)}) collective-permute-start(bf16[2,112,768]{2,1,0:T(8,128)(2,1)S(1)} %get-tuple-element.339), channel_id=1, source_target_pairs={{0,4},{2,6},{4,0},{6,2},{8,12},{10,14},{12,8},{14,10},{16,20},{18,... | collective-permute-start | bytes 1032200 | tf_op jit(solution)/shard_map/ppermute | solution.py:946
  382.8 19.1 %collective-permute-start.21 = (bf16[4,112,768]{2,1,0:T(8,128)(2,1)}, bf16[4,112,768]{2,1,0:T(8,128)(2,1)}, u32[]{:S(2)}, u32[]{:S(2)}) collective-permute-start(bf16[4,112,768]{2,1,0:T(8,128)(2,1)} %pad_maximum_fusion.9), channel_id=1, source_target_pairs={{0,2},{2,0},{4,6},{6,4},{8,10},{10,8},{12,14},{14,12},{16,18},{18,... | collective-permute-start | bytes 2064392 | tf_op jit(solution)/shard_map/ppermute | solution.py:946
  384.3 17.6 %collective-permute-start.20 = (bf16[4,112,768]{2,1,0:T(8,128)(2,1)}, bf16[4,112,768]{2,1,0:T(8,128)(2,1)}, u32[]{:S(2)}, u32[]{:S(2)}) collective-permute-start(bf16[4,112,768]{2,1,0:T(8,128)(2,1)} %pad_maximum_fusion.8), channel_id=1, source_target_pairs={{0,4},{2,6},{4,0},{6,2},{8,12},{10,14},{12,8},{14,10},{16,20},{18,... | collective-permute-start | bytes 2064392 | tf_op jit(solution)/shard_map/ppermute | solution.py:946
  403.1 30.8 %collective-permute-start.38 = (bf16[144,768]{1,0:T(8,128)(2,1)S(1)}, bf16[144,768]{1,0:T(8,128)(2,1)S(1)}, u32[]{:S(2)}, u32[]{:S(2)}) collective-permute-start(bf16[144,768]{1,0:T(8,128)(2,1)S(1)} %get-tuple-element.356), channel_id=1, source_target_pairs={{0,8},{2,10},{4,12},{6,14},{8,0},{10,2},{12,4},{14,6},{16,24},{18,... | collective-permute-start | bytes 663560 | tf_op jit(solution)/shard_map/ppermute | solution.py:1088
  409.9 37.8 %collective-permute-start.39 = (bf16[144,768]{1,0:T(8,128)(2,1)S(1)}, bf16[144,768]{1,0:T(8,128)(2,1)S(1)}, u32[]{:S(2)}, u32[]{:S(2)}) collective-permute-start(bf16[144,768]{1,0:T(8,128)(2,1)S(1)} %get-tuple-element.356), channel_id=1, source_target_pairs={{0,16},{2,18},{4,20},{6,22},{8,24},{10,26},{12,28},{14,30},{16,0},... | collective-permute-start | bytes 663560 | tf_op jit(solution)/shard_map/ppermute | solution.py:1088
  415.6 8.4 %collective-permute-start.23 = (bf16[192,1152]{1,0:T(8,128)(2,1)S(1)}, bf16[192,1152]{1,0:T(8,128)(2,1)S(1)}, u32[]{:S(2)}, u32[]{:S(2)}) collective-permute-start(bf16[192,1152]{1,0:T(8,128)(2,1)S(1)} %get-tuple-element.297), channel_id=1, source_target_pairs={{0,2},{2,0},{4,6},{6,4},{8,10},{10,8},{12,14},{14,12},{16,18},{18,... | collective-permute-start | bytes 1327112 | tf_op jit(solution)/shard_map/ppermute | solution.py:1088
  415.7 12.7 %collective-permute-start.24 = (bf16[192,1152]{1,0:T(8,128)(2,1)S(1)}, bf16[192,1152]{1,0:T(8,128)(2,1)S(1)}, u32[]{:S(2)}, u32[]{:S(2)}) collective-permute-start(bf16[192,1152]{1,0:T(8,128)(2,1)S(1)} %get-tuple-element.298), channel_id=1, source_target_pairs={{0,4},{2,6},{4,0},{6,2},{8,12},{10,14},{12,8},{14,10},{16,20},{18,... | collective-permute-start | bytes 1327112 | tf_op jit(solution)/shard_map/ppermute | solution.py:1088
  416.0 13.9 %collective-permute-start.25 = (bf16[192,1152]{1,0:T(8,128)(2,1)S(1)}, bf16[192,1152]{1,0:T(8,128)(2,1)S(1)}, u32[]{:S(2)}, u32[]{:S(2)}) collective-permute-start(bf16[192,1152]{1,0:T(8,128)(2,1)S(1)} %get-tuple-element.299), channel_id=1, source_target_pairs={{0,6},{2,4},{4,2},{6,0},{8,14},{10,12},{12,10},{14,8},{16,22},{18,... | collective-permute-start | bytes 1327112 | tf_op jit(solution)/shard_map/ppermute | solution.py:1088
  424.0 25.1 %collective-permute-start.40 = (bf16[144,768]{1,0:T(8,128)(2,1)S(1)}, bf16[144,768]{1,0:T(8,128)(2,1)S(1)}, u32[]{:S(2)}, u32[]{:S(2)}) collective-permute-start(bf16[144,768]{1,0:T(8,128)(2,1)S(1)} %get-tuple-element.356), channel_id=1, source_target_pairs={{0,24},{2,26},{4,28},{6,30},{8,16},{10,18},{12,20},{14,22},{16,8},... | collective-permute-start | bytes 663560 | tf_op jit(solution)/shard_map/ppermute | solution.py:1088
  430.2 8.0 %collective-permute-start.26 = (bf16[48,1152]{1,0:T(8,128)(2,1)S(1)}, bf16[48,1152]{1,0:T(8,128)(2,1)S(1)}, u32[]{:S(2)}, u32[]{:S(2)}) collective-permute-start(bf16[48,1152]{1,0:T(8,128)(2,1)S(1)} %get-tuple-element.352), channel_id=1, source_target_pairs={{0,8},{2,10},{4,12},{6,14},{8,0},{10,2},{12,4},{14,6},{16,24},{18,... | collective-permute-start | bytes 331784 | tf_op jit(solution)/shard_map/ppermute | solution.py:1088
  431.0 7.2 %collective-permute-start.27 = (bf16[48,1152]{1,0:T(8,128)(2,1)S(1)}, bf16[48,1152]{1,0:T(8,128)(2,1)S(1)}, u32[]{:S(2)}, u32[]{:S(2)}) collective-permute-start(bf16[48,1152]{1,0:T(8,128)(2,1)S(1)} %get-tuple-element.354), channel_id=1, source_target_pairs={{0,16},{2,18},{4,20},{6,22},{8,24},{10,26},{12,28},{14,30},{16,0},... | collective-permute-start | bytes 331784 | tf_op jit(solution)/shard_map/ppermute | solution.py:1088
  434.0 9.6 %collective-permute-start.28 = (bf16[48,1152]{1,0:T(8,128)(2,1)S(1)}, bf16[48,1152]{1,0:T(8,128)(2,1)S(1)}, u32[]{:S(2)}, u32[]{:S(2)}) collective-permute-start(bf16[48,1152]{1,0:T(8,128)(2,1)S(1)} %get-tuple-element.353), channel_id=1, source_target_pairs={{0,24},{2,26},{4,28},{6,30},{8,16},{10,18},{12,20},{14,22},{16,8},... | collective-permute-start | bytes 331784 | tf_op jit(solution)/shard_map/ppermute | solution.py:1088
  438.2 25.8 %collective-permute-start.41 = (bf16[2,144,768]{2,1,0:T(8,128)(2,1)}, bf16[2,144,768]{2,1,0:T(8,128)(2,1)}, u32[]{:S(2)}, u32[]{:S(2)}) collective-permute-start(bf16[2,144,768]{2,1,0:T(8,128)(2,1)} %pad_maximum_fusion.12), channel_id=1, source_target_pairs={{0,2},{2,0},{4,6},{6,4},{8,10},{10,8},{12,14},{14,12},{16,18},{18,... | collective-permute-start | bytes 1327112 | tf_op jit(solution)/shard_map/ppermute | solution.py:946
  443.6 7.5 %collective-permute-start.29 = (bf16[48,1152]{1,0:T(8,128)(2,1)S(1)}, bf16[48,1152]{1,0:T(8,128)(2,1)S(1)}, u32[]{:S(2)}, u32[]{:S(2)}) collective-permute-start(bf16[48,1152]{1,0:T(8,128)(2,1)S(1)} %fusion.9), channel_id=1, source_target_pairs={{0,8},{2,10},{4,12},{6,14},{8,0},{10,2},{12,4},{14,6},{16,24},{18,... | collective-permute-start | bytes 331784 | tf_op jit(solution)/shard_map/ppermute | solution.py:1088
  445.8 5.6 %collective-permute-start.30 = (bf16[48,1152]{1,0:T(8,128)(2,1)S(1)}, bf16[48,1152]{1,0:T(8,128)(2,1)S(1)}, u32[]{:S(2)}, u32[]{:S(2)}) collective-permute-start(bf16[48,1152]{1,0:T(8,128)(2,1)S(1)} %fusion.9), channel_id=1, source_target_pairs={{0,16},{2,18},{4,20},{6,22},{8,24},{10,26},{12,28},{14,30},{16,0},... | collective-permute-start | bytes 331784 | tf_op jit(solution)/shard_map/ppermute | solution.py:1088
  447.8 6.6 %collective-permute-start.31 = (bf16[48,1152]{1,0:T(8,128)(2,1)S(1)}, bf16[48,1152]{1,0:T(8,128)(2,1)S(1)}, u32[]{:S(2)}, u32[]{:S(2)}) collective-permute-start(bf16[48,1152]{1,0:T(8,128)(2,1)S(1)} %fusion.9), channel_id=1, source_target_pairs={{0,24},{2,26},{4,28},{6,30},{8,16},{10,18},{12,20},{14,22},{16,8},... | collective-permute-start | bytes 331784 | tf_op jit(solution)/shard_map/ppermute | solution.py:1088
  450.0 14.0 %collective-permute-start.42 = (bf16[2,144,768]{2,1,0:T(8,128)(2,1)}, bf16[2,144,768]{2,1,0:T(8,128)(2,1)}, u32[]{:S(2)}, u32[]{:S(2)}) collective-permute-start(bf16[2,144,768]{2,1,0:T(8,128)(2,1)} %pad_maximum_fusion.13), channel_id=1, source_target_pairs={{0,4},{2,6},{4,0},{6,2},{8,12},{10,14},{12,8},{14,10},{16,20},{18,... | collective-permute-start | bytes 1327112 | tf_op jit(solution)/shard_map/ppermute | solution.py:946
  454.6 12.9 %collective-permute-start.32 = (bf16[192,1152]{1,0:T(8,128)(2,1)S(1)}, bf16[192,1152]{1,0:T(8,128)(2,1)}, u32[]{:S(2)}, u32[]{:S(2)}) collective-permute-start(bf16[192,1152]{1,0:T(8,128)(2,1)S(1)} %bitcast.108), channel_id=1, source_target_pairs={{0,2},{2,0},{4,6},{6,4},{8,10},{10,8},{12,14},{14,12},{16,18},{18,... | collective-permute-start | bytes 1327112 | tf_op jit(solution)/shard_map/ppermute | solution.py:1088
  454.7 18.7 %collective-permute-start.33 = (bf16[192,1152]{1,0:T(8,128)(2,1)S(1)}, bf16[192,1152]{1,0:T(8,128)(2,1)}, u32[]{:S(2)}, u32[]{:S(2)}) collective-permute-start(bf16[192,1152]{1,0:T(8,128)(2,1)S(1)} %bitcast.109), channel_id=1, source_target_pairs={{0,4},{2,6},{4,0},{6,2},{8,12},{10,14},{12,8},{14,10},{16,20},{18,... | collective-permute-start | bytes 1327112 | tf_op jit(solution)/shard_map/ppermute | solution.py:1088
  455.9 17.5 %collective-permute-start.34 = (bf16[192,1152]{1,0:T(8,128)(2,1)S(1)}, bf16[192,1152]{1,0:T(8,128)(2,1)}, u32[]{:S(2)}, u32[]{:S(2)}) collective-permute-start(bf16[192,1152]{1,0:T(8,128)(2,1)S(1)} %bitcast.110), channel_id=1, source_target_pairs={{0,6},{2,4},{4,2},{6,0},{8,14},{10,12},{12,10},{14,8},{16,22},{18,... | collective-permute-start | bytes 1327112 | tf_op jit(solution)/shard_map/ppermute | solution.py:1088
  464.0 34.6 %collective-permute-start.22 = (bf16[1536,768]{1,0:T(8,128)(2,1)S(1)}, bf16[1536,768]{1,0:T(8,128)(2,1)}, u32[]{:S(2)}, u32[]{:S(2)}) collective-permute-start(bf16[1536,768]{1,0:T(8,128)(2,1)S(1)} %convolution_convert_fusion), channel_id=1, source_target_pairs={{0,1},{1,0},{2,3},{3,2},{4,5},{5,4},{6,7},{7,6},{8,9},{9,8},{10,11... | collective-permute-start | bytes 7077896 | tf_op jit(solution)/shard_map/ppermute | solution.py:1061
  466.3 24.0 %collective-permute-start.43 = (bf16[4,144,768]{2,1,0:T(8,128)(2,1)S(1)}, bf16[4,144,768]{2,1,0:T(8,128)(2,1)S(1)}, u32[]{:S(2)}, u32[]{:S(2)}) collective-permute-start(bf16[4,144,768]{2,1,0:T(8,128)(2,1)S(1)} %get-tuple-element.347), channel_id=1, source_target_pairs={{0,4},{2,6},{4,0},{6,2},{8,12},{10,14},{12,8},{14,10},{16,20},{18,... | collective-permute-start | bytes 2654216 | tf_op jit(solution)/shard_map/ppermute | solution.py:946
  467.5 22.8 %collective-permute-start.44 = (bf16[4,144,768]{2,1,0:T(8,128)(2,1)S(1)}, bf16[4,144,768]{2,1,0:T(8,128)(2,1)S(1)}, u32[]{:S(2)}, u32[]{:S(2)}) collective-permute-start(bf16[4,144,768]{2,1,0:T(8,128)(2,1)S(1)} %get-tuple-element.345), channel_id=1, source_target_pairs={{0,2},{2,0},{4,6},{6,4},{8,10},{10,8},{12,14},{14,12},{16,18},{18,... | collective-permute-start | bytes 2654216 | tf_op jit(solution)/shard_map/ppermute | solution.py:946
  (37 other events, 495.4 us)

commit v2 on v1

--- a/solution.py
+++ b/solution.py
@@ -758,8 +758,7 @@
     )(unit, inverse, grad_sum, own, other, gain, out_weight, *into)
 
 
-NORM_SLOT = 16
-OUT_SLOT = 8
+SLOT = 8
 
 
 def first_rows(source, mine_ref, away, second, count):
@@ -785,11 +784,11 @@
     )(mine, *rows, *columns, *lines)
 
 
-def outer_terms(mine, act, grad_ffn, norm_lines):
+def outer_terms(mine, act, grad_ffn):
     units, width = act.shape[1], grad_ffn.shape[1]
-    counts = [units // 16, NORM_SLOT]
-
-    def body(mine_ref, act_ref, ffn_ref, norm_ref, *rest):
+    counts = [units // 16]
+
+    def body(mine_ref, act_ref, ffn_ref, *rest):
         outs, (outer,) = rest[:4], rest[4:]
 
         @pl.when(pl.program_id(0) == 0)
@@ -800,38 +799,34 @@
 
         @pl.when(pl.program_id(0) == pl.num_programs(0) - 1)
         def _():
-            slot = lax.broadcasted_iota(jnp.int32, (NORM_SLOT, width), 0) == 0
+            for away, ref in enumerate(outs):
+                for second in range(4):
+                    rows = first_rows(outer, mine_ref, away, second, counts[0])
+                    ref[second] = rows.astype(BF16)
+
+    return terms_call(body, mine, [act, grad_ffn], [], [], counts, width, [(units, width)], 9)
+
+
+def inner_terms(mine, normed, grad_pre, mixed, grad_proj, norm_lines):
+    units, width, cols = grad_pre.shape[1], normed.shape[1], mixed.shape[0]
+    counts = [width // 16, width // 16, cols // 16, SLOT]
+
+    def body(mine_ref, low_ref, pre_ref, proj_ref, mixed_ref, norm_ref, *rest):
+        outs, (inner, out) = rest[:4], rest[4:]
+
+        @pl.when(pl.program_id(0) == 0)
+        def _():
+            inner[...] = jnp.zeros_like(inner)
+            out[...] = jnp.zeros_like(out)
+
+        inner[...] += contract(low_ref[...], pre_ref[...], 0, 0)
+        out[...] += contract(mixed_ref[...], proj_ref[...], 1, 0)
+
+        @pl.when(pl.program_id(0) == pl.num_programs(0) - 1)
+        def _():
+            slot = lax.broadcasted_iota(jnp.int32, (SLOT, width), 0) == 0
             for away, ref in enumerate(outs):
                 line = norm_ref[pl.ds(lax.bitwise_xor(mine_ref[0], away), 1), :]
-                for second in range(4):
-                    rows = first_rows(outer, mine_ref, away, second, counts[0])
-                    ref[second, pl.ds(0, counts[0]), :] = rows.astype(BF16)
-                    lines = jnp.where(slot, line if second == 0 else 0.0, 0.0)
-                    ref[second, pl.ds(counts[0], NORM_SLOT), :] = lines.astype(BF16)
-
-    return terms_call(
-        body, mine, [act, grad_ffn], [], [norm_lines], counts, width, [(units, width)], 9
-    )
-
-
-def inner_terms(mine, normed, grad_pre, mixed, grad_proj):
-    units, width, cols = grad_pre.shape[1], normed.shape[1], mixed.shape[0]
-    counts = [width // 16, width // 16, cols // 16, OUT_SLOT]
-
-    def body(mine_ref, low_ref, pre_ref, proj_ref, mixed_ref, *rest):
-        outs, (inner, out) = rest[:4], rest[4:]
-
-        @pl.when(pl.program_id(0) == 0)
-        def _():
-            inner[...] = jnp.zeros_like(inner)
-            out[...] = jnp.zeros_like(out)
-
-        inner[...] += contract(low_ref[...], pre_ref[...], 0, 0)
-        out[...] += contract(mixed_ref[...], proj_ref[...], 1, 0)
-
-        @pl.when(pl.program_id(0) == pl.num_programs(0) - 1)
-        def _():
-            for away, ref in enumerate(outs):
                 for second in range(4):
                     both = first_rows(inner, mine_ref, away, second, counts[0]).astype(BF16)
                     ref[second, pl.ds(0, counts[0]), :] = both[:, :width]
@@ -839,16 +834,16 @@
                     tail = jnp.concatenate(
                         [
                             first_rows(out, mine_ref, away, second, counts[2]),
-                            jnp.zeros((OUT_SLOT, width), F32),
+                            jnp.where(slot, line if second == 0 else 0.0, 0.0),
                         ],
                         axis=0,
                     )
-                    ref[second, pl.ds(counts[0] + counts[1], counts[2] + OUT_SLOT), :] = (
+                    ref[second, pl.ds(counts[0] + counts[1], counts[2] + SLOT), :] = (
                         tail.astype(BF16)
                     )
 
     return terms_call(
-        body, mine, [normed, grad_pre, grad_proj], [mixed], [], counts, width,
+        body, mine, [normed, grad_pre, grad_proj], [mixed], [norm_lines], counts, width,
         [(width, units), (cols, width)], 9,
     )
 
@@ -861,9 +856,30 @@
     return terms_for(jnp.concatenate(pieces, axis=1), bits)
 
 
-def gathered_sums(gathered, counts, targets, shapes):
+def lay_out(piece, counts, order, first, is_line, outs):
+    width = piece.shape[1]
+    rows = piece[...].astype(F32)
+
+    def at(count):
+        return pl.ds(order * count if isinstance(order, int) else pl.multiple_of(order * count, count), count)
+
+    if len(counts) == 1:
+        outs[0][at(counts[0]), :] = rows
+        return
+    inner, out, norm, taps = outs
+    marks = [sum(counts[:index]) for index in range(len(counts))]
+    inner[at(counts[0]), pl.ds(0, width)] = rows[: marks[1]]
+    inner[at(counts[1]), pl.ds(width, width)] = rows[marks[1] : marks[2]]
+    out[at(counts[2]), :] = rows[marks[2] : marks[3]]
+    taps[pl.ds(order, 1), :] = rows[marks[3] + 1 : marks[3] + 2]
+
+    @pl.when(is_line)
+    def _():
+        norm[pl.ds(first, 1), :] = rows[marks[3] : marks[3] + 1]
+
+
+def gathered_sums(gathered, counts, shapes):
     peers = gathered.shape[0]
-    width = gathered.shape[2]
     groups = bit_groups(peers)
 
     def body(in_ref, *outs):
@@ -872,69 +888,37 @@
             for bits in groups:
                 size = 1 << len(bits)
                 order = order * size + ((at_place >> bits[0]) & (size - 1))
-            at = 0
-            for count, target in zip(counts, targets):
-                if target is not None:
-                    index, column = target
-                    rows = in_ref[at_place, pl.ds(at, count), :].astype(F32)
-                    if column is not None:
-                        outs[index][pl.ds(order * count, count), pl.ds(column, width)] = rows
-                    elif order % (peers // 4) == 0:
-                        outs[index][pl.ds(order // (peers // 4), 1), :] = rows[:1]
-                at += count
-
+            share = peers // 4
+            lay_out(in_ref.at[at_place], counts, order, order // share, order % share == 0, outs)
+
+    return sums_call(body, [], [gathered], shapes)
+
+
+def placed_sums(mine, arrays, aways, counts, shapes):
+    def body(mine_ref, *refs):
+        ins, outs = refs[: len(arrays)], refs[len(arrays) :]
+        for ref, pairs in zip(ins, aways):
+            for piece, (first_away, second_away) in enumerate(pairs):
+                first = lax.bitwise_xor(mine_ref[0], first_away)
+                second = lax.bitwise_xor(mine_ref[1], second_away)
+                lay_out(ref.at[piece], counts, first * 4 + second, first, second == 0, outs)
+
+    return sums_call(body, [mine], arrays, shapes)
+
+
+def sums_call(body, scalars, arrays, shapes):
     def whole(shape):
         return pl.BlockSpec(shape, lambda: (0,) * len(shape))
 
     return pl.pallas_call(
         body,
-        in_specs=[whole(gathered.shape)],
+        in_specs=[pl.BlockSpec(memory_space=pltpu.SMEM)] * len(scalars)
+        + [whole(array.shape) for array in arrays],
         out_specs=[whole(shape) for shape in shapes],
         out_shape=[jax.ShapeDtypeStruct(shape, F32) for shape in shapes],
         compiler_params=pltpu.CompilerParams(vmem_limit_bytes=VMEM_BYTES),
         cost_estimate=lasting(4),
-    )(gathered)
-
-
-def placed_sums(mine, arrays, aways, counts, targets, shapes):
-    width = arrays[0].shape[2]
-
-    def body(mine_ref, *refs):
-        ins, outs = refs[: len(arrays)], refs[len(arrays) :]
-        pieces = [(ref, at, *away) for ref, pairs in zip(ins, aways) for at, away in enumerate(pairs)]
-        for ref, piece, first_away, second_away in pieces:
-            first = lax.bitwise_xor(mine_ref[0], first_away)
-            second = lax.bitwise_xor(mine_ref[1], second_away)
-            order = first * 4 + second
-            at = 0
-            for count, target in zip(counts, targets):
-                rows = pl.ds(at, count)
-                at += count
-                if target is None:
-                    continue
-                out = outs[target[0]]
-                if target[1] is not None:
-                    to = pl.ds(pl.multiple_of(order * count, count), count)
-                    out[to, pl.ds(target[1], width)] = ref[piece, rows, :].astype(F32)
-                elif out.shape[0] > 4:
-                    out[pl.ds(order, 1), :] = ref[piece, rows, :].astype(F32)[:1]
-                else:
-
-                    @pl.when(second == 0)
-                    def _():
-                        out[pl.ds(first, 1), :] = ref[piece, rows, :].astype(F32)[:1]
-
-    def whole(shape):
-        return pl.BlockSpec(shape, lambda: (0,) * len(shape))
-
-    return pl.pallas_call(
-        body,
-        in_specs=[pl.BlockSpec(memory_space=pltpu.SMEM)] + [whole(array.shape) for array in arrays],
-        out_specs=[whole(shape) for shape in shapes],
-        out_shape=[jax.ShapeDtypeStruct(shape, F32) for shape in shapes],
-        compiler_params=pltpu.CompilerParams(vmem_limit_bytes=VMEM_BYTES),
-        cost_estimate=lasting(4),
-    )(mine, *arrays)
+    )(*scalars, *arrays)
 
 
 def by_twos(steps):
@@ -966,16 +950,10 @@
     )
 
 
-def placed(own, near, far, counts, targets, shapes):
-    peers = lax.axis_size("seq")
+def placed(own, near, far, counts, shapes):
     place = lax.axis_index("seq")
     if not near:
-        gathered = lax.all_gather(own, "seq", axis=0)
-        single = [target for target in targets if target is not None and target[1] is None]
-        if not single or shapes[single[0][0]][0] == 4:
-            return gathered_sums(gathered, counts, targets, shapes)
-        sums = gathered_sums(gathered, counts[:-1], targets[:-1], shapes[:-1])
-        return [*sums, gathered[:, sum(counts[:-1])].astype(F32)]
+        return gathered_sums(lax.all_gather(own, "seq", axis=0), counts, shapes)
     mine = jnp.stack([place & 3, (place >> 2) & 3]).astype(jnp.int32)
     aways = [
         [(0, 0), (0, 1), (0, 2), (0, 3)],
@@ -984,7 +962,7 @@
         [(2, 0), (2, 1), (3, 0), (3, 1)],
         [(1, 2), (1, 3), (3, 2), (3, 3)],
     ]
-    return placed_sums(mine, [own, *near, *far], aways, counts, targets, shapes)
+    return placed_sums(mine, [own, *near, *far], aways, counts, shapes)
 
 
 def unit_back(moved_pairs, moved_values, short_parts, unit, inverse):
@@ -1230,11 +1208,11 @@
     peers = lax.axis_size("seq")
     steps = bit_groups(peers)
     mine = (lax.axis_index("seq") & 3).astype(jnp.int32)[None]
-    outer_counts, outer_terms_now = outer_terms(mine, act_low, grad_ffn_low, norm_lines)
+    outer_counts, outer_terms_now = outer_terms(mine, act_low, grad_ffn_low)
     outer_terms_now, grad_pre_low = after(outer_terms_now, grad_pre_low)
     outer_came = terms_sent(outer_terms_now, steps[0])
     inner_counts, inner_terms_now = inner_terms(
-        mine, normed_low, grad_pre_low, mixed, grad_proj_low
+        mine, normed_low, grad_pre_low, mixed, grad_proj_low, norm_lines
     )
     inner_terms_now, long_grad = after(inner_terms_now, long_grad)
     long_grad = by_position(long_grad, 1)[0]
@@ -1295,12 +1273,15 @@
     owner = (jnp.arange(heads_dev) == unit_head) & (place < units)
     kernel_part = short_taps[:, 0, taps] + jnp.where(owner[:, None], long_taps[:, taps], 0.0)
     taps_line = kernel_part.reshape(1, -1)
-    taps_line = jnp.pad(taps_line, ((0, 15), (0, width - taps_line.shape[1]))).astype(BF16)
-    outer_sum, norm_sums = placed(
-        outer_own, outer_near, outer_far, outer_counts, [(0, 0), (1, None)],
-        [outer_weight.shape, (4, width)],
-    )
-    inner_own = gather_second(jnp.concatenate([inner_part, taps_line], axis=0), steps)
+    taps_line = jnp.pad(taps_line, ((0, 0), (0, width - taps_line.shape[1]))).astype(BF16)
+    (outer_sum,) = placed(
+        outer_own, outer_near, outer_far, outer_counts, [outer_weight.shape]
+    )
+    taps_at = sum(inner_counts[:-1]) + 1
+    inner_part = jnp.concatenate(
+        [inner_part[:taps_at], taps_line, inner_part[taps_at + 1 :]], axis=0
+    )
+    inner_own = gather_second(inner_part, steps)
     inner_near = gather_near(inner_own, steps)
     inner_far = gather_far(inner_own, inner_near, steps)
 
@@ -1319,10 +1300,9 @@
         weight_part = terms_gathered(weight_part, bits).reshape(-1, 3 * head_cols)
     weight_sum = weight_part.astype(F32)
     token_grad = grad_hidden + (token_own.astype(F32) + other_half(token_own).astype(F32))
-    inner_sum, out_sum, tap_lines = placed(
-        inner_own, inner_near, inner_far, inner_counts + [16],
-        [(0, 0), (0, width), (1, 0), None, (2, None)],
-        [inner_weight.shape, out_weight.shape, (peers, width)],
+    inner_sum, out_sum, norm_sums, tap_lines = placed(
+        inner_own, inner_near, inner_far, inner_counts,
+        [inner_weight.shape, out_weight.shape, (4, width), (peers, width)],
     )
     kernel_sum = jnp.sum(tap_lines[:, : heads_dev * CONV_WIDTH], axis=0).reshape(
         heads_dev, CONV_WIDTH

time: 514 us -> 503 us (0.979)
  waiting for transfers between devices: 51.9 us -> 46.7 us
  transfers between devices with their start and end apart: 50 -> 50, of which waited for: 18 -> 15; matrix products, arithmetic and copies ran while one was open for 7% -> 7% of each run, Pallas kernels for 36% -> 37%
where the time goes in v2:
time: 503 us; the launch traced here: 494 us
  Pallas kernels  288 us (57%)
  starting transfers between devices  103 us (20%)
  waiting for transfers between devices  46.7 us (9%)
  other arithmetic  23.1 us (5%)
  local copies, waits for them, and re-layouts  22.8 us (5%)
  matrix products  9.22 us (2%)
    pallas_call x1, Pallas kernels, long_forward(): pl.pallas_call(body, grid=(blocks,), in_specs=[pl.BlockSpec((head_dim, PI...  71.3 us
    ppermute x30, starting transfers between devices, terms_sent(): lax.ppermute(term, 'seq', [(i, i ^ away << bits[0]) for i in range(peers)])  45 us
    all_to_all x5, starting transfers between devices, exchange(): return lax.all_to_all(pieces, 'seq', 0, 0, axis_index_groups=groups)  41.5 us
    pallas_call x1, Pallas kernels, long_back_pairs(): pl.pallas_call(body, grid=(blocks,), in_specs=[piece, whole, whole, piece...  32.2 us
    ppermute x30, waiting for transfers between devices, terms_sent(): lax.ppermute(term, 'seq', [(i, i ^ away << bits[0]) for i in range(peers)])  29 us
    pallas_call x1, Pallas kernels, short_forward(): pl.pallas_call(body, grid=(blocks,), in_specs=[pl.BlockSpec(memory_space=...  26.4 us
    pallas_call x1, Pallas kernels, short_backward(): pl.pallas_call(body, grid=(blocks,), in_specs=[pl.BlockSpec(memory_space=...  24.7 us
    pallas_call x2, Pallas kernels, feed_forward(): pl.pallas_call(body, grid=(count,), in_specs=[rows, own_rows, own_rows, l...  24 us
  transfers between devices with their start and end apart: 50, of which 15 were waited for; matrix products, arithmetic and copies ran while one was open for 7% of the time, Pallas kernels for 37%

profile of v2, /device:TPU:0, one launch (start us, length us, event | category | flops | bytes accessed | tf_op | source)
XLA Modules:
  0.0 494.4 jit_solution(18338630789886724558)
XLA Ops:
  0.6 9.9 %shard_map.237 = (bf16[16,192,256]{2,1,0:T(8,128)(2,1)}, bf16[3,6,64,1024]{3,2,1,0:T(8,128)(2,1)}, f32[2,6,64,1536]{3,2,1,0:T(8,128)}, f32[2,6,1,1536]{3,2,1,0:T(1,128)}) custom-call(bf16[1536,768]{1,0:T(8,128)(2,1)} %t_ref.5, bf16[768,384]{1,0:T(8,128)(2,1)} %wq_ref.1, bf16[768,384]{1,0:T(8,128)(2,1)} %wk_ref.1, bf16[768,384]{1,0:T(8,128)(2,1)} %wv_ref.1), custom_call_target="tpu_custom_call" | custom-call | flops 11500000256 | tf_op jit(solution)/shard_map/pallas_call | solution.py:473
  10.6 8.5 %all-to-all-start = ((bf16[16,192,256]{2,1,0:T(8,128)(2,1)}), bf16[16,192,256]{2,1,0:T(8,128)(2,1)S(1)}, u32[]{:S(2)}, u32[]{:S(2)}) async-start(bf16[16,192,256]{2,1,0:T(8,128)(2,1)} %get-tuple-element.162), calls=%async_computation | async-start | bytes 3145728 | tf_op jit(solution)/shard_map/all_to_all | solution.py:1122
  22.8 26.4 %shard_map.238 = (bf16[6,64,1024]{2,1,0:T(8,128)(2,1)}, bf16[4,6,1024,256]{3,2,1,0:T(8,128)(2,1)}, bf16[4,6,1024,256]{3,2,1,0:T(8,128)(2,1)}) custom-call(s32[2,4]{1,0:T(2,128)} %pad_add_fusion.reach_ref, s32[1,1024]{1,0:T(1,128)} %bitcast.135, s32[1088,1]{1,0:T(8,128)} %broadcast_in_dim.117.col_ref, ...), custom_call_target="tpu_custom_call" | custom-call | flops 32199999488 | tf_op jit(solution)/shard_map/pallas_call | solution.py:325
  49.2 3.3 shard_map.239
  55.9 71.3 %shard_map.240 = (bf16[16,64,256]{2,1,0:T(8,128)(2,1)}, bf16[16,4096,256]{2,1,0:T(8,128)(2,1)}, bf16[16,4096,256]{2,1,0:T(8,128)(2,1)}) custom-call(bf16[64,4096]{1,0:T(8,128)(2,1)} %bitcast.124, bf16[64,4096]{1,0:T(8,128)(2,1)} %bitcast.126, bf16[64,4096]{1,0:T(8,128)(2,1)} %bitcast.102, f32[1,640]{1,0:T(1,128)} %pad_dynamic-slice_fusion.line_ref), custom_call_target="tpu_custom_call" | custom-call | flops 80499998720 | tf_op jit(solution)/shard_map/pallas_call | solution.py:154
  128.5 15.1 %all-to-all-start.1 = ((bf16[16,64,256]{2,1,0:T(8,128)(2,1)}), bf16[16,64,256]{2,1,0:T(8,128)(2,1)S(1)}, u32[]{:S(2)}, u32[]{:S(2)}) async-start(bf16[16,64,256]{2,1,0:T(8,128)(2,1)} %get-tuple-element.169), calls=%async_computation.1 | async-start | bytes 1048576 | tf_op jit(solution)/shard_map/all_to_all | solution.py:1122
  143.6 14.6 %shard_map.241 = (f32[1536,768]{1,0:T(8,128)}, f32[1536,1]{1,0:T(8,128)}, bf16[1536,768]{1,0:T(8,128)(2,1)}, bf16[1536,1536]{1,0:T(8,128)(2,1)}, bf16[1536,1536]{1,0:T(8,128)(2,1)}, /*index=5*/bf16[1024,768]{1,0:T(8,128)(2,1)}) custom-call(bf16[1536,768]{1,0:T(8,128)(2,1)} %t_ref.5, bf16[1024,768]{1,0:T(8,128)(2,1)} %get-tuple-element.170.own_ref, ...), custom_call_target="tpu_custom_call" | custom-call | flops 13799999488 | tf_op jit(solution)/shard_map/pallas_call | solution.py:598
  159.8 3.0 shard_map.242
  162.9 2.5 collective-permute-done.1.other_ref
  166.2 9.4 %shard_map.243 = (f32[1536,768]{1,0:T(8,128)}, f32[1536,1]{1,0:T(8,128)}, bf16[1536,768]{1,0:T(8,128)(2,1)}, bf16[1536,1536]{1,0:T(8,128)(2,1)}, bf16[1536,1536]{1,0:T(8,128)(2,1)}, /*index=5*/bf16[512,768]{1,0:T(8,128)(2,1)}) custom-call(bf16[1536,768]{1,0:T(8,128)(2,1)} %t_ref.5, ...), custom_call_target="tpu_custom_call", output_to_operand_aliasing={{0}: (7, {}), {1}: (8, {}), {2}: (9, {}), {3}: (10, {}), {4... | custom-call | flops 6899999744 | tf_op jit(solution)/shard_map/pallas_call | solution.py:598
  179.0 8.7 %shard_map.244 = (bf16[1536,768]{1,0:T(8,128)(2,1)}, f32[1536,768]{1,0:T(8,128)}, bf16[1536,768]{1,0:T(8,128)(2,1)}, bf16[1536,1536]{1,0:T(8,128)(2,1)}, bf16[51...) custom-call(f32[1536,768]{1,0:T(8,128)} %get-tuple-element.180.unit_ref, ...), custom_call_target="tpu_custom_call" | custom-call | flops 6899999744 | tf_op jit(solution)/shard_map/pallas_call | solution.py:664
  188.0 2.4 collective-permute-done.3.other_ref
  191.2 5.2 %shard_map.245 = (f32[1536,768]{1,0:T(8,128)}, bf16[1536,768]{1,0:T(8,128)(2,1)}, bf16[16,64,256]{2,1,0:T(8,128)(2,1)}, f32[1,768]{1,0:T(1,128)}, f32[1,768]{1,0:T(1,128)}) custom-call(f32[1536,768]{1,0:T(8,128)} %get-tuple-element.180.unit_ref, f32[1536,1]{1,0:T(8,128)} %get-tuple-element.181.inv_ref, f32[1536,768]{1,0:T(8,128)} %get-tuple-element.194.sum_ref.rest_1_, ...), custom_call_target="tpu_custom_call" | custom-call | flops 4600000000 | tf_op jit(solution)/shard_map/pallas_call | solution.py:739
  197.6 13.3 %shard_map.246 = (bf16[1536,768]{1,0:T(8,128)(2,1)}, f32[1536,768]{1,0:T(8,128)}, bf16[1536,768]{1,0:T(8,128)(2,1)}, bf16[1536,1536]{1,0:T(8,128)(2,1)}, bf16[10...) custom-call(f32[1536,768]{1,0:T(8,128)} %get-tuple-element.180.unit_, ...), custom_call_target="tpu_custom_call", output_to_operand_aliasing={{0}: (11, {}), {1}: (12, {}), {2}: (13, {}), {3}: (14, {})} | custom-call | flops 13799999488 | tf_op jit(solution)/shard_map/pallas_call | solution.py:664
  211.1 8.2 %shard_map.248 = (bf16[4,96,768]{2,1,0:T(8,128)(2,1)}, bf16[4,96,768]{2,1,0:T(8,128)(2,1)}, bf16[4,96,768]{2,1,0:T(8,128)(2,1)}, bf16[4,96,768]{2,1,0:T(8,128)(2,1)}) custom-call(s32[1]{0:T(128)} %bitcast.8.mine_ref, bf16[1536,1536]{1,0:T(8,128)(2,1)} %get-tuple-element.203.act_ref, bf16[1536,768]{1,0:T(8,128)(2,1)} %get-tuple-element.204.ffn_ref), custom_call_target="tpu_custom_call" | custom-call | flops 10350000128 | tf_op jit(solution)/shard_map/pallas_call | solution.py:772
  219.3 6.2 %all-to-all-start.2 = ((bf16[16,64,256]{2,1,0:T(8,128)(2,1)}), bf16[16,64,256]{2,1,0:T(8,128)(2,1)S(1)}, u32[]{:S(2)}, u32[]{:S(2)}) async-start(bf16[16,64,256]{2,1,0:T(8,128)(2,1)} %get-tuple-element.230), calls=%async_computation.2 | async-start | bytes 1048576 | tf_op jit(solution)/shard_map/all_to_all | solution.py:1122
  225.5 1.9 collective-permute-start.6
  229.1 6.9 %shard_map.247 = (f32[1536,768]{1,0:T(8,128)}, bf16[1536,768]{1,0:T(8,128)(2,1)}, bf16[6,64,1024]{2,1,0:T(8,128)(2,1)}, f32[1,768]{1,0:T(1,128)}, f32[1,768]{1,0:T(1,128)}) custom-call(f32[1536,768]{1,0:T(8,128)} %get-tuple-element.180.unit_ref, f32[1536,1]{1,0:T(8,128)} %get-tuple-element.181.inv_ref, ...), custom_call_target="tpu_custom_call", output_to_operand_aliasing={{0}: (7, {}), {1}: (8, {})} | custom-call | flops 9200000000 | tf_op jit(solution)/shard_map/pallas_call | solution.py:739
  238.1 10.3 %shard_map.249 = (bf16[4,128,768]{2,1,0:T(8,128)(2,1)}, bf16[4,128,768]{2,1,0:T(8,128)(2,1)}, bf16[4,128,768]{2,1,0:T(8,128)(2,1)}, bf16[4,128,768]{2,1,0:T(8,128)(2,1)}) custom-call(s32[1]{0:T(128)} %bitcast.8.mine_ref, bf16[1536,768]{1,0:T(8,128)(2,1)} %get-tuple-element.214.low_ref, bf16[1536,1536]{1,0:T(8,128)(2,1)} %get-tuple-element.215.pre_ref, ...), custom_call_target="tpu_custom_call" | custom-call | flops 10350000128 | tf_op jit(solution)/shard_map/pallas_call | solution.py:772
  249.2 23.0 %shard_map.250 = (bf16[16,64,256]{2,1,0:T(8,128)(2,1)}, f32[1,640]{1,0:T(1,128)}) custom-call(bf16[64,4096]{1,0:T(8,128)(2,1)} %bitcast.103, bf16[64,4096]{1,0:T(8,128)(2,1)} %bitcast.105, bf16[16,4096,256]{2,1,0:T(8,128)(2,1)} %get-tuple-element.236.w_ref), custom_call_target="tpu_custom_call" | custom-call | flops 1150000000 | tf_op jit(solution)/shard_map/pallas_call | solution.py:200
  273.2 2.8 collective-permute-start.10
  278.1 6.1 %all-to-all-start.3 = ((bf16[16,64,256]{2,1,0:T(8,128)(2,1)}), bf16[16,64,256]{2,1,0:T(8,128)(2,1)}, u32[]{:S(2)}, u32[]{:S(2)}) async-start(bf16[16,64,256]{2,1,0:T(8,128)(2,1)} %get-tuple-element.252), calls=%async_computation.3 | async-start | bytes 1048576 | tf_op jit(solution)/shard_map/all_to_all | solution.py:1122
  284.2 1.9 collective-permute-start.12
  289.1 32.2 %shard_map.251 = (bf16[16,64,256]{2,1,0:T(8,128)(2,1)}, bf16[16,64,256]{2,1,0:T(8,128)(2,1)}) custom-call(bf16[64,4096]{1,0:T(8,128)(2,1)} %bitcast.125, bf16[64,4096]{1,0:T(8,128)(2,1)} %bitcast.127, bf16[64,4096]{1,0:T(8,128)(2,1)} %bitcast.104, bf16[64,4096]{1,0:T(8,128)(2,1)} %bitcast.106, bf16[16,4096,256]{2,1,0:T(8,128)(2,1)} %get-tuple-element.254.s_ref), custom_call_target="tpu_custom_call" | custom-call | flops 46000001024 | tf_op jit(solution)/shard_map/pallas_call | solution.py:258
  330.0 2.4 collective-permute-start.16
  333.0 5.6 %all-to-all-start.4 = ((bf16[16,128,256]{2,1,0:T(8,128)(2,1)}), bf16[16,128,256]{2,1,0:T(8,128)(2,1)S(1)}, u32[]{:S(2)}, u32[]{:S(2)}) async-start(bf16[16,128,256]{2,1,0:T(8,128)(2,1)} %pad_maximum_fusion.2), calls=%async_computation.4 | async-start | bytes 2097152 | tf_op jit(solution)/shard_map/all_to_all | solution.py:1122
  340.4 2.4 collective-permute-start.36
  343.1 6.9 %collective-permute-done.16 = bf16[96,768]{1,0:T(8,128)(2,1)S(1)} collective-permute-done((bf16[96,768]{1,0:T(8,128)(2,1)S(1)}, bf16[96,768]{1,0:T(8,128)(2,1)S(1)}, u32[]{:S(2)}, u32[]{:S(2)}) %collective-permute-start.16) | collective-permute-done | bytes 147488 | tf_op jit(solution)/shard_map/ppermute | solution.py:1066
  351.8 24.7 %shard_map.252 = (f32[6,64,1024]{2,1,0:T(8,128)}, f32[6,64,1024]{2,1,0:T(8,128)}, f32[6,64,1024]{2,1,0:T(8,128)}, f32[6,1,640]{2,1,0:T(1,128)}) custom-call(s32[2,4]{1,0:T(2,128)} %pad_add_fusion.reach_ref, s32[1,1024]{1,0:T(1,128)} %bitcast.136, s32[1088,1]{1,0:T(8,128)} %broadcast_in_dim.117.col_ref, ...), custom_call_target="tpu_custom_call" | custom-call | flops 32199999488 | tf_op jit(solution)/shard_map/pallas_call | solution.py:400
  379.1 8.2 %collective-permute-start.20 = (bf16[4,96,768]{2,1,0:T(8,128)(2,1)}, bf16[4,96,768]{2,1,0:T(8,128)(2,1)}, u32[]{:S(2)}, u32[]{:S(2)}) collective-permute-start(bf16[4,96,768]{2,1,0:T(8,128)(2,1)} %pad_maximum_fusion.8), channel_id=1, source_target_pairs={{0,4},{2,6},{4,0},{6,2},{8,12},{10,14},{12,8},{14,10},{16,20},{18,... | collective-permute-start | bytes 1769480 | tf_op jit(solution)/shard_map/ppermute | solution.py:930
  387.3 8.4 %shard_map.253 = bf16[1152,1536]{1,0:T(8,128)(2,1)} custom-call(bf16[16,128,256]{2,1,0:T(8,128)(2,1)} %copy-done.2, bf16[16,64,256]{2,1,0:T(8,128)(2,1)} %all-to-all-done.3.refs_1_, f32[6,64,1024]{2,1,0:T(8,128)} %get-tuple-element.283.refs_2_, f32[6,64,1024]{2,1,0:T(8,128)} %get-tuple-element.284.refs_3_, f32[6,64,1024]{2,1,0:T(8,128)} %get-tuple-element.285.refs_4_, ...), custom_call_target="tpu_custom_call" | custom-call | flops 9200000000 | tf_op jit(solution)/shard_map/pallas_call | solution.py:1018
  398.1 4.3 collective-permute-start.38
  402.4 5.4 %convolution_convert_fusion.1 = bf16[1152,768]{0,1:T(8,128)(2,1)S(1)} fusion(bf16[1152,1536]{1,0:T(8,128)(2,1)} %shard_map.253, bf16[1536,768]{1,0:T(8,128)(2,1)S(1)} %copy-done.1), kind=kOutput, calls=%fused_computation.2 | convolution fusion | flops 2718793728 | bytes 7667712 | tf_op jit(solution)/shard_map/dot_general | solution.py:68
  409.6 2.1 collective-permute-start.24
  411.8 3.8 convolution_convert_fusion
  416.4 2.4 collective-permute-start.40
  418.8 3.5 collective-permute-done.24
  422.3 3.9 collective-permute-done.25
  426.9 3.0 collective-permute-start.27
  432.1 2.7 collective-permute-start.41
  442.1 4.1 collective-permute-done.30
  446.5 2.1 collective-permute-start.32
  450.1 4.1 shard_map.255
  454.2 2.2 pad_maximum_fusion.6
  458.4 5.2 %collective-permute-done.33 = bf16[192,1152]{1,0:T(8,128)(2,1)} collective-permute-done((bf16[192,1152]{1,0:T(8,128)(2,1)S(1)}, bf16[192,1152]{1,0:T(8,128)(2,1)}, u32[]{:S(2)}, u32[]{:S(2)}) %collective-permute-start.33) | collective-permute-done | bytes 442400 | tf_op jit(solution)/shard_map/ppermute | solution.py:1066
  467.9 10.5 %collective-permute-done.43.refs_3_ = bf16[4,128,768]{2,1,0:T(8,128)(2,1)S(1)} collective-permute-done((bf16[4,128,768]{2,1,0:T(8,128)(2,1)S(1)}, bf16[4,128,768]{2,1,0:T(8,128)(2,1)S(1)}, u32[]{:S(2)}, u32[]{:S(2)}) %collective-permute-start.43) | collective-permute-done | bytes 786464 | tf_op jit(solution)/shard_map/ppermute | solution.py:930
  480.2 5.0 %shard_map.254 = (f32[768,1536]{1,0:T(8,128)}, f32[384,768]{1,0:T(8,128)}, f32[4,768]{1,0:T(4,128)}, f32[16,768]{1,0:T(8,128)}) custom-call(s32[2]{0:T(128)} %pad_add_fusion.2.mine_ref, bf16[4,128,768]{2,1,0:T(8,128)(2,1)} %get-tuple-element.351.refs_0_, bf16[2,128,768]{2,1,0:T(8,128)(2,1)} %collective-permute-done.41.refs_1_, ...), custom_call_target="tpu_custom_call" | custom-call | flops 4600000000 | tf_op jit(solution)/shard_map/pallas_call | solution.py:913
  488.1 5.9 %add_add_fusion = f32[1536,768]{1,0:T(8,128)} fusion(f32[1536,768]{1,0:T(8,128)} %get-tuple-element.202, bf16[1536,768]{1,0:T(8,128)(2,1)} %collective-permute-done.22, bf16[1536,768]{1,0:T(8,128)(2,1)S(1)} %convolution_convert_fusion), kind=kLoop, calls=%fused_computation | loop fusion | flops 4718592 | bytes 14155776 | tf_op jit(solution)/shard_map/add | solution.py:1302
  (225 shorter events, 70.7 us)
Async XLA Ops:
  10.6 42.7 %all-to-all-start = ((bf16[16,192,256]{2,1,0:T(8,128)(2,1)}), bf16[16,192,256]{2,1,0:T(8,128)(2,1)S(1)}, u32[]{:S(2)}, u32[]{:S(2)}) async-start(bf16[16,192,256]{2,1,0:T(8,128)(2,1)} %get-tuple-element.162), calls=%async_computation | async-start | bytes 3145728 | tf_op jit(solution)/shard_map/all_to_all | solution.py:1122
  127.2 16.4 %collective-permute-start = (bf16[1024,768]{1,0:T(8,128)(2,1)S(1)}, bf16[1024,768]{1,0:T(8,128)(2,1)}, u32[]{:S(2)}, u32[]{:S(2)}) collective-permute-start(bf16[1024,768]{1,0:T(8,128)(2,1)S(1)} %copy-done.28), channel_id=1, source_target_pairs={{0,1},{1,0},{2,3},{3,2},{4,5},{5,4},{6,7},{7,6},{8,9},{9,8},{10,11... | collective-permute-start | bytes 4718600 | tf_op jit(solution)/shard_map/ppermute | solution.py:1039
  128.5 30.5 %all-to-all-start.1 = ((bf16[16,64,256]{2,1,0:T(8,128)(2,1)}), bf16[16,64,256]{2,1,0:T(8,128)(2,1)S(1)}, u32[]{:S(2)}, u32[]{:S(2)}) async-start(bf16[16,64,256]{2,1,0:T(8,128)(2,1)} %get-tuple-element.169), calls=%async_computation.1 | async-start | bytes 1048576 | tf_op jit(solution)/shard_map/all_to_all | solution.py:1122
  177.0 19.4 %collective-permute-start.4 = (bf16[1024,768]{1,0:T(8,128)(2,1)S(1)}, bf16[1024,768]{1,0:T(8,128)(2,1)S(1)}, u32[]{:S(2)}, u32[]{:S(2)}) collective-permute-start(bf16[1024,768]{1,0:T(8,128)(2,1)S(1)} %copy-done.27), channel_id=1, source_target_pairs={{0,1},{1,0},{2,3},{3,2},{4,5},{5,4},{6,7},{7,6},{8,9},{9,8},{10,11... | collective-permute-start | bytes 4718600 | tf_op jit(solution)/shard_map/ppermute | solution.py:1039
  187.8 2.6 collective-permute-start.3
  210.8 18.3 %collective-permute-start.5 = (bf16[1024,768]{1,0:T(8,128)(2,1)}, bf16[1024,768]{1,0:T(8,128)(2,1)}, u32[]{:S(2)}, u32[]{:S(2)}) collective-permute-start(bf16[1024,768]{1,0:T(8,128)(2,1)} %get-tuple-element.199.own_ref), channel_id=1, source_target_pairs={{0,1},{1,0},{2,3},{3,2},{4,5},{5,4},{6,7},{7,6},{8,9},{9,8},{10,11... | collective-permute-start | bytes 4718600 | tf_op jit(solution)/shard_map/ppermute | solution.py:1039
  219.3 29.1 %all-to-all-start.2 = ((bf16[16,64,256]{2,1,0:T(8,128)(2,1)}), bf16[16,64,256]{2,1,0:T(8,128)(2,1)S(1)}, u32[]{:S(2)}, u32[]{:S(2)}) async-start(bf16[16,64,256]{2,1,0:T(8,128)(2,1)} %get-tuple-element.230), calls=%async_computation.2 | async-start | bytes 1048576 | tf_op jit(solution)/shard_map/all_to_all | solution.py:1122
  225.5 46.7 %collective-permute-start.6 = (bf16[4,96,768]{2,1,0:T(8,128)(2,1)}, bf16[4,96,768]{2,1,0:T(8,128)(2,1)S(1)}, u32[]{:S(2)}, u32[]{:S(2)}) collective-permute-start(bf16[4,96,768]{2,1,0:T(8,128)(2,1)} %get-tuple-element.210), channel_id=1, source_target_pairs={{0,2},{2,0},{4,6},{6,4},{8,10},{10,8},{12,14},{14,12},{16,18},{18,... | collective-permute-start | bytes 1769480 | tf_op jit(solution)/shard_map/ppermute | solution.py:1066
  227.4 44.8 %collective-permute-start.7 = (bf16[4,96,768]{2,1,0:T(8,128)(2,1)}, bf16[4,96,768]{2,1,0:T(8,128)(2,1)S(1)}, u32[]{:S(2)}, u32[]{:S(2)}) collective-permute-start(bf16[4,96,768]{2,1,0:T(8,128)(2,1)} %get-tuple-element.211), channel_id=1, source_target_pairs={{0,4},{2,6},{4,0},{6,2},{8,12},{10,14},{12,8},{14,10},{16,20},{18,... | collective-permute-start | bytes 1769480 | tf_op jit(solution)/shard_map/ppermute | solution.py:1066
  228.9 43.3 %collective-permute-start.8 = (bf16[4,96,768]{2,1,0:T(8,128)(2,1)}, bf16[4,96,768]{2,1,0:T(8,128)(2,1)S(1)}, u32[]{:S(2)}, u32[]{:S(2)}) collective-permute-start(bf16[4,96,768]{2,1,0:T(8,128)(2,1)} %get-tuple-element.212), channel_id=1, source_target_pairs={{0,6},{2,4},{4,2},{6,0},{8,14},{10,12},{12,10},{14,8},{16,22},{18,... | collective-permute-start | bytes 1769480 | tf_op jit(solution)/shard_map/ppermute | solution.py:1066
  273.2 14.3 %collective-permute-start.10 = (bf16[96,768]{1,0:T(8,128)(2,1)S(1)}, bf16[96,768]{1,0:T(8,128)(2,1)}, u32[]{:S(2)}, u32[]{:S(2)}) collective-permute-start(bf16[96,768]{1,0:T(8,128)(2,1)S(1)} %get-tuple-element.245), channel_id=1, source_target_pairs={{0,16},{2,18},{4,20},{6,22},{8,24},{10,26},{12,28},{14,30},{16,0},... | collective-permute-start | bytes 442376 | tf_op jit(solution)/shard_map/ppermute | solution.py:1066
  276.6 45.6 %collective-permute-start.11 = (bf16[96,768]{1,0:T(8,128)(2,1)}, bf16[96,768]{1,0:T(8,128)(2,1)}, u32[]{:S(2)}, u32[]{:S(2)}) collective-permute-start(bf16[96,768]{1,0:T(8,128)(2,1)} %get-tuple-element.246), channel_id=1, source_target_pairs={{0,24},{2,26},{4,28},{6,30},{8,16},{10,18},{12,20},{14,22},{16,8},... | collective-permute-start | bytes 442376 | tf_op jit(solution)/shard_map/ppermute | solution.py:1066
  278.0 44.1 %collective-permute-start.9 = (bf16[96,768]{1,0:T(8,128)(2,1)S(1)}, bf16[96,768]{1,0:T(8,128)(2,1)}, u32[]{:S(2)}, u32[]{:S(2)}) collective-permute-start(bf16[96,768]{1,0:T(8,128)(2,1)S(1)} %get-tuple-element.244), channel_id=1, source_target_pairs={{0,8},{2,10},{4,12},{6,14},{8,0},{10,2},{12,4},{14,6},{16,24},{18,... | collective-permute-start | bytes 442376 | tf_op jit(solution)/shard_map/ppermute | solution.py:1066
  278.1 46.8 %all-to-all-start.3 = ((bf16[16,64,256]{2,1,0:T(8,128)(2,1)}), bf16[16,64,256]{2,1,0:T(8,128)(2,1)}, u32[]{:S(2)}, u32[]{:S(2)}) async-start(bf16[16,64,256]{2,1,0:T(8,128)(2,1)} %get-tuple-element.252), calls=%async_computation.3 | async-start | bytes 1048576 | tf_op jit(solution)/shard_map/all_to_all | solution.py:1122
  284.2 37.9 %collective-permute-start.12 = (bf16[4,128,768]{2,1,0:T(8,128)(2,1)}, bf16[4,128,768]{2,1,0:T(8,128)(2,1)S(1)}, u32[]{:S(2)}, u32[]{:S(2)}) collective-permute-start(bf16[4,128,768]{2,1,0:T(8,128)(2,1)} %get-tuple-element.248), channel_id=1, source_target_pairs={{0,2},{2,0},{4,6},{6,4},{8,10},{10,8},{12,14},{14,12},{16,18},{18,... | collective-permute-start | bytes 2359304 | tf_op jit(solution)/shard_map/ppermute | solution.py:1066
  286.1 37.8 %collective-permute-start.13 = (bf16[4,128,768]{2,1,0:T(8,128)(2,1)}, bf16[4,128,768]{2,1,0:T(8,128)(2,1)S(1)}, u32[]{:S(2)}, u32[]{:S(2)}) collective-permute-start(bf16[4,128,768]{2,1,0:T(8,128)(2,1)} %get-tuple-element.249), channel_id=1, source_target_pairs={{0,4},{2,6},{4,0},{6,2},{8,12},{10,14},{12,8},{14,10},{16,20},{18,... | collective-permute-start | bytes 2359304 | tf_op jit(solution)/shard_map/ppermute | solution.py:1066
  287.6 37.4 %collective-permute-start.14 = (bf16[4,128,768]{2,1,0:T(8,128)(2,1)}, bf16[4,128,768]{2,1,0:T(8,128)(2,1)S(1)}, u32[]{:S(2)}, u32[]{:S(2)}) collective-permute-start(bf16[4,128,768]{2,1,0:T(8,128)(2,1)} %get-tuple-element.250), channel_id=1, source_target_pairs={{0,6},{2,4},{4,2},{6,0},{8,14},{10,12},{12,10},{14,8},{16,22},{18,... | collective-permute-start | bytes 2359304 | tf_op jit(solution)/shard_map/ppermute | solution.py:1066
  328.4 14.3 %collective-permute-start.15 = (bf16[96,768]{1,0:T(8,128)(2,1)S(1)}, bf16[96,768]{1,0:T(8,128)(2,1)S(1)}, u32[]{:S(2)}, u32[]{:S(2)}) collective-permute-start(bf16[96,768]{1,0:T(8,128)(2,1)S(1)} %add_convert_fusion.4), channel_id=1, source_target_pairs={{0,8},{2,10},{4,12},{6,14},{8,0},{10,2},{12,4},{14,6},{16,24},{18,... | collective-permute-start | bytes 442376 | tf_op jit(solution)/shard_map/ppermute | solution.py:1066
  330.0 20.1 %collective-permute-start.16 = (bf16[96,768]{1,0:T(8,128)(2,1)S(1)}, bf16[96,768]{1,0:T(8,128)(2,1)S(1)}, u32[]{:S(2)}, u32[]{:S(2)}) collective-permute-start(bf16[96,768]{1,0:T(8,128)(2,1)S(1)} %add_convert_fusion.4), channel_id=1, source_target_pairs={{0,16},{2,18},{4,20},{6,22},{8,24},{10,26},{12,28},{14,30},{16,0},... | collective-permute-start | bytes 442376 | tf_op jit(solution)/shard_map/ppermute | solution.py:1066
  332.3 17.7 %collective-permute-start.17 = (bf16[96,768]{1,0:T(8,128)(2,1)S(1)}, bf16[96,768]{1,0:T(8,128)(2,1)S(1)}, u32[]{:S(2)}, u32[]{:S(2)}) collective-permute-start(bf16[96,768]{1,0:T(8,128)(2,1)S(1)} %add_convert_fusion.4), channel_id=1, source_target_pairs={{0,24},{2,26},{4,28},{6,30},{8,16},{10,18},{12,20},{14,22},{16,8},... | collective-permute-start | bytes 442376 | tf_op jit(solution)/shard_map/ppermute | solution.py:1066
  333.0 43.5 %all-to-all-start.4 = ((bf16[16,128,256]{2,1,0:T(8,128)(2,1)}), bf16[16,128,256]{2,1,0:T(8,128)(2,1)S(1)}, u32[]{:S(2)}, u32[]{:S(2)}) async-start(bf16[16,128,256]{2,1,0:T(8,128)(2,1)} %pad_maximum_fusion.2), calls=%async_computation.4 | async-start | bytes 2097152 | tf_op jit(solution)/shard_map/all_to_all | solution.py:1122
  338.7 58.0 %collective-permute-start.35 = (bf16[128,768]{1,0:T(8,128)(2,1)}, bf16[128,768]{1,0:T(8,128)(2,1)}, u32[]{:S(2)}, u32[]{:S(2)}) collective-permute-start(bf16[128,768]{1,0:T(8,128)(2,1)} %get-tuple-element.300), channel_id=1, source_target_pairs={{0,8},{2,10},{4,12},{6,14},{8,0},{10,2},{12,4},{14,6},{16,24},{18,... | collective-permute-start | bytes 589832 | tf_op jit(solution)/shard_map/ppermute | solution.py:1066
  340.4 56.3 %collective-permute-start.36 = (bf16[128,768]{1,0:T(8,128)(2,1)}, bf16[128,768]{1,0:T(8,128)(2,1)}, u32[]{:S(2)}, u32[]{:S(2)}) collective-permute-start(bf16[128,768]{1,0:T(8,128)(2,1)} %get-tuple-element.301), channel_id=1, source_target_pairs={{0,16},{2,18},{4,20},{6,22},{8,24},{10,26},{12,28},{14,30},{16,0},... | collective-permute-start | bytes 589832 | tf_op jit(solution)/shard_map/ppermute | solution.py:1066
  342.8 54.0 %collective-permute-start.37 = (bf16[128,768]{1,0:T(8,128)(2,1)}, bf16[128,768]{1,0:T(8,128)(2,1)}, u32[]{:S(2)}, u32[]{:S(2)}) collective-permute-start(bf16[128,768]{1,0:T(8,128)(2,1)} %get-tuple-element.302), channel_id=1, source_target_pairs={{0,24},{2,26},{4,28},{6,30},{8,16},{10,18},{12,20},{14,22},{16,8},... | collective-permute-start | bytes 589832 | tf_op jit(solution)/shard_map/ppermute | solution.py:1066
  350.2 26.3 %collective-permute-start.18 = (bf16[2,96,768]{2,1,0:T(8,128)(2,1)S(1)}, bf16[2,96,768]{2,1,0:T(8,128)(2,1)S(1)}, u32[]{:S(2)}, u32[]{:S(2)}) collective-permute-start(bf16[2,96,768]{2,1,0:T(8,128)(2,1)S(1)} %get-tuple-element.338), channel_id=1, source_target_pairs={{0,2},{2,0},{4,6},{6,4},{8,10},{10,8},{12,14},{14,12},{16,18},{18,... | collective-permute-start | bytes 884744 | tf_op jit(solution)/shard_map/ppermute | solution.py:930
  351.8 24.8 %collective-permute-start.19 = (bf16[2,96,768]{2,1,0:T(8,128)(2,1)S(1)}, bf16[2,96,768]{2,1,0:T(8,128)(2,1)S(1)}, u32[]{:S(2)}, u32[]{:S(2)}) collective-permute-start(bf16[2,96,768]{2,1,0:T(8,128)(2,1)S(1)} %get-tuple-element.337), channel_id=1, source_target_pairs={{0,4},{2,6},{4,0},{6,2},{8,12},{10,14},{12,8},{14,10},{16,20},{18,... | collective-permute-start | bytes 884744 | tf_op jit(solution)/shard_map/ppermute | solution.py:930
  377.7 19.0 %collective-permute-start.21 = (bf16[4,96,768]{2,1,0:T(8,128)(2,1)}, bf16[4,96,768]{2,1,0:T(8,128)(2,1)}, u32[]{:S(2)}, u32[]{:S(2)}) collective-permute-start(bf16[4,96,768]{2,1,0:T(8,128)(2,1)} %pad_maximum_fusion.9), channel_id=1, source_target_pairs={{0,2},{2,0},{4,6},{6,4},{8,10},{10,8},{12,14},{14,12},{16,18},{18,... | collective-permute-start | bytes 1769480 | tf_op jit(solution)/shard_map/ppermute | solution.py:930
  379.1 17.6 %collective-permute-start.20 = (bf16[4,96,768]{2,1,0:T(8,128)(2,1)}, bf16[4,96,768]{2,1,0:T(8,128)(2,1)}, u32[]{:S(2)}, u32[]{:S(2)}) collective-permute-start(bf16[4,96,768]{2,1,0:T(8,128)(2,1)} %pad_maximum_fusion.8), channel_id=1, source_target_pairs={{0,4},{2,6},{4,0},{6,2},{8,12},{10,14},{12,8},{14,10},{16,20},{18,... | collective-permute-start | bytes 1769480 | tf_op jit(solution)/shard_map/ppermute | solution.py:930
  398.1 31.7 %collective-permute-start.38 = (bf16[128,768]{1,0:T(8,128)(2,1)S(1)}, bf16[128,768]{1,0:T(8,128)(2,1)S(1)}, u32[]{:S(2)}, u32[]{:S(2)}) collective-permute-start(bf16[128,768]{1,0:T(8,128)(2,1)S(1)} %fusion.11), channel_id=1, source_target_pairs={{0,8},{2,10},{4,12},{6,14},{8,0},{10,2},{12,4},{14,6},{16,24},{18,... | collective-permute-start | bytes 589832 | tf_op jit(solution)/shard_map/ppermute | solution.py:1066
  402.4 37.1 %collective-permute-start.39 = (bf16[128,768]{1,0:T(8,128)(2,1)S(1)}, bf16[128,768]{1,0:T(8,128)(2,1)S(1)}, u32[]{:S(2)}, u32[]{:S(2)}) collective-permute-start(bf16[128,768]{1,0:T(8,128)(2,1)S(1)} %fusion.11), channel_id=1, source_target_pairs={{0,16},{2,18},{4,20},{6,22},{8,24},{10,26},{12,28},{14,30},{16,0},... | collective-permute-start | bytes 589832 | tf_op jit(solution)/shard_map/ppermute | solution.py:1066
  408.0 8.4 %collective-permute-start.23 = (bf16[192,1152]{1,0:T(8,128)(2,1)S(1)}, bf16[192,1152]{1,0:T(8,128)(2,1)S(1)}, u32[]{:S(2)}, u32[]{:S(2)}) collective-permute-start(bf16[192,1152]{1,0:T(8,128)(2,1)S(1)} %get-tuple-element.296), channel_id=1, source_target_pairs={{0,2},{2,0},{4,6},{6,4},{8,10},{10,8},{12,14},{14,12},{16,18},{18,... | collective-permute-start | bytes 1327112 | tf_op jit(solution)/shard_map/ppermute | solution.py:1066
  409.6 12.7 %collective-permute-start.24 = (bf16[192,1152]{1,0:T(8,128)(2,1)S(1)}, bf16[192,1152]{1,0:T(8,128)(2,1)S(1)}, u32[]{:S(2)}, u32[]{:S(2)}) collective-permute-start(bf16[192,1152]{1,0:T(8,128)(2,1)S(1)} %get-tuple-element.297), channel_id=1, source_target_pairs={{0,4},{2,6},{4,0},{6,2},{8,12},{10,14},{12,8},{14,10},{16,20},{18,... | collective-permute-start | bytes 1327112 | tf_op jit(solution)/shard_map/ppermute | solution.py:1066
  411.7 14.5 %collective-permute-start.25 = (bf16[192,1152]{1,0:T(8,128)(2,1)S(1)}, bf16[192,1152]{1,0:T(8,128)(2,1)S(1)}, u32[]{:S(2)}, u32[]{:S(2)}) collective-permute-start(bf16[192,1152]{1,0:T(8,128)(2,1)S(1)} %get-tuple-element.298), channel_id=1, source_target_pairs={{0,6},{2,4},{4,2},{6,0},{8,14},{10,12},{12,10},{14,8},{16,22},{18,... | collective-permute-start | bytes 1327112 | tf_op jit(solution)/shard_map/ppermute | solution.py:1066
  416.4 24.6 %collective-permute-start.40 = (bf16[128,768]{1,0:T(8,128)(2,1)S(1)}, bf16[128,768]{1,0:T(8,128)(2,1)S(1)}, u32[]{:S(2)}, u32[]{:S(2)}) collective-permute-start(bf16[128,768]{1,0:T(8,128)(2,1)S(1)} %fusion.11), channel_id=1, source_target_pairs={{0,24},{2,26},{4,28},{6,30},{8,16},{10,18},{12,20},{14,22},{16,8},... | collective-permute-start | bytes 589832 | tf_op jit(solution)/shard_map/ppermute | solution.py:1066
  426.5 5.6 %collective-permute-start.26 = (bf16[48,1152]{1,0:T(8,128)(2,1)S(1)}, bf16[48,1152]{1,0:T(8,128)(2,1)S(1)}, u32[]{:S(2)}, u32[]{:S(2)}) collective-permute-start(bf16[48,1152]{1,0:T(8,128)(2,1)S(1)} %get-tuple-element.347), channel_id=1, source_target_pairs={{0,8},{2,10},{4,12},{6,14},{8,0},{10,2},{12,4},{14,6},{16,24},{18,... | collective-permute-start | bytes 331784 | tf_op jit(solution)/shard_map/ppermute | solution.py:1066
  426.9 8.0 %collective-permute-start.27 = (bf16[48,1152]{1,0:T(8,128)(2,1)S(1)}, bf16[48,1152]{1,0:T(8,128)(2,1)S(1)}, u32[]{:S(2)}, u32[]{:S(2)}) collective-permute-start(bf16[48,1152]{1,0:T(8,128)(2,1)S(1)} %get-tuple-element.349), channel_id=1, source_target_pairs={{0,16},{2,18},{4,20},{6,22},{8,24},{10,26},{12,28},{14,30},{16,0},... | collective-permute-start | bytes 331784 | tf_op jit(solution)/shard_map/ppermute | solution.py:1066
  429.9 6.6 %collective-permute-start.28 = (bf16[48,1152]{1,0:T(8,128)(2,1)S(1)}, bf16[48,1152]{1,0:T(8,128)(2,1)S(1)}, u32[]{:S(2)}, u32[]{:S(2)}) collective-permute-start(bf16[48,1152]{1,0:T(8,128)(2,1)S(1)} %get-tuple-element.348), channel_id=1, source_target_pairs={{0,24},{2,26},{4,28},{6,30},{8,16},{10,18},{12,20},{14,22},{16,8},... | collective-permute-start | bytes 331784 | tf_op jit(solution)/shard_map/ppermute | solution.py:1066
  432.1 22.1 %collective-permute-start.41 = (bf16[2,128,768]{2,1,0:T(8,128)(2,1)}, bf16[2,128,768]{2,1,0:T(8,128)(2,1)}, u32[]{:S(2)}, u32[]{:S(2)}) collective-permute-start(bf16[2,128,768]{2,1,0:T(8,128)(2,1)} %pad_maximum_fusion.12), channel_id=1, source_target_pairs={{0,2},{2,0},{4,6},{6,4},{8,10},{10,8},{12,14},{14,12},{16,18},{18,... | collective-permute-start | bytes 1179656 | tf_op jit(solution)/shard_map/ppermute | solution.py:930
  436.5 5.6 %collective-permute-start.29 = (bf16[48,1152]{1,0:T(8,128)(2,1)S(1)}, bf16[48,1152]{1,0:T(8,128)(2,1)S(1)}, u32[]{:S(2)}, u32[]{:S(2)}) collective-permute-start(bf16[48,1152]{1,0:T(8,128)(2,1)S(1)} %fusion.9), channel_id=1, source_target_pairs={{0,8},{2,10},{4,12},{6,14},{8,0},{10,2},{12,4},{14,6},{16,24},{18,... | collective-permute-start | bytes 331784 | tf_op jit(solution)/shard_map/ppermute | solution.py:1066
  438.2 8.0 %collective-permute-start.30 = (bf16[48,1152]{1,0:T(8,128)(2,1)S(1)}, bf16[48,1152]{1,0:T(8,128)(2,1)S(1)}, u32[]{:S(2)}, u32[]{:S(2)}) collective-permute-start(bf16[48,1152]{1,0:T(8,128)(2,1)S(1)} %fusion.9), channel_id=1, source_target_pairs={{0,16},{2,18},{4,20},{6,22},{8,24},{10,26},{12,28},{14,30},{16,0},... | collective-permute-start | bytes 331784 | tf_op jit(solution)/shard_map/ppermute | solution.py:1066
  439.5 6.8 %collective-permute-start.31 = (bf16[48,1152]{1,0:T(8,128)(2,1)S(1)}, bf16[48,1152]{1,0:T(8,128)(2,1)S(1)}, u32[]{:S(2)}, u32[]{:S(2)}) collective-permute-start(bf16[48,1152]{1,0:T(8,128)(2,1)S(1)} %fusion.9), channel_id=1, source_target_pairs={{0,24},{2,26},{4,28},{6,30},{8,16},{10,18},{12,20},{14,22},{16,8},... | collective-permute-start | bytes 331784 | tf_op jit(solution)/shard_map/ppermute | solution.py:1066
  441.8 12.4 %collective-permute-start.42 = (bf16[2,128,768]{2,1,0:T(8,128)(2,1)}, bf16[2,128,768]{2,1,0:T(8,128)(2,1)}, u32[]{:S(2)}, u32[]{:S(2)}) collective-permute-start(bf16[2,128,768]{2,1,0:T(8,128)(2,1)} %pad_maximum_fusion.13), channel_id=1, source_target_pairs={{0,4},{2,6},{4,0},{6,2},{8,12},{10,14},{12,8},{14,10},{16,20},{18,... | collective-permute-start | bytes 1179656 | tf_op jit(solution)/shard_map/ppermute | solution.py:930
  446.5 10.5 %collective-permute-start.32 = (bf16[192,1152]{1,0:T(8,128)(2,1)S(1)}, bf16[192,1152]{1,0:T(8,128)(2,1)}, u32[]{:S(2)}, u32[]{:S(2)}) collective-permute-start(bf16[192,1152]{1,0:T(8,128)(2,1)S(1)} %bitcast.111), channel_id=1, source_target_pairs={{0,2},{2,0},{4,6},{6,4},{8,10},{10,8},{12,14},{14,12},{16,18},{18,... | collective-permute-start | bytes 1327112 | tf_op jit(solution)/shard_map/ppermute | solution.py:1066
  448.5 15.1 %collective-permute-start.33 = (bf16[192,1152]{1,0:T(8,128)(2,1)S(1)}, bf16[192,1152]{1,0:T(8,128)(2,1)}, u32[]{:S(2)}, u32[]{:S(2)}) collective-permute-start(bf16[192,1152]{1,0:T(8,128)(2,1)S(1)} %bitcast.112), channel_id=1, source_target_pairs={{0,4},{2,6},{4,0},{6,2},{8,12},{10,14},{12,8},{14,10},{16,20},{18,... | collective-permute-start | bytes 1327112 | tf_op jit(solution)/shard_map/ppermute | solution.py:1066
  448.5 15.1 %collective-permute-start.34 = (bf16[192,1152]{1,0:T(8,128)(2,1)S(1)}, bf16[192,1152]{1,0:T(8,128)(2,1)}, u32[]{:S(2)}, u32[]{:S(2)}) collective-permute-start(bf16[192,1152]{1,0:T(8,128)(2,1)S(1)} %bitcast.113), channel_id=1, source_target_pairs={{0,6},{2,4},{4,2},{6,0},{8,14},{10,12},{12,10},{14,8},{16,22},{18,... | collective-permute-start | bytes 1327112 | tf_op jit(solution)/shard_map/ppermute | solution.py:1066
  454.2 33.9 %collective-permute-start.22 = (bf16[1536,768]{1,0:T(8,128)(2,1)S(1)}, bf16[1536,768]{1,0:T(8,128)(2,1)}, u32[]{:S(2)}, u32[]{:S(2)}) collective-permute-start(bf16[1536,768]{1,0:T(8,128)(2,1)S(1)} %convolution_convert_fusion), channel_id=1, source_target_pairs={{0,1},{1,0},{2,3},{3,2},{4,5},{5,4},{6,7},{7,6},{8,9},{9,8},{10,11... | collective-permute-start | bytes 7077896 | tf_op jit(solution)/shard_map/ppermute | solution.py:1039
  456.4 22.0 %collective-permute-start.43 = (bf16[4,128,768]{2,1,0:T(8,128)(2,1)S(1)}, bf16[4,128,768]{2,1,0:T(8,128)(2,1)S(1)}, u32[]{:S(2)}, u32[]{:S(2)}) collective-permute-start(bf16[4,128,768]{2,1,0:T(8,128)(2,1)S(1)} %get-tuple-element.352), channel_id=1, source_target_pairs={{0,4},{2,6},{4,0},{6,2},{8,12},{10,14},{12,8},{14,10},{16,20},{18,... | collective-permute-start | bytes 2359304 | tf_op jit(solution)/shard_map/ppermute | solution.py:930
  457.0 21.5 %collective-permute-start.44 = (bf16[4,128,768]{2,1,0:T(8,128)(2,1)S(1)}, bf16[4,128,768]{2,1,0:T(8,128)(2,1)S(1)}, u32[]{:S(2)}, u32[]{:S(2)}) collective-permute-start(bf16[4,128,768]{2,1,0:T(8,128)(2,1)S(1)} %get-tuple-element.350), channel_id=1, source_target_pairs={{0,2},{2,0},{4,6},{6,4},{8,10},{10,8},{12,14},{14,12},{16,18},{18,... | collective-permute-start | bytes 2359304 | tf_op jit(solution)/shard_map/ppermute | solution.py:930
  (41 other events, 559.2 us)

commit v3 on v2

--- a/solution.py
+++ b/solution.py
@@ -1154,13 +1154,13 @@
 
     long_moved = exchange(long_send)
     short_att, short_w, short_s = short_forward(reach, ids_row, ids_col, short_pack, lines)
-    mixed, short_proj = project_out_short(short_att, out_weight, row_total)
-    long_moved, short_proj = after(long_moved, short_proj)
+    long_moved, short_att = after(long_moved, short_att)
     long_pack = by_position(long_moved, 3)
     long_att, long_w, long_s = long_forward(long_pack[0], long_pack[1], long_pack[2], long_line)
 
-    long_att, short_proj = after(long_att, short_proj)
+    long_att, short_att = after(long_att, short_att)
     long_att = exchange(long_att)
+    mixed, short_proj = project_out_short(short_att, out_weight, row_total)
     *forward, short_ffn = feed_forward(
         ITEMS, tokens, short_proj, other_half(short_proj), gain_one, bias_one, inner_weight,
         outer_weight,

time: 503 us -> 502 us (level)
  starting transfers between devices: 103 us -> 94.7 us
  waiting for transfers between devices: 46.7 us -> 52.2 us
    ppermute x8, starting transfers between devices: 15.3 us -> 10 us  [across(): return lax.ppermute(array, 'seq', [(i, i ^ mask) for i in range(peers)])]
  transfers between devices with their start and end apart: 50 -> 50, of which waited for: 15 -> 14; matrix products, arithmetic and copies ran while one was open for 7% -> 7% of each run, Pallas kernels for 37% -> 36%
where the time goes in v3:
time: 502 us; the launch traced here: 493 us
  Pallas kernels  288 us (57%)
  starting transfers between devices  94.7 us (19%)
  waiting for transfers between devices  52.2 us (10%)
  local copies, waits for them, and re-layouts  23.9 us (5%)
  other arithmetic  23 us (5%)
  matrix products  9.22 us (2%)
    pallas_call x1, Pallas kernels, long_forward(): pl.pallas_call(body, grid=(blocks,), in_specs=[pl.BlockSpec((head_dim, PI...  71.2 us
    ppermute x30, starting transfers between devices, terms_sent(): lax.ppermute(term, 'seq', [(i, i ^ away << bits[0]) for i in range(peers)])  43.8 us
    all_to_all x5, starting transfers between devices, exchange(): return lax.all_to_all(pieces, 'seq', 0, 0, axis_index_groups=groups)  39.5 us
    ppermute x30, waiting for transfers between devices, terms_sent(): lax.ppermute(term, 'seq', [(i, i ^ away << bits[0]) for i in range(peers)])  32.9 us
    pallas_call x1, Pallas kernels, long_back_pairs(): pl.pallas_call(body, grid=(blocks,), in_specs=[piece, whole, whole, piece...  32.2 us
    pallas_call x1, Pallas kernels, short_forward(): pl.pallas_call(body, grid=(blocks,), in_specs=[pl.BlockSpec(memory_space=...  26.4 us
    pallas_call x1, Pallas kernels, short_backward(): pl.pallas_call(body, grid=(blocks,), in_specs=[pl.BlockSpec(memory_space=...  24.7 us
    pallas_call x2, Pallas kernels, feed_forward(): pl.pallas_call(body, grid=(count,), in_specs=[rows, own_rows, own_rows, l...  24 us
  transfers between devices with their start and end apart: 50, of which 14 were waited for; matrix products, arithmetic and copies ran while one was open for 7% of the time, Pallas kernels for 36%

profile of v3, /device:TPU:0, one launch (start us, length us, event | category | flops | bytes accessed | tf_op | source)
XLA Modules:
  0.0 492.8 jit_solution(3236888832893267051)
XLA Ops:
  0.6 9.9 %shard_map.237 = (bf16[16,192,256]{2,1,0:T(8,128)(2,1)}, bf16[3,6,64,1024]{3,2,1,0:T(8,128)(2,1)}, f32[2,6,64,1536]{3,2,1,0:T(8,128)}, f32[2,6,1,1536]{3,2,1,0:T(1,128)}) custom-call(bf16[1536,768]{1,0:T(8,128)(2,1)} %t_ref.5, bf16[768,384]{1,0:T(8,128)(2,1)} %wq_ref.1, bf16[768,384]{1,0:T(8,128)(2,1)} %wk_ref.1, bf16[768,384]{1,0:T(8,128)(2,1)} %wv_ref.1), custom_call_target="tpu_custom_call" | custom-call | flops 11500000256 | tf_op jit(solution)/shard_map/pallas_call | solution.py:473
  10.6 8.4 %all-to-all-start = ((bf16[16,192,256]{2,1,0:T(8,128)(2,1)}), bf16[16,192,256]{2,1,0:T(8,128)(2,1)S(1)}, u32[]{:S(2)}, u32[]{:S(2)}) async-start(bf16[16,192,256]{2,1,0:T(8,128)(2,1)} %get-tuple-element.162), calls=%async_computation | async-start | bytes 3145728 | tf_op jit(solution)/shard_map/all_to_all | solution.py:1122
  22.8 26.4 %shard_map.238 = (bf16[6,64,1024]{2,1,0:T(8,128)(2,1)}, bf16[4,6,1024,256]{3,2,1,0:T(8,128)(2,1)}, bf16[4,6,1024,256]{3,2,1,0:T(8,128)(2,1)}) custom-call(s32[2,4]{1,0:T(2,128)} %pad_add_fusion.reach_ref, s32[1,1024]{1,0:T(1,128)} %bitcast.135, s32[1088,1]{1,0:T(8,128)} %broadcast_in_dim.117.col_ref, ...), custom_call_target="tpu_custom_call" | custom-call | flops 32199999488 | tf_op jit(solution)/shard_map/pallas_call | solution.py:325
  49.1 4.1 all-to-all-done
  55.9 71.2 %shard_map.239 = (bf16[16,64,256]{2,1,0:T(8,128)(2,1)}, bf16[16,4096,256]{2,1,0:T(8,128)(2,1)}, bf16[16,4096,256]{2,1,0:T(8,128)(2,1)}) custom-call(bf16[64,4096]{1,0:T(8,128)(2,1)} %bitcast.124, bf16[64,4096]{1,0:T(8,128)(2,1)} %bitcast.126, bf16[64,4096]{1,0:T(8,128)(2,1)} %bitcast.102, f32[1,640]{1,0:T(1,128)} %pad_dynamic-slice_fusion.line_ref), custom_call_target="tpu_custom_call" | custom-call | flops 80499998720 | tf_op jit(solution)/shard_map/pallas_call | solution.py:154
  127.1 3.4 shard_map.240
  131.6 12.7 %all-to-all-start.1 = ((bf16[16,64,256]{2,1,0:T(8,128)(2,1)}), bf16[16,64,256]{2,1,0:T(8,128)(2,1)S(1)}, u32[]{:S(2)}, u32[]{:S(2)}) async-start(bf16[16,64,256]{2,1,0:T(8,128)(2,1)} %get-tuple-element.168), calls=%async_computation.1 | async-start | bytes 1048576 | tf_op jit(solution)/shard_map/all_to_all | solution.py:1122
  145.4 14.6 %shard_map.241 = (f32[1536,768]{1,0:T(8,128)}, f32[1536,1]{1,0:T(8,128)}, bf16[1536,768]{1,0:T(8,128)(2,1)}, bf16[1536,1536]{1,0:T(8,128)(2,1)}, bf16[1536,1536]{1,0:T(8,128)(2,1)}, /*index=5*/bf16[1024,768]{1,0:T(8,128)(2,1)}) custom-call(bf16[1536,768]{1,0:T(8,128)(2,1)} %t_ref.5, bf16[1024,768]{1,0:T(8,128)(2,1)} %get-tuple-element.170.own_ref, ...), custom_call_target="tpu_custom_call" | custom-call | flops 13799999488 | tf_op jit(solution)/shard_map/pallas_call | solution.py:598
  160.8 3.0 shard_map.242
  164.1 2.3 collective-permute-done.1.other_ref
  167.2 9.4 %shard_map.243 = (f32[1536,768]{1,0:T(8,128)}, f32[1536,1]{1,0:T(8,128)}, bf16[1536,768]{1,0:T(8,128)(2,1)}, bf16[1536,1536]{1,0:T(8,128)(2,1)}, bf16[1536,1536]{1,0:T(8,128)(2,1)}, /*index=5*/bf16[512,768]{1,0:T(8,128)(2,1)}) custom-call(bf16[1536,768]{1,0:T(8,128)(2,1)} %t_ref.5, ...), custom_call_target="tpu_custom_call", output_to_operand_aliasing={{0}: (7, {}), {1}: (8, {}), {2}: (9, {}), {3}: (10, {}), {4... | custom-call | flops 6899999744 | tf_op jit(solution)/shard_map/pallas_call | solution.py:598
  180.0 8.7 %shard_map.244 = (bf16[1536,768]{1,0:T(8,128)(2,1)}, f32[1536,768]{1,0:T(8,128)}, bf16[1536,768]{1,0:T(8,128)(2,1)}, bf16[1536,1536]{1,0:T(8,128)(2,1)}, bf16[51...) custom-call(f32[1536,768]{1,0:T(8,128)} %get-tuple-element.180.unit_ref, ...), custom_call_target="tpu_custom_call" | custom-call | flops 6899999744 | tf_op jit(solution)/shard_map/pallas_call | solution.py:664
  189.0 2.3 collective-permute-done.3.other_ref
  192.2 5.2 %shard_map.245 = (f32[1536,768]{1,0:T(8,128)}, bf16[1536,768]{1,0:T(8,128)(2,1)}, bf16[16,64,256]{2,1,0:T(8,128)(2,1)}, f32[1,768]{1,0:T(1,128)}, f32[1,768]{1,0:T(1,128)}) custom-call(f32[1536,768]{1,0:T(8,128)} %get-tuple-element.180.unit_ref, f32[1536,1]{1,0:T(8,128)} %get-tuple-element.181.inv_ref, f32[1536,768]{1,0:T(8,128)} %get-tuple-element.194.sum_ref.rest_1_, ...), custom_call_target="tpu_custom_call" | custom-call | flops 4600000000 | tf_op jit(solution)/shard_map/pallas_call | solution.py:739
  198.5 13.3 %shard_map.246 = (bf16[1536,768]{1,0:T(8,128)(2,1)}, f32[1536,768]{1,0:T(8,128)}, bf16[1536,768]{1,0:T(8,128)(2,1)}, bf16[1536,1536]{1,0:T(8,128)(2,1)}, bf16[10...) custom-call(f32[1536,768]{1,0:T(8,128)} %get-tuple-element.180.unit_, ...), custom_call_target="tpu_custom_call", output_to_operand_aliasing={{0}: (11, {}), {1}: (12, {}), {2}: (13, {}), {3}: (14, {})} | custom-call | flops 13799999488 | tf_op jit(solution)/shard_map/pallas_call | solution.py:664
  212.1 8.2 %shard_map.248 = (bf16[4,96,768]{2,1,0:T(8,128)(2,1)}, bf16[4,96,768]{2,1,0:T(8,128)(2,1)}, bf16[4,96,768]{2,1,0:T(8,128)(2,1)}, bf16[4,96,768]{2,1,0:T(8,128)(2,1)}) custom-call(s32[1]{0:T(128)} %bitcast.8.mine_ref, bf16[1536,1536]{1,0:T(8,128)(2,1)} %get-tuple-element.203.act_ref, bf16[1536,768]{1,0:T(8,128)(2,1)} %get-tuple-element.204.ffn_ref), custom_call_target="tpu_custom_call" | custom-call | flops 10350000128 | tf_op jit(solution)/shard_map/pallas_call | solution.py:772
  220.3 6.9 %all-to-all-start.2 = ((bf16[16,64,256]{2,1,0:T(8,128)(2,1)}), bf16[16,64,256]{2,1,0:T(8,128)(2,1)S(1)}, u32[]{:S(2)}, u32[]{:S(2)}) async-start(bf16[16,64,256]{2,1,0:T(8,128)(2,1)} %get-tuple-element.230), calls=%async_computation.2 | async-start | bytes 1048576 | tf_op jit(solution)/shard_map/all_to_all | solution.py:1122
  227.3 1.9 collective-permute-start.6
  230.9 6.9 %shard_map.247 = (f32[1536,768]{1,0:T(8,128)}, bf16[1536,768]{1,0:T(8,128)(2,1)}, bf16[6,64,1024]{2,1,0:T(8,128)(2,1)}, f32[1,768]{1,0:T(1,128)}, f32[1,768]{1,0:T(1,128)}) custom-call(f32[1536,768]{1,0:T(8,128)} %get-tuple-element.180.unit_ref, f32[1536,1]{1,0:T(8,128)} %get-tuple-element.181.inv_ref, ...), custom_call_target="tpu_custom_call", output_to_operand_aliasing={{0}: (7, {}), {1}: (8, {})} | custom-call | flops 9200000000 | tf_op jit(solution)/shard_map/pallas_call | solution.py:739
  239.9 10.3 %shard_map.249 = (bf16[4,128,768]{2,1,0:T(8,128)(2,1)}, bf16[4,128,768]{2,1,0:T(8,128)(2,1)}, bf16[4,128,768]{2,1,0:T(8,128)(2,1)}, bf16[4,128,768]{2,1,0:T(8,128)(2,1)}) custom-call(s32[1]{0:T(128)} %bitcast.8.mine_ref, bf16[1536,768]{1,0:T(8,128)(2,1)} %get-tuple-element.214.low_ref, bf16[1536,1536]{1,0:T(8,128)(2,1)} %get-tuple-element.215.pre_ref, ...), custom_call_target="tpu_custom_call" | custom-call | flops 10350000128 | tf_op jit(solution)/shard_map/pallas_call | solution.py:772
  251.0 23.0 %shard_map.250 = (bf16[16,64,256]{2,1,0:T(8,128)(2,1)}, f32[1,640]{1,0:T(1,128)}) custom-call(bf16[64,4096]{1,0:T(8,128)(2,1)} %bitcast.103, bf16[64,4096]{1,0:T(8,128)(2,1)} %bitcast.105, bf16[16,4096,256]{2,1,0:T(8,128)(2,1)} %get-tuple-element.236.w_ref), custom_call_target="tpu_custom_call" | custom-call | flops 1150000000 | tf_op jit(solution)/shard_map/pallas_call | solution.py:200
  275.1 2.8 collective-permute-start.10
  280.0 6.1 %all-to-all-start.3 = ((bf16[16,64,256]{2,1,0:T(8,128)(2,1)}), bf16[16,64,256]{2,1,0:T(8,128)(2,1)}, u32[]{:S(2)}, u32[]{:S(2)}) async-start(bf16[16,64,256]{2,1,0:T(8,128)(2,1)} %get-tuple-element.252), calls=%async_computation.3 | async-start | bytes 1048576 | tf_op jit(solution)/shard_map/all_to_all | solution.py:1122
  286.1 1.9 collective-permute-start.12
  290.9 32.2 %shard_map.251 = (bf16[16,64,256]{2,1,0:T(8,128)(2,1)}, bf16[16,64,256]{2,1,0:T(8,128)(2,1)}) custom-call(bf16[64,4096]{1,0:T(8,128)(2,1)} %bitcast.125, bf16[64,4096]{1,0:T(8,128)(2,1)} %bitcast.127, bf16[64,4096]{1,0:T(8,128)(2,1)} %bitcast.104, bf16[64,4096]{1,0:T(8,128)(2,1)} %bitcast.106, bf16[16,4096,256]{2,1,0:T(8,128)(2,1)} %get-tuple-element.254.s_ref), custom_call_target="tpu_custom_call" | custom-call | flops 46000001024 | tf_op jit(solution)/shard_map/pallas_call | solution.py:258
  331.7 2.4 collective-permute-start.16
  334.8 5.4 %all-to-all-start.4 = ((bf16[16,128,256]{2,1,0:T(8,128)(2,1)}), bf16[16,128,256]{2,1,0:T(8,128)(2,1)S(1)}, u32[]{:S(2)}, u32[]{:S(2)}) async-start(bf16[16,128,256]{2,1,0:T(8,128)(2,1)} %pad_maximum_fusion.2), calls=%async_computation.4 | async-start | bytes 2097152 | tf_op jit(solution)/shard_map/all_to_all | solution.py:1122
  340.3 1.9 collective-permute-start.35
  342.2 2.4 collective-permute-start.36
  344.7 7.1 %collective-permute-done.16 = bf16[96,768]{1,0:T(8,128)(2,1)S(1)} collective-permute-done((bf16[96,768]{1,0:T(8,128)(2,1)S(1)}, bf16[96,768]{1,0:T(8,128)(2,1)S(1)}, u32[]{:S(2)}, u32[]{:S(2)}) %collective-permute-start.16) | collective-permute-done | bytes 147488 | tf_op jit(solution)/shard_map/ppermute | solution.py:1066
  353.6 24.7 %shard_map.252 = (f32[6,64,1024]{2,1,0:T(8,128)}, f32[6,64,1024]{2,1,0:T(8,128)}, f32[6,64,1024]{2,1,0:T(8,128)}, f32[6,1,640]{2,1,0:T(1,128)}) custom-call(s32[2,4]{1,0:T(2,128)} %pad_add_fusion.reach_ref, s32[1,1024]{1,0:T(1,128)} %bitcast.136, s32[1088,1]{1,0:T(8,128)} %broadcast_in_dim.117.col_ref, ...), custom_call_target="tpu_custom_call" | custom-call | flops 32199999488 | tf_op jit(solution)/shard_map/pallas_call | solution.py:400
  380.9 2.0 collective-permute-start.20
  383.0 8.4 %shard_map.253 = bf16[1152,1536]{1,0:T(8,128)(2,1)} custom-call(bf16[16,128,256]{2,1,0:T(8,128)(2,1)} %copy-done.2, bf16[16,64,256]{2,1,0:T(8,128)(2,1)} %all-to-all-done.3.refs_1_, f32[6,64,1024]{2,1,0:T(8,128)} %get-tuple-element.283.refs_2_, f32[6,64,1024]{2,1,0:T(8,128)} %get-tuple-element.284.refs_3_, f32[6,64,1024]{2,1,0:T(8,128)} %get-tuple-element.285.refs_4_, ...), custom_call_target="tpu_custom_call" | custom-call | flops 9200000000 | tf_op jit(solution)/shard_map/pallas_call | solution.py:1018
  393.7 4.3 collective-permute-start.38
  398.1 5.4 %convolution_convert_fusion.1 = bf16[1152,768]{0,1:T(8,128)(2,1)S(1)} fusion(bf16[1152,1536]{1,0:T(8,128)(2,1)} %shard_map.253, bf16[1536,768]{1,0:T(8,128)(2,1)S(1)} %copy-done.1), kind=kOutput, calls=%fused_computation.2 | convolution fusion | flops 2718793728 | bytes 7667712 | tf_op jit(solution)/shard_map/dot_general | solution.py:68
  407.3 3.8 convolution_convert_fusion
  411.1 2.5 collective-permute-done.23
  414.5 4.9 collective-permute-done.24
  426.7 5.1 %collective-permute-done.27 = bf16[48,1152]{1,0:T(8,128)(2,1)S(1)} collective-permute-done((bf16[48,1152]{1,0:T(8,128)(2,1)S(1)}, bf16[48,1152]{1,0:T(8,128)(2,1)S(1)}, u32[]{:S(2)}, u32[]{:S(2)}) %collective-permute-start.27) | collective-permute-done | bytes 110624 | tf_op jit(solution)/shard_map/ppermute | solution.py:1066
  431.9 3.0 collective-permute-start.29
  439.0 3.9 collective-permute-done.30
  446.7 4.1 shard_map.255
  450.9 2.2 pad_maximum_fusion.6
  454.6 1.9 collective-permute-start.44
  456.5 6.2 %collective-permute-done.33 = bf16[192,1152]{1,0:T(8,128)(2,1)} collective-permute-done((bf16[192,1152]{1,0:T(8,128)(2,1)S(1)}, bf16[192,1152]{1,0:T(8,128)(2,1)}, u32[]{:S(2)}, u32[]{:S(2)}) %collective-permute-start.33) | collective-permute-done | bytes 442400 | tf_op jit(solution)/shard_map/ppermute | solution.py:1066
  467.0 9.9 %collective-permute-done.43.refs_3_ = bf16[4,128,768]{2,1,0:T(8,128)(2,1)S(1)} collective-permute-done((bf16[4,128,768]{2,1,0:T(8,128)(2,1)S(1)}, bf16[4,128,768]{2,1,0:T(8,128)(2,1)S(1)}, u32[]{:S(2)}, u32[]{:S(2)}) %collective-permute-start.43) | collective-permute-done | bytes 786464 | tf_op jit(solution)/shard_map/ppermute | solution.py:930
  478.6 5.0 %shard_map.254 = (f32[768,1536]{1,0:T(8,128)}, f32[384,768]{1,0:T(8,128)}, f32[4,768]{1,0:T(4,128)}, f32[16,768]{1,0:T(8,128)}) custom-call(s32[2]{0:T(128)} %pad_add_fusion.2.mine_ref, bf16[4,128,768]{2,1,0:T(8,128)(2,1)} %get-tuple-element.351.refs_0_, bf16[2,128,768]{2,1,0:T(8,128)(2,1)} %collective-permute-done.41.refs_1_, ...), custom_call_target="tpu_custom_call" | custom-call | flops 4600000000 | tf_op jit(solution)/shard_map/pallas_call | solution.py:913
  486.5 5.9 %add_add_fusion = f32[1536,768]{1,0:T(8,128)} fusion(f32[1536,768]{1,0:T(8,128)} %get-tuple-element.202, bf16[1536,768]{1,0:T(8,128)(2,1)} %collective-permute-done.22, bf16[1536,768]{1,0:T(8,128)(2,1)S(1)} %convolution_convert_fusion), kind=kLoop, calls=%fused_computation | loop fusion | flops 4718592 | bytes 14155776 | tf_op jit(solution)/shard_map/add | solution.py:1302
  (229 shorter events, 73.6 us)
Async XLA Ops:
  10.6 42.6 %all-to-all-start = ((bf16[16,192,256]{2,1,0:T(8,128)(2,1)}), bf16[16,192,256]{2,1,0:T(8,128)(2,1)S(1)}, u32[]{:S(2)}, u32[]{:S(2)}) async-start(bf16[16,192,256]{2,1,0:T(8,128)(2,1)} %get-tuple-element.162), calls=%async_computation | async-start | bytes 3145728 | tf_op jit(solution)/shard_map/all_to_all | solution.py:1122
  130.4 13.8 %collective-permute-start = (bf16[1024,768]{1,0:T(8,128)(2,1)}, bf16[1024,768]{1,0:T(8,128)(2,1)S(1)}, u32[]{:S(2)}, u32[]{:S(2)}) collective-permute-start(bf16[1024,768]{1,0:T(8,128)(2,1)} %get-tuple-element.170.own_ref), channel_id=1, source_target_pairs={{0,1},{1,0},{2,3},{3,2},{4,5},{5,4},{6,7},{7,6},{8,9},{9,8},{10,11... | collective-permute-start | bytes 4718600 | tf_op jit(solution)/shard_map/ppermute | solution.py:1039
  131.6 28.4 %all-to-all-start.1 = ((bf16[16,64,256]{2,1,0:T(8,128)(2,1)}), bf16[16,64,256]{2,1,0:T(8,128)(2,1)S(1)}, u32[]{:S(2)}, u32[]{:S(2)}) async-start(bf16[16,64,256]{2,1,0:T(8,128)(2,1)} %get-tuple-element.168), calls=%async_computation.1 | async-start | bytes 1048576 | tf_op jit(solution)/shard_map/all_to_all | solution.py:1122
  178.1 19.3 %collective-permute-start.4 = (bf16[1024,768]{1,0:T(8,128)(2,1)S(1)}, bf16[1024,768]{1,0:T(8,128)(2,1)S(1)}, u32[]{:S(2)}, u32[]{:S(2)}) collective-permute-start(bf16[1024,768]{1,0:T(8,128)(2,1)S(1)} %copy-done.29), channel_id=1, source_target_pairs={{0,1},{1,0},{2,3},{3,2},{4,5},{5,4},{6,7},{7,6},{8,9},{9,8},{10,11... | collective-permute-start | bytes 4718600 | tf_op jit(solution)/shard_map/ppermute | solution.py:1039
  188.8 2.6 collective-permute-start.3
  211.8 19.1 %collective-permute-start.5 = (bf16[1024,768]{1,0:T(8,128)(2,1)}, bf16[1024,768]{1,0:T(8,128)(2,1)}, u32[]{:S(2)}, u32[]{:S(2)}) collective-permute-start(bf16[1024,768]{1,0:T(8,128)(2,1)} %get-tuple-element.199.own_ref), channel_id=1, source_target_pairs={{0,1},{1,0},{2,3},{3,2},{4,5},{5,4},{6,7},{7,6},{8,9},{9,8},{10,11... | collective-permute-start | bytes 4718600 | tf_op jit(solution)/shard_map/ppermute | solution.py:1039
  220.3 29.9 %all-to-all-start.2 = ((bf16[16,64,256]{2,1,0:T(8,128)(2,1)}), bf16[16,64,256]{2,1,0:T(8,128)(2,1)S(1)}, u32[]{:S(2)}, u32[]{:S(2)}) async-start(bf16[16,64,256]{2,1,0:T(8,128)(2,1)} %get-tuple-element.230), calls=%async_computation.2 | async-start | bytes 1048576 | tf_op jit(solution)/shard_map/all_to_all | solution.py:1122
  227.3 46.8 %collective-permute-start.6 = (bf16[4,96,768]{2,1,0:T(8,128)(2,1)}, bf16[4,96,768]{2,1,0:T(8,128)(2,1)S(1)}, u32[]{:S(2)}, u32[]{:S(2)}) collective-permute-start(bf16[4,96,768]{2,1,0:T(8,128)(2,1)} %get-tuple-element.210), channel_id=1, source_target_pairs={{0,2},{2,0},{4,6},{6,4},{8,10},{10,8},{12,14},{14,12},{16,18},{18,... | collective-permute-start | bytes 1769480 | tf_op jit(solution)/shard_map/ppermute | solution.py:1066
  229.2 44.8 %collective-permute-start.7 = (bf16[4,96,768]{2,1,0:T(8,128)(2,1)}, bf16[4,96,768]{2,1,0:T(8,128)(2,1)S(1)}, u32[]{:S(2)}, u32[]{:S(2)}) collective-permute-start(bf16[4,96,768]{2,1,0:T(8,128)(2,1)} %get-tuple-element.211), channel_id=1, source_target_pairs={{0,4},{2,6},{4,0},{6,2},{8,12},{10,14},{12,8},{14,10},{16,20},{18,... | collective-permute-start | bytes 1769480 | tf_op jit(solution)/shard_map/ppermute | solution.py:1066
  230.7 43.4 %collective-permute-start.8 = (bf16[4,96,768]{2,1,0:T(8,128)(2,1)}, bf16[4,96,768]{2,1,0:T(8,128)(2,1)S(1)}, u32[]{:S(2)}, u32[]{:S(2)}) collective-permute-start(bf16[4,96,768]{2,1,0:T(8,128)(2,1)} %get-tuple-element.212), channel_id=1, source_target_pairs={{0,6},{2,4},{4,2},{6,0},{8,14},{10,12},{12,10},{14,8},{16,22},{18,... | collective-permute-start | bytes 1769480 | tf_op jit(solution)/shard_map/ppermute | solution.py:1066
  275.1 14.3 %collective-permute-start.10 = (bf16[96,768]{1,0:T(8,128)(2,1)S(1)}, bf16[96,768]{1,0:T(8,128)(2,1)S(1)}, u32[]{:S(2)}, u32[]{:S(2)}) collective-permute-start(bf16[96,768]{1,0:T(8,128)(2,1)S(1)} %get-tuple-element.245), channel_id=1, source_target_pairs={{0,16},{2,18},{4,20},{6,22},{8,24},{10,26},{12,28},{14,30},{16,0},... | collective-permute-start | bytes 442376 | tf_op jit(solution)/shard_map/ppermute | solution.py:1066
  278.4 45.5 %collective-permute-start.11 = (bf16[96,768]{1,0:T(8,128)(2,1)}, bf16[96,768]{1,0:T(8,128)(2,1)}, u32[]{:S(2)}, u32[]{:S(2)}) collective-permute-start(bf16[96,768]{1,0:T(8,128)(2,1)} %get-tuple-element.246), channel_id=1, source_target_pairs={{0,24},{2,26},{4,28},{6,30},{8,16},{10,18},{12,20},{14,22},{16,8},... | collective-permute-start | bytes 442376 | tf_op jit(solution)/shard_map/ppermute | solution.py:1066
  279.9 44.0 %collective-permute-start.9 = (bf16[96,768]{1,0:T(8,128)(2,1)S(1)}, bf16[96,768]{1,0:T(8,128)(2,1)}, u32[]{:S(2)}, u32[]{:S(2)}) collective-permute-start(bf16[96,768]{1,0:T(8,128)(2,1)S(1)} %get-tuple-element.244), channel_id=1, source_target_pairs={{0,8},{2,10},{4,12},{6,14},{8,0},{10,2},{12,4},{14,6},{16,24},{18,... | collective-permute-start | bytes 442376 | tf_op jit(solution)/shard_map/ppermute | solution.py:1066
  280.0 46.8 %all-to-all-start.3 = ((bf16[16,64,256]{2,1,0:T(8,128)(2,1)}), bf16[16,64,256]{2,1,0:T(8,128)(2,1)}, u32[]{:S(2)}, u32[]{:S(2)}) async-start(bf16[16,64,256]{2,1,0:T(8,128)(2,1)} %get-tuple-element.252), calls=%async_computation.3 | async-start | bytes 1048576 | tf_op jit(solution)/shard_map/all_to_all | solution.py:1122
  286.1 37.8 %collective-permute-start.12 = (bf16[4,128,768]{2,1,0:T(8,128)(2,1)}, bf16[4,128,768]{2,1,0:T(8,128)(2,1)S(1)}, u32[]{:S(2)}, u32[]{:S(2)}) collective-permute-start(bf16[4,128,768]{2,1,0:T(8,128)(2,1)} %get-tuple-element.248), channel_id=1, source_target_pairs={{0,2},{2,0},{4,6},{6,4},{8,10},{10,8},{12,14},{14,12},{16,18},{18,... | collective-permute-start | bytes 2359304 | tf_op jit(solution)/shard_map/ppermute | solution.py:1066
  287.9 37.8 %collective-permute-start.13 = (bf16[4,128,768]{2,1,0:T(8,128)(2,1)}, bf16[4,128,768]{2,1,0:T(8,128)(2,1)S(1)}, u32[]{:S(2)}, u32[]{:S(2)}) collective-permute-start(bf16[4,128,768]{2,1,0:T(8,128)(2,1)} %get-tuple-element.249), channel_id=1, source_target_pairs={{0,4},{2,6},{4,0},{6,2},{8,12},{10,14},{12,8},{14,10},{16,20},{18,... | collective-permute-start | bytes 2359304 | tf_op jit(solution)/shard_map/ppermute | solution.py:1066
  289.4 37.4 %collective-permute-start.14 = (bf16[4,128,768]{2,1,0:T(8,128)(2,1)}, bf16[4,128,768]{2,1,0:T(8,128)(2,1)S(1)}, u32[]{:S(2)}, u32[]{:S(2)}) collective-permute-start(bf16[4,128,768]{2,1,0:T(8,128)(2,1)} %get-tuple-element.250), channel_id=1, source_target_pairs={{0,6},{2,4},{4,2},{6,0},{8,14},{10,12},{12,10},{14,8},{16,22},{18,... | collective-permute-start | bytes 2359304 | tf_op jit(solution)/shard_map/ppermute | solution.py:1066
  330.2 14.3 %collective-permute-start.15 = (bf16[96,768]{1,0:T(8,128)(2,1)S(1)}, bf16[96,768]{1,0:T(8,128)(2,1)S(1)}, u32[]{:S(2)}, u32[]{:S(2)}) collective-permute-start(bf16[96,768]{1,0:T(8,128)(2,1)S(1)} %add_convert_fusion.4), channel_id=1, source_target_pairs={{0,8},{2,10},{4,12},{6,14},{8,0},{10,2},{12,4},{14,6},{16,24},{18,... | collective-permute-start | bytes 442376 | tf_op jit(solution)/shard_map/ppermute | solution.py:1066
  331.7 20.1 %collective-permute-start.16 = (bf16[96,768]{1,0:T(8,128)(2,1)S(1)}, bf16[96,768]{1,0:T(8,128)(2,1)S(1)}, u32[]{:S(2)}, u32[]{:S(2)}) collective-permute-start(bf16[96,768]{1,0:T(8,128)(2,1)S(1)} %add_convert_fusion.4), channel_id=1, source_target_pairs={{0,16},{2,18},{4,20},{6,22},{8,24},{10,26},{12,28},{14,30},{16,0},... | collective-permute-start | bytes 442376 | tf_op jit(solution)/shard_map/ppermute | solution.py:1066
  334.1 17.7 %collective-permute-start.17 = (bf16[96,768]{1,0:T(8,128)(2,1)S(1)}, bf16[96,768]{1,0:T(8,128)(2,1)S(1)}, u32[]{:S(2)}, u32[]{:S(2)}) collective-permute-start(bf16[96,768]{1,0:T(8,128)(2,1)S(1)} %add_convert_fusion.4), channel_id=1, source_target_pairs={{0,24},{2,26},{4,28},{6,30},{8,16},{10,18},{12,20},{14,22},{16,8},... | collective-permute-start | bytes 442376 | tf_op jit(solution)/shard_map/ppermute | solution.py:1066
  334.8 43.5 %all-to-all-start.4 = ((bf16[16,128,256]{2,1,0:T(8,128)(2,1)}), bf16[16,128,256]{2,1,0:T(8,128)(2,1)S(1)}, u32[]{:S(2)}, u32[]{:S(2)}) async-start(bf16[16,128,256]{2,1,0:T(8,128)(2,1)} %pad_maximum_fusion.2), calls=%async_computation.4 | async-start | bytes 2097152 | tf_op jit(solution)/shard_map/all_to_all | solution.py:1122
  340.3 52.1 %collective-permute-start.35 = (bf16[128,768]{1,0:T(8,128)(2,1)}, bf16[128,768]{1,0:T(8,128)(2,1)}, u32[]{:S(2)}, u32[]{:S(2)}) collective-permute-start(bf16[128,768]{1,0:T(8,128)(2,1)} %get-tuple-element.300), channel_id=1, source_target_pairs={{0,8},{2,10},{4,12},{6,14},{8,0},{10,2},{12,4},{14,6},{16,24},{18,... | collective-permute-start | bytes 589832 | tf_op jit(solution)/shard_map/ppermute | solution.py:1066
  342.2 50.2 %collective-permute-start.36 = (bf16[128,768]{1,0:T(8,128)(2,1)}, bf16[128,768]{1,0:T(8,128)(2,1)}, u32[]{:S(2)}, u32[]{:S(2)}) collective-permute-start(bf16[128,768]{1,0:T(8,128)(2,1)} %get-tuple-element.301), channel_id=1, source_target_pairs={{0,16},{2,18},{4,20},{6,22},{8,24},{10,26},{12,28},{14,30},{16,0},... | collective-permute-start | bytes 589832 | tf_op jit(solution)/shard_map/ppermute | solution.py:1066
  344.6 47.8 %collective-permute-start.37 = (bf16[128,768]{1,0:T(8,128)(2,1)}, bf16[128,768]{1,0:T(8,128)(2,1)}, u32[]{:S(2)}, u32[]{:S(2)}) collective-permute-start(bf16[128,768]{1,0:T(8,128)(2,1)} %get-tuple-element.302), channel_id=1, source_target_pairs={{0,24},{2,26},{4,28},{6,30},{8,16},{10,18},{12,20},{14,22},{16,8},... | collective-permute-start | bytes 589832 | tf_op jit(solution)/shard_map/ppermute | solution.py:1066
  352.0 26.3 %collective-permute-start.18 = (bf16[2,96,768]{2,1,0:T(8,128)(2,1)S(1)}, bf16[2,96,768]{2,1,0:T(8,128)(2,1)S(1)}, u32[]{:S(2)}, u32[]{:S(2)}) collective-permute-start(bf16[2,96,768]{2,1,0:T(8,128)(2,1)S(1)} %get-tuple-element.338), channel_id=1, source_target_pairs={{0,2},{2,0},{4,6},{6,4},{8,10},{10,8},{12,14},{14,12},{16,18},{18,... | collective-permute-start | bytes 884744 | tf_op jit(solution)/shard_map/ppermute | solution.py:930
  353.6 24.8 %collective-permute-start.19 = (bf16[2,96,768]{2,1,0:T(8,128)(2,1)S(1)}, bf16[2,96,768]{2,1,0:T(8,128)(2,1)S(1)}, u32[]{:S(2)}, u32[]{:S(2)}) collective-permute-start(bf16[2,96,768]{2,1,0:T(8,128)(2,1)S(1)} %get-tuple-element.337), channel_id=1, source_target_pairs={{0,4},{2,6},{4,0},{6,2},{8,12},{10,14},{12,8},{14,10},{16,20},{18,... | collective-permute-start | bytes 884744 | tf_op jit(solution)/shard_map/ppermute | solution.py:930
  379.5 12.8 %collective-permute-start.21 = (bf16[4,96,768]{2,1,0:T(8,128)(2,1)}, bf16[4,96,768]{2,1,0:T(8,128)(2,1)}, u32[]{:S(2)}, u32[]{:S(2)}) collective-permute-start(bf16[4,96,768]{2,1,0:T(8,128)(2,1)} %pad_maximum_fusion.9), channel_id=1, source_target_pairs={{0,2},{2,0},{4,6},{6,4},{8,10},{10,8},{12,14},{14,12},{16,18},{18,... | collective-permute-start | bytes 1769480 | tf_op jit(solution)/shard_map/ppermute | solution.py:930
  380.9 11.4 %collective-permute-start.20 = (bf16[4,96,768]{2,1,0:T(8,128)(2,1)}, bf16[4,96,768]{2,1,0:T(8,128)(2,1)}, u32[]{:S(2)}, u32[]{:S(2)}) collective-permute-start(bf16[4,96,768]{2,1,0:T(8,128)(2,1)} %pad_maximum_fusion.8), channel_id=1, source_target_pairs={{0,4},{2,6},{4,0},{6,2},{8,12},{10,14},{12,8},{14,10},{16,20},{18,... | collective-permute-start | bytes 1769480 | tf_op jit(solution)/shard_map/ppermute | solution.py:930
  393.7 28.6 %collective-permute-start.38 = (bf16[128,768]{1,0:T(8,128)(2,1)S(1)}, bf16[128,768]{1,0:T(8,128)(2,1)S(1)}, u32[]{:S(2)}, u32[]{:S(2)}) collective-permute-start(bf16[128,768]{1,0:T(8,128)(2,1)S(1)} %fusion.11), channel_id=1, source_target_pairs={{0,8},{2,10},{4,12},{6,14},{8,0},{10,2},{12,4},{14,6},{16,24},{18,... | collective-permute-start | bytes 589832 | tf_op jit(solution)/shard_map/ppermute | solution.py:1066
  398.0 37.6 %collective-permute-start.39 = (bf16[128,768]{1,0:T(8,128)(2,1)S(1)}, bf16[128,768]{1,0:T(8,128)(2,1)S(1)}, u32[]{:S(2)}, u32[]{:S(2)}) collective-permute-start(bf16[128,768]{1,0:T(8,128)(2,1)S(1)} %fusion.11), channel_id=1, source_target_pairs={{0,16},{2,18},{4,20},{6,22},{8,24},{10,26},{12,28},{14,30},{16,0},... | collective-permute-start | bytes 589832 | tf_op jit(solution)/shard_map/ppermute | solution.py:1066
  403.7 9.9 %collective-permute-start.23 = (bf16[192,1152]{1,0:T(8,128)(2,1)S(1)}, bf16[192,1152]{1,0:T(8,128)(2,1)S(1)}, u32[]{:S(2)}, u32[]{:S(2)}) collective-permute-start(bf16[192,1152]{1,0:T(8,128)(2,1)S(1)} %get-tuple-element.296), channel_id=1, source_target_pairs={{0,2},{2,0},{4,6},{6,4},{8,10},{10,8},{12,14},{14,12},{16,18},{18,... | collective-permute-start | bytes 1327112 | tf_op jit(solution)/shard_map/ppermute | solution.py:1066
  405.5 13.9 %collective-permute-start.24 = (bf16[192,1152]{1,0:T(8,128)(2,1)S(1)}, bf16[192,1152]{1,0:T(8,128)(2,1)S(1)}, u32[]{:S(2)}, u32[]{:S(2)}) collective-permute-start(bf16[192,1152]{1,0:T(8,128)(2,1)S(1)} %get-tuple-element.297), channel_id=1, source_target_pairs={{0,4},{2,6},{4,0},{6,2},{8,12},{10,14},{12,8},{14,10},{16,20},{18,... | collective-permute-start | bytes 1327112 | tf_op jit(solution)/shard_map/ppermute | solution.py:1066
  406.3 13.1 %collective-permute-start.25 = (bf16[192,1152]{1,0:T(8,128)(2,1)S(1)}, bf16[192,1152]{1,0:T(8,128)(2,1)S(1)}, u32[]{:S(2)}, u32[]{:S(2)}) collective-permute-start(bf16[192,1152]{1,0:T(8,128)(2,1)S(1)} %get-tuple-element.298), channel_id=1, source_target_pairs={{0,6},{2,4},{4,2},{6,0},{8,14},{10,12},{12,10},{14,8},{16,22},{18,... | collective-permute-start | bytes 1327112 | tf_op jit(solution)/shard_map/ppermute | solution.py:1066
  413.6 23.8 %collective-permute-start.40 = (bf16[128,768]{1,0:T(8,128)(2,1)S(1)}, bf16[128,768]{1,0:T(8,128)(2,1)S(1)}, u32[]{:S(2)}, u32[]{:S(2)}) collective-permute-start(bf16[128,768]{1,0:T(8,128)(2,1)S(1)} %fusion.11), channel_id=1, source_target_pairs={{0,24},{2,26},{4,28},{6,30},{8,16},{10,18},{12,20},{14,22},{16,8},... | collective-permute-start | bytes 589832 | tf_op jit(solution)/shard_map/ppermute | solution.py:1066
  419.6 5.6 %collective-permute-start.26 = (bf16[48,1152]{1,0:T(8,128)(2,1)S(1)}, bf16[48,1152]{1,0:T(8,128)(2,1)S(1)}, u32[]{:S(2)}, u32[]{:S(2)}) collective-permute-start(bf16[48,1152]{1,0:T(8,128)(2,1)S(1)} %get-tuple-element.347), channel_id=1, source_target_pairs={{0,8},{2,10},{4,12},{6,14},{8,0},{10,2},{12,4},{14,6},{16,24},{18,... | collective-permute-start | bytes 331784 | tf_op jit(solution)/shard_map/ppermute | solution.py:1066
  420.9 10.9 %collective-permute-start.27 = (bf16[48,1152]{1,0:T(8,128)(2,1)S(1)}, bf16[48,1152]{1,0:T(8,128)(2,1)S(1)}, u32[]{:S(2)}, u32[]{:S(2)}) collective-permute-start(bf16[48,1152]{1,0:T(8,128)(2,1)S(1)} %get-tuple-element.349), channel_id=1, source_target_pairs={{0,16},{2,18},{4,20},{6,22},{8,24},{10,26},{12,28},{14,30},{16,0},... | collective-permute-start | bytes 331784 | tf_op jit(solution)/shard_map/ppermute | solution.py:1066
  422.4 9.5 %collective-permute-start.28 = (bf16[48,1152]{1,0:T(8,128)(2,1)S(1)}, bf16[48,1152]{1,0:T(8,128)(2,1)S(1)}, u32[]{:S(2)}, u32[]{:S(2)}) collective-permute-start(bf16[48,1152]{1,0:T(8,128)(2,1)S(1)} %get-tuple-element.348), channel_id=1, source_target_pairs={{0,24},{2,26},{4,28},{6,30},{8,16},{10,18},{12,20},{14,22},{16,8},... | collective-permute-start | bytes 331784 | tf_op jit(solution)/shard_map/ppermute | solution.py:1066
  425.2 25.7 %collective-permute-start.41 = (bf16[2,128,768]{2,1,0:T(8,128)(2,1)}, bf16[2,128,768]{2,1,0:T(8,128)(2,1)}, u32[]{:S(2)}, u32[]{:S(2)}) collective-permute-start(bf16[2,128,768]{2,1,0:T(8,128)(2,1)} %pad_maximum_fusion.12), channel_id=1, source_target_pairs={{0,2},{2,0},{4,6},{6,4},{8,10},{10,8},{12,14},{14,12},{16,18},{18,... | collective-permute-start | bytes 1179656 | tf_op jit(solution)/shard_map/ppermute | solution.py:930
  431.9 7.2 %collective-permute-start.29 = (bf16[48,1152]{1,0:T(8,128)(2,1)S(1)}, bf16[48,1152]{1,0:T(8,128)(2,1)S(1)}, u32[]{:S(2)}, u32[]{:S(2)}) collective-permute-start(bf16[48,1152]{1,0:T(8,128)(2,1)S(1)} %fusion.9), channel_id=1, source_target_pairs={{0,8},{2,10},{4,12},{6,14},{8,0},{10,2},{12,4},{14,6},{16,24},{18,... | collective-permute-start | bytes 331784 | tf_op jit(solution)/shard_map/ppermute | solution.py:1066
  434.9 8.0 %collective-permute-start.30 = (bf16[48,1152]{1,0:T(8,128)(2,1)S(1)}, bf16[48,1152]{1,0:T(8,128)(2,1)S(1)}, u32[]{:S(2)}, u32[]{:S(2)}) collective-permute-start(bf16[48,1152]{1,0:T(8,128)(2,1)S(1)} %fusion.9), channel_id=1, source_target_pairs={{0,16},{2,18},{4,20},{6,22},{8,24},{10,26},{12,28},{14,30},{16,0},... | collective-permute-start | bytes 331784 | tf_op jit(solution)/shard_map/ppermute | solution.py:1066
  435.7 7.2 %collective-permute-start.31 = (bf16[48,1152]{1,0:T(8,128)(2,1)S(1)}, bf16[48,1152]{1,0:T(8,128)(2,1)S(1)}, u32[]{:S(2)}, u32[]{:S(2)}) collective-permute-start(bf16[48,1152]{1,0:T(8,128)(2,1)S(1)} %fusion.9), channel_id=1, source_target_pairs={{0,24},{2,26},{4,28},{6,30},{8,16},{10,18},{12,20},{14,22},{16,8},... | collective-permute-start | bytes 331784 | tf_op jit(solution)/shard_map/ppermute | solution.py:1066
  438.1 12.8 %collective-permute-start.42 = (bf16[2,128,768]{2,1,0:T(8,128)(2,1)}, bf16[2,128,768]{2,1,0:T(8,128)(2,1)}, u32[]{:S(2)}, u32[]{:S(2)}) collective-permute-start(bf16[2,128,768]{2,1,0:T(8,128)(2,1)} %pad_maximum_fusion.13), channel_id=1, source_target_pairs={{0,4},{2,6},{4,0},{6,2},{8,12},{10,14},{12,8},{14,10},{16,20},{18,... | collective-permute-start | bytes 1179656 | tf_op jit(solution)/shard_map/ppermute | solution.py:930
  443.1 11.5 %collective-permute-start.32 = (bf16[192,1152]{1,0:T(8,128)(2,1)S(1)}, bf16[192,1152]{1,0:T(8,128)(2,1)}, u32[]{:S(2)}, u32[]{:S(2)}) collective-permute-start(bf16[192,1152]{1,0:T(8,128)(2,1)S(1)} %bitcast.111), channel_id=1, source_target_pairs={{0,2},{2,0},{4,6},{6,4},{8,10},{10,8},{12,14},{14,12},{16,18},{18,... | collective-permute-start | bytes 1327112 | tf_op jit(solution)/shard_map/ppermute | solution.py:1066
  445.0 17.7 %collective-permute-start.33 = (bf16[192,1152]{1,0:T(8,128)(2,1)S(1)}, bf16[192,1152]{1,0:T(8,128)(2,1)}, u32[]{:S(2)}, u32[]{:S(2)}) collective-permute-start(bf16[192,1152]{1,0:T(8,128)(2,1)S(1)} %bitcast.112), channel_id=1, source_target_pairs={{0,4},{2,6},{4,0},{6,2},{8,12},{10,14},{12,8},{14,10},{16,20},{18,... | collective-permute-start | bytes 1327112 | tf_op jit(solution)/shard_map/ppermute | solution.py:1066
  446.7 16.0 %collective-permute-start.34 = (bf16[192,1152]{1,0:T(8,128)(2,1)S(1)}, bf16[192,1152]{1,0:T(8,128)(2,1)}, u32[]{:S(2)}, u32[]{:S(2)}) collective-permute-start(bf16[192,1152]{1,0:T(8,128)(2,1)S(1)} %bitcast.113), channel_id=1, source_target_pairs={{0,6},{2,4},{4,2},{6,0},{8,14},{10,12},{12,10},{14,8},{16,22},{18,... | collective-permute-start | bytes 1327112 | tf_op jit(solution)/shard_map/ppermute | solution.py:1066
  450.9 35.6 %collective-permute-start.22 = (bf16[1536,768]{1,0:T(8,128)(2,1)S(1)}, bf16[1536,768]{1,0:T(8,128)(2,1)}, u32[]{:S(2)}, u32[]{:S(2)}) collective-permute-start(bf16[1536,768]{1,0:T(8,128)(2,1)S(1)} %convolution_convert_fusion), channel_id=1, source_target_pairs={{0,1},{1,0},{2,3},{3,2},{4,5},{5,4},{6,7},{7,6},{8,9},{9,8},{10,11... | collective-permute-start | bytes 7077896 | tf_op jit(solution)/shard_map/ppermute | solution.py:1039
  453.1 23.7 %collective-permute-start.43 = (bf16[4,128,768]{2,1,0:T(8,128)(2,1)S(1)}, bf16[4,128,768]{2,1,0:T(8,128)(2,1)S(1)}, u32[]{:S(2)}, u32[]{:S(2)}) collective-permute-start(bf16[4,128,768]{2,1,0:T(8,128)(2,1)S(1)} %get-tuple-element.352), channel_id=1, source_target_pairs={{0,4},{2,6},{4,0},{6,2},{8,12},{10,14},{12,8},{14,10},{16,20},{18,... | collective-permute-start | bytes 2359304 | tf_op jit(solution)/shard_map/ppermute | solution.py:930
  454.6 22.2 %collective-permute-start.44 = (bf16[4,128,768]{2,1,0:T(8,128)(2,1)S(1)}, bf16[4,128,768]{2,1,0:T(8,128)(2,1)S(1)}, u32[]{:S(2)}, u32[]{:S(2)}) collective-permute-start(bf16[4,128,768]{2,1,0:T(8,128)(2,1)S(1)} %get-tuple-element.350), channel_id=1, source_target_pairs={{0,2},{2,0},{4,6},{6,4},{8,10},{10,8},{12,14},{14,12},{16,18},{18,... | collective-permute-start | bytes 2359304 | tf_op jit(solution)/shard_map/ppermute | solution.py:930
  (43 other events, 343.4 us)
